TPU v7x, 32 devices: a whole 2x2x4 slice. The times are simulated.
32 devices in a mesh: patch: 16 (over z, y, core), head: 2 (over x).
Axes of the slice: x: 2, y: 2, z: 4, core: 2. Of those that a mesh axis runs over, the one named last changes fastest.
Arguments:
- hidden_states: bfloat16 [2048, 3072], P('patch', 'head'), may hold values from -500 to 500, as said below
- shift_mod: float32 [3072], replicated, may hold values from -3 to 3
- scale_mod: float32 [3072], replicated, may hold values from -3 to 3
- gate_mod: float32 [3072], P('head'), may hold values from 1 to 6
- qkv_weight: bfloat16 [3072, 3, 2048], P('patch', None, 'head'), may hold values from -0.109375 to 0.109375
- query_gain: float32 [128], replicated, may hold values from 1 to 2.5
- key_gain: float32 [128], replicated, may hold values from 1 to 2.5
- text_keys: bfloat16 [512, 2048], P(None, 'head'), may hold values from -6 to 6
- text_values: bfloat16 [512, 2048], P(None, 'head'), may hold values from -6 to 6
- stale_keys: bfloat16 [2048, 2048], P('patch', 'head'), may hold values from -330 to 330, as said below
- stale_values: bfloat16 [2048, 2048], P('patch', 'head'), may hold values from -6 to 6
- out_weight: bfloat16 [2048, 3072], P('head'), may hold values from -0.125 to 0.125
Outputs:
- update: bfloat16 [2048, 3072], P('patch', 'head')
Inputs may be any that keep to these rules, and one draw needn't show every extreme that they name: `hidden_states`: finite real values. `stale_keys`: finite real values.
All inputs are finite; a program needn't handle non-finite values.
Results may differ from a plain program's by a relative error of at most 0.02.
The roundings to bfloat16 on the way count: a program that leaves them out, or rounds other values in their place, can miss the bound.
Values may be sent and summed in bfloat16 or wider, within the bound.
No kernel may reach another device: no remote copies, remote signals or barrier semaphores. Data moves between devices by JAX's collectives and lax.ppermute only.
A program may use at most 128 MiB of HBM per device.

v0:
```python
import jax
import jax.numpy as jnp
from jax import lax
from jax.sharding import PartitionSpec as P


def head_norm(raw, gain):
    power = jnp.mean(raw * raw, axis=-1, keepdims=True)
    return raw * lax.rsqrt(power + 1e-06) * gain


def per_device(
    hidden_states,
    shift_mod,
    scale_mod,
    gate_mod,
    qkv_weight,
    query_gain,
    key_gain,
    text_keys,
    text_values,
    stale_keys,
    stale_values,
    out_weight,
):
    tok_rows = hidden_states.shape[0]
    local_width = qkv_weight.shape[2]
    head_size = query_gain.shape[0]
    local_heads = local_width // head_size
    gathered = lax.all_gather(hidden_states, "head", axis=1, tiled=True)
    states = gathered.astype(jnp.float32)
    center = jnp.mean(states, axis=-1, keepdims=True)
    spread = jnp.mean((states - center) ** 2, axis=-1, keepdims=True)
    normed = (states - center) * lax.rsqrt(spread + 1e-06)
    modulated = ((1.0 + scale_mod) * normed + shift_mod).astype(jnp.bfloat16)
    piece = lax.all_gather(qkv_weight, "patch", axis=0, tiled=True)
    flat_piece = piece.reshape(piece.shape[0], 3 * local_width)
    projected = jnp.dot(modulated, flat_piece, preferred_element_type=jnp.float32)
    projected = projected.reshape(tok_rows, 3, local_heads, head_size)
    queries = head_norm(projected[:, 0], query_gain).astype(jnp.bfloat16)
    fresh_keys = (
        head_norm(projected[:, 1], key_gain).astype(jnp.bfloat16).reshape(tok_rows, local_width)
    )
    fresh_values = projected[:, 2].astype(jnp.bfloat16).reshape(tok_rows, local_width)
    factor = head_size ** (-0.5)

    def scores_of(key_rows):
        shaped = key_rows.reshape(key_rows.shape[0], local_heads, head_size)
        return (
            jnp.einsum("qhd,khd->hqk", queries, shaped, preferred_element_type=jnp.float32) * factor
        )

    def values_of(exps, value_rows):
        shaped = value_rows.reshape(value_rows.shape[0], local_heads, head_size)
        return jnp.einsum(
            "hqk,khd->qhd", exps.astype(jnp.bfloat16), shaped, preferred_element_type=jnp.float32
        )

    first_keys = jnp.concatenate([text_keys, fresh_keys], axis=0)
    first_values = jnp.concatenate([text_values, fresh_values], axis=0)
    first_scores = scores_of(first_keys)
    running_max = jnp.max(first_scores, axis=-1)
    first_exps = jnp.exp(first_scores - running_max[:, :, None])
    running_totals = jnp.sum(first_exps, axis=-1)
    running_mixed = values_of(first_exps, first_values)
    own_start = lax.axis_index("patch") * tok_rows
    piece_keys = lax.all_gather(stale_keys, "patch", axis=0, tiled=True)
    piece_values = lax.all_gather(stale_values, "patch", axis=0, tiled=True)
    piece_rows = piece_keys.shape[0]
    scores = scores_of(piece_keys)
    positions = jnp.arange(piece_rows, dtype=jnp.int32)
    own_rows = (positions >= own_start) & (positions < own_start + tok_rows)
    scores = jnp.where(own_rows[None, None, :], -jnp.inf, scores)
    new_max = jnp.maximum(running_max, jnp.max(scores, axis=-1))
    rescale = jnp.exp(running_max - new_max)
    exps = jnp.exp(scores - new_max[:, :, None])
    new_totals = running_totals * rescale + jnp.sum(exps, axis=-1)
    new_mixed = running_mixed * jnp.transpose(rescale)[:, :, None] + values_of(exps, piece_values)
    attention = (
        (new_mixed / jnp.transpose(new_totals)[:, :, None])
        .astype(jnp.bfloat16)
        .reshape(tok_rows, local_width)
    )
    partial_terms = jnp.dot(attention, out_weight, preferred_element_type=jnp.float32)
    summed = lax.psum_scatter(
        partial_terms.astype(jnp.bfloat16), "head", scatter_dimension=1, tiled=True
    ).astype(jnp.float32)
    return (summed * gate_mod).astype(jnp.bfloat16)


def solution(mesh):
    placed = (
        P("patch", "head"),
        P(),
        P(),
        P("head"),
        P("patch", None, "head"),
        P(),
        P(),
        P(None, "head"),
        P(None, "head"),
        P("patch", "head"),
        P("patch", "head"),
        P("head", None),
    )
    return jax.shard_map(
        per_device, mesh=mesh, in_specs=placed, out_specs=P("patch", "head"), check_vma=False
    )
```

profile of v0, /device:TPU:0, one launch (start us, length us, event | category | flops | bytes accessed | tf_op | source)
XLA Modules:
  0.0 255.9 jit_solution(7188720591230585824)
XLA Ops:
  6.5 0.7 all-gather.8.cloned.1.call-update
  7.3 0.0 all-gather.4.cloned.1.call-start
  7.3 0.7 all-gather.4.cloned.1.call-update
  8.0 0.0 all-gather.6.cloned.1.call-start
  8.1 1.9 copy.29
  9.9 0.0 all-gather.6.cloned.1.call-update
  10.0 0.0 reduce-scatter.2.cloned.1.call-start
  10.0 0.5 copy.27
  10.6 0.7 copy.28
  11.3 1.3 copy.24
  12.6 13.0 %all_gather.12 = bf16[128,3072]{1,0:T(8,128)(2,1)S(1)} all-gather(bf16[128,1536]{1,0:T(8,128)(2,1)} %param.12), channel_id=1, replica_groups=mesh['patch'=16,'head'=2] {'head'}, dimensions={1}, use_global_device_ids=true | all-gather | bytes 1179648 | tf_op jit(solution)/shard_map/all_gather | solution.py:30
  25.6 0.2 convert_reduce_fusion
  25.8 0.4 fusion.13
  26.1 36.7 %all-gather.8.cloned.1.call-done = bf16[2048,1024]{1,0:T(8,128)(2,1)} async-done(((bf16[128,1024]{1,0:T(8,128)(2,1)}), bf16[2048,1024]{1,0:T(8,128)(2,1)}) %all-gather.8.cloned.1.call-update) | async-done | bytes 4194320 | tf_op jit(solution)/shard_map/all_gather | solution.py:68
  62.8 6.5 %copy.31 = bf16[2048,1024]{0,1:T(8,128)(2,1)} copy(bf16[2048,1024]{1,0:T(8,128)(2,1)} %all-gather.8.cloned.1.call-done) | data formatting | bytes 8388608 | tf_op jit(solution)/shard_map/all_gather | solution.py:68
  69.3 92.5 %all-gather.4.cloned.1.call-done = bf16[3072,3,1024]{2,0,1:T(8,128)(2,1)} async-done(((bf16[192,3,1024]{2,0,1:T(8,128)(2,1)}), bf16[3072,3,1024]{2,0,1:T(8,128)(2,1)}) %all-gather.4.cloned.1.call-update) | async-done | bytes 18874384 | tf_op jit(solution)/shard_map/all_gather | solution.py:36
  161.8 24.7 %copy.25 = bf16[3072,3,1024]{0,2,1:T(8,128)(2,1)} copy(bf16[3072,3,1024]{2,0,1:T(8,128)(2,1)} %all-gather.4.cloned.1.call-done) | data formatting | bytes 37748736 | tf_op jit(solution)/shard_map/all_gather | solution.py:36
  186.5 10.2 %fusion.51 = f32[128,3,8,128]{3,0,2,1:T(8,128)S(1)} fusion(bf16[3,8,128,3072]{3,2,1,0:T(8,128)(2,1)} %bitcast.64, bf16[128,3072]{1,0:T(8,128)(2,1)S(1)} %all_gather.12, f32[3072]{0:T(1024)S(1)} %copy-done.5, f32[128]{0:T(128)S(1)} %add_rsqrt_fusion.2, f32[128]{0:T(128)S(1)} %broadcast_multiply_fusion, f32[3072]{0:T(1024)S(1)} %broadcast_add_fusion), kind=kOutput, calls=%fused_computation.40 | convolution fusion | flops 2418278400 | bytes 21259264 | tf_op jit(solution)/shard_map/dot_general | solution.py:38
  196.8 0.2 copy.26
  197.0 0.3 multiply_reduce_fusion.2
  197.4 0.2 multiply_convert_fusion.1
  197.6 2.2 multiply_reduce_fusion
  199.8 17.4 %all-gather.6.cloned.1.call-done = bf16[2048,1024]{0,1:T(8,128)(2,1)} async-done(((bf16[128,1024]{0,1:T(8,128)(2,1)}), bf16[2048,1024]{0,1:T(8,128)(2,1)}) %all-gather.6.cloned.1.call-update) | async-done | bytes 4194320 | tf_op jit(solution)/shard_map/all_gather | solution.py:67
  217.2 3.7 %fusion = (f32[8,128]{1,0:T(8,128)S(1)}, f32[8,128,2048]{2,1,0:T(8,128)S(1)}) fusion(pred[2048]{0:T(1024)(128)(4,1)S(1)} %fusion.59, bf16[2048,8,128]{0,2,1:T(8,128)(2,1)} %bitcast.67, f32[128,3,8,128]{3,0,2,1:T(8,128)S(1)} %fusion.51, f32[128]{0:T(128)S(1)} %copy-done.8, f32[128,8]{0,1:T(8,128)S(1)} %add_rsqrt_fusion.1), kind=kOutput, calls=%fused_computation.2 | convolution fusion | flops 543554560 | bytes 13117952 | tf_op jit(solution)/shard_map/qhd,khd->hqk/dot_general | solution.py:50
  220.9 0.7 fusion.9
  221.6 1.9 fusion.1
  223.5 1.6 fusion.39
  225.1 0.8 copy-done.1
  225.9 4.0 %fusion.47 = bf16[128,8,128]{0,2,1:T(8,128)(2,1)S(1)} fusion(f32[128,8,128]{0,2,1:T(8,128)} %fusion.39, bf16[2048,8,128]{0,2,1:T(8,128)(2,1)S(1)} %bitcast.68, f32[8,128,2048]{2,1,0:T(8,128)S(1)} %get-tuple-element.12, f32[8,128]{1,0:T(8,128)S(1)} %max.12, pred[2048]{0:T(1024)(128)(4,1)S(1)} %fusion.59, f32[128,8]{0,1:T(8,128)S(1)} %get-tuple-element.7), kind=kOutput, calls=%fused_computation.38 | convolution fusion | flops 545652736 | bytes 13379584 | tf_op jit(solution)/shard_map/hqk,khd->qhd/dot_general | solution.py:55
  229.9 1.9 convolution_convert_fusion
  231.8 15.8 %reduce-scatter.2.cloned.1.call-done = bf16[128,1536]{1,0:T(8,128)(2,1)} async-done(((bf16[128,3072]{1,0:T(8,128)(2,1)}), bf16[128,1536]{1,0:T(8,128)(2,1)}) %reduce-scatter.2.cloned.1.call-update) | async-done | bytes 393232 | tf_op jit(solution)/shard_map/reduce_scatter | solution.py:85
  247.6 1.8 multiply_convert_fusion
  (35 shorter events, 0.2 us)
Async XLA Ops:
  6.5 3.5 %copy-start.2 = (bf16[512,1024]{1,0:T(8,128)(2,1)S(1)}, bf16[512,1024]{1,0:T(8,128)(2,1)}, u32[]{:S(2)}) copy-start(bf16[512,1024]{1,0:T(8,128)(2,1)} %param.19) | copy-start | bytes 3145732
  6.5 56.3 %all-gather.8.cloned.1.call-start = ((), (), s32[]{:S(2)}) async-start(), calls=%async_computation.3 | async-start | bytes 4456448 | tf_op jit(solution)/shard_map/all_gather | solution.py:68
  7.3 154.6 %all-gather.4.cloned.1.call-start = ((), (), s32[]{:S(2)}) async-start(), calls=%async_computation.1 | async-start | bytes 20054016 | tf_op jit(solution)/shard_map/all_gather | solution.py:36
  8.0 3.2 %copy-start.3 = (bf16[512,1024]{1,0:T(8,128)(2,1)S(1)}, bf16[512,1024]{1,0:T(8,128)(2,1)}, u32[]{:S(2)}) copy-start(bf16[512,1024]{1,0:T(8,128)(2,1)} %param.20) | copy-start | bytes 3145732
  8.0 209.2 %all-gather.6.cloned.1.call-start = ((), (), s32[]{:S(2)}) async-start(), calls=%async_computation.2 | async-start | bytes 4456448 | tf_op jit(solution)/shard_map/all_gather | solution.py:67
  10.0 237.6 %reduce-scatter.2.cloned.1.call-start = ((), (), s32[]{:S(2)}) async-start(), calls=%async_computation.4 | async-start | bytes 1179648 | tf_op jit(solution)/shard_map/reduce_scatter | solution.py:85
  11.3 14.9 %copy-start.6 = (f32[3072]{0:T(1024)S(1)}, f32[3072]{0:T(1024)}, u32[]{:S(2)}) copy-start(f32[3072]{0:T(1024)} %param.14) | copy-start | bytes 36868
  69.3 117.2 %copy-start.5 = (f32[3072]{0:T(1024)S(1)}, f32[3072]{0:T(1024)}, u32[]{:S(2)}) copy-start(f32[3072]{0:T(1024)} %param.13) | copy-start | bytes 36868
  186.5 10.9 %copy-start.9 = (f32[128]{0:T(128)S(1)}, f32[128]{0:T(128)}, u32[]{:S(2)}) copy-start(f32[128]{0:T(128)} %param.18) | copy-start | bytes 1540
  196.8 0.8 copy-start.8
  217.2 3.7 %copy-start = (f32[8,128,640]{2,1,0:T(8,128)S(1)}, f32[8,128,640]{2,1,0:T(8,128)}, u32[]{:S(2)}) copy-start(f32[8,128,640]{2,1,0:T(8,128)} %get-tuple-element.10) | copy-start | bytes 7864324
  221.6 1.9 copy-start.4
  223.5 2.4 copy-start.1
  223.5 6.3 %slice-start = ((s8[6291456]{0:T(1024)(128)(4,1)}), s8[4194304]{0:T(1024)(128)(4,1)S(1)}, s32[]{:S(2)}) async-start(s8[6291456]{0:T(1024)(128)(4,1)} %bitcast.65), calls=%async_computation.5 | async-start | bytes 8388608
  225.9 4.0 %slice-start.1 = ((s8[6291456]{0:T(1024)(128)(4,1)}), s8[2097152]{0:T(1024)(128)(4,1)S(1)}, s32[]{:S(2)}) async-start(s8[6291456]{0:T(1024)(128)(4,1)} %bitcast.65), calls=%async_computation.6 | async-start | bytes 4194304
  229.9 17.7 %copy-start.7 = (f32[1536]{0:T(1024)S(1)}, f32[1536]{0:T(1024)}, u32[]{:S(2)}) copy-start(f32[1536]{0:T(1024)} %param.15) | copy-start | bytes 18436
Sparse Core Ops, SparseCore 0:
  9.5 53.2 all-gather.7
  64.4 97.4 all-gather.3
  164.0 53.2 all-gather.5
  231.9 15.5 reduce-scatter.1
where the time goes:
time: 257 us; the launch traced here: 256 us
  waiting for transfers between devices  164 us (64%)
  local copies, waits for them, and re-layouts  36.6 us (14%)
  matrix products  23.5 us (9%)
  between operations  13.4 us (5%)
  blocking collectives  13 us (5%)
  other arithmetic  5.51 us (2%)
    all_gather x1, waiting for transfers between devices, per_device(): piece = lax.all_gather(qkv_weight, 'patch', axis=0, tiled=True)  92.5 us
    all_gather x1, waiting for transfers between devices, per_device(): piece_values = lax.all_gather(stale_values, 'patch', axis=0, tiled=True)  36.7 us
    all_gather x1, local copies, waits for them, and re-layouts, per_device(): piece = lax.all_gather(qkv_weight, 'patch', axis=0, tiled=True)  24.7 us
    all_gather x1, waiting for transfers between devices, per_device(): piece_keys = lax.all_gather(stale_keys, 'patch', axis=0, tiled=True)  17.4 us
    reduce_scatter x1, waiting for transfers between devices, per_device(): lax.psum_scatter(partial_terms.astype(jnp.bfloat16), 'head', scatter_dime...  15.8 us
    all_gather x1, blocking collectives, per_device(): gathered = lax.all_gather(hidden_states, 'head', axis=1, tiled=True)  13 us
    dot_general x1, matrix products, per_device(): jnp.dot(modulated, flat_piece, preferred_element_type=jnp.float32)  10.2 us
    all_gather x1, local copies, waits for them, and re-layouts, per_device(): piece_values = lax.all_gather(stale_values, 'patch', axis=0, tiled=True)  6.5 us
  transfers between devices with their start and end apart: 4, of which 4 were waited for; matrix products, arithmetic and copies ran while one was open for 19% of the time, Pallas kernels for 0%

commit v1 on v0

v1 whole, which is shorter than its diff:
```python
import functools
import math

import jax
import jax.numpy as jnp
from jax import lax
from jax.experimental import pallas as pl
from jax.experimental.pallas import tpu as pltpu
from jax.sharding import Mesh
from jax.sharding import PartitionSpec as P

ANY = pl.BlockSpec(memory_space=pl.ANY)
VMEM = pl.BlockSpec(memory_space=pltpu.VMEM)
MIB = 1024 * 1024
ACROSS = (((1,), (1,)), ((), ()))


def params(limit):
    return pltpu.CompilerParams(vmem_limit_bytes=limit * MIB)


def column(index, width):
    return pl.ds(pl.multiple_of(index * width, 128), width)


def gray(place):
    return place ^ (place >> 1)


def group_at(step, groups):
    return gray(lax.rem(gray(lax.axis_index("group")) + (step + groups), groups))


def pack_kernel(groups, weight, keys, values, *refs):
    outs, sems = refs[:-1], refs[-1]
    started = []
    for step in range(groups):
        rows, pair = outs[step], outs[groups + step]
        cols = column(group_at(step, groups), rows.shape[2])
        copies = [(weight.at[:, :, cols], rows)]
        copies += [(keys.at[:, cols], pair.at[0]), (values.at[:, cols], pair.at[1])]
        for index, (source, target) in enumerate(copies):
            copy = pltpu.make_async_copy(source, target, sems.at[step, index])
            copy.start()
            started.append(copy)
    for copy in started:
        copy.wait()


def pack(weight, keys, values, groups):
    parts, depth, full = weight.shape
    tok, width = keys.shape[0], full // groups
    rows = jax.ShapeDtypeStruct((parts, depth, width), jnp.bfloat16)
    pair = jax.ShapeDtypeStruct((2, tok, width), jnp.bfloat16)
    outs = pl.pallas_call(
        functools.partial(pack_kernel, groups),
        out_shape=[rows] * groups + [pair] * groups,
        in_specs=[ANY] * 3,
        out_specs=[ANY] * (2 * groups),
        scratch_shapes=[pltpu.SemaphoreType.DMA((groups, 3))],
        compiler_params=params(4),
        cost_estimate=pl.CostEstimate(
            flops=0, bytes_accessed=4 * full * (parts * depth + 2 * tok), transcendentals=0
        ),
    )(weight, keys, values)
    return outs[:groups], outs[groups:]


def modulate_kernel(n_head, scale, shift, *refs):
    pieces, out, rows = refs[:n_head], refs[n_head], refs[n_head + 1]
    for hop, piece in enumerate(pieces):
        part = lax.rem(lax.axis_index("head") + (n_head - hop), n_head)
        rows[:, column(part, piece.shape[1])] = piece[...].astype(jnp.float32)
    states = rows[...]
    center = jnp.mean(states, axis=-1, keepdims=True)
    apart = states - center
    spread = jnp.mean(apart * apart, axis=-1, keepdims=True)
    normed = apart * lax.rsqrt(spread + 1e-06)
    out[...] = ((1.0 + scale[...]) * normed + shift[...]).astype(jnp.bfloat16)


def modulate(pieces, scale_mod, shift_mod):
    rows, _ = pieces[0].shape
    full = scale_mod.shape[0]
    return pl.pallas_call(
        functools.partial(modulate_kernel, len(pieces)),
        out_shape=jax.ShapeDtypeStruct((rows, full), jnp.bfloat16),
        in_specs=[VMEM] * (2 + len(pieces)),
        out_specs=VMEM,
        scratch_shapes=[pltpu.VMEM((rows, full), jnp.float32)],
        compiler_params=params(12),
        cost_estimate=pl.CostEstimate(
            flops=10 * rows * full, bytes_accessed=4 * rows * full, transcendentals=rows
        ),
    )(scale_mod.reshape(1, full), shift_mod.reshape(1, full), *pieces)


def project_kernel(groups, rest, n_mod, stacks, q_gain, k_gain, *refs):
    mods, arrays = refs[:n_mod], refs[n_mod : n_mod + len(stacks)]
    out, table = refs[n_mod + len(stacks) :]
    depth = arrays[0].shape[2]
    for array, keys in zip(arrays, stacks):
        for at, (step, bits) in enumerate(keys):
            patch = group_at(-step, groups) * rest + (lax.axis_index("rest") ^ bits)
            table[:, pl.ds(pl.multiple_of(patch * depth, 16), depth), :] = array[at]
    rows = jnp.concatenate([mod[...] for mod in mods], axis=0)
    size = q_gain.shape[1]
    for part in range(3):
        raw = jnp.dot(rows, table[part], preferred_element_type=jnp.float32)
        if part == 2:
            out[part] = raw.astype(jnp.bfloat16)
            continue
        gain = (q_gain, k_gain)[part][...]
        for head in range(raw.shape[1] // size):
            one = raw[:, head * size : (head + 1) * size]
            power = jnp.mean(one * one, axis=-1, keepdims=True)
            scaled = one * lax.rsqrt(power + 1e-06) * gain
            out[part, :, head * size : (head + 1) * size] = scaled.astype(jnp.bfloat16)


def project(mods, arrays, stacks, groups, rest, query_gain, key_gain):
    rows, full = mods[0].shape[0] * len(mods), mods[0].shape[1]
    width = arrays[0].shape[3]
    size = query_gain.shape[0]
    return pl.pallas_call(
        functools.partial(project_kernel, groups, rest, len(mods), stacks),
        out_shape=jax.ShapeDtypeStruct((3, rows, width), jnp.bfloat16),
        in_specs=[VMEM] * (2 + len(mods) + len(arrays)),
        out_specs=VMEM,
        scratch_shapes=[pltpu.VMEM((3, full, width), jnp.bfloat16)],
        compiler_params=params(16),
        cost_estimate=pl.CostEstimate(
            flops=6 * rows * full * width,
            bytes_accessed=2 * rows * full + 6 * full * width,
            transcendentals=0,
        ),
    )(query_gain.reshape(1, size), key_gain.reshape(1, size), *mods, *arrays)


def attend_kernel(groups, size, stacks, qkv, text_k, text_v, *refs):
    arrays, refs = refs[: len(stacks)], refs[len(stacks) :]
    outs, scores, weights = refs[:groups], refs[groups : groups + 2], refs[groups + 2 :]
    tok, width = outs[0].shape
    text, total = text_k.shape[0], scores[0].shape[1]
    heads, many = width // size, scores[0].shape[0]
    factor = size ** (-0.5)
    mine = lax.axis_index("group")
    slots = [key for keys in stacks for key in keys]
    windows = {}
    for index, (step, bits) in enumerate(slots):
        if bits == 0:
            windows[step] = slice(text + index * tok, text + (index + 1) * tok)

    def listed(cached, which, head):
        cols = slice(head * size, (head + 1) * size)
        rows = [cached[:, column(mine * heads + head, size)]]
        for array, keys in zip(arrays, stacks):
            rows += [array[at, which, :, cols] for at in range(len(keys))]
        return jnp.concatenate(rows, axis=0)

    def spot(index):
        head, begin = index % heads, index // heads * many
        blocks = range(begin // tok, (begin + many) // tok)
        return head, slice(head * size, (head + 1) * size), begin, blocks

    def multiply(index):
        head, cols, begin, blocks = spot(index)
        held = scores[index % 2]
        held[...] = lax.dot_general(
            qkv[0, begin : begin + many, cols],
            listed(text_k, 0, head),
            ACROSS,
            preferred_element_type=jnp.float32,
        )
        for block in blocks:
            rows = slice(block * tok, (block + 1) * tok)
            held[block * tok - begin : (block + 1) * tok - begin, windows[block]] = lax.dot_general(
                qkv[0, rows, cols], qkv[1, rows, cols], ACROSS, preferred_element_type=jnp.float32
            )

    count = groups * tok // many * heads
    multiply(0)
    for index in range(count):
        if index + 1 < count:
            multiply(index + 1)
        head, cols, begin, blocks = spot(index)
        held, soft = scores[index % 2], weights[index % 2]
        for block in blocks:
            here = slice(block * tok - begin, (block + 1) * tok - begin)
            most = held[here, :size]
            for at in range(size, total, size):
                most = jnp.maximum(most, held[here, at : at + size])
            peak = jnp.max(most, axis=-1, keepdims=True)
            summed = jnp.zeros((tok, size), jnp.float32)
            for at in range(0, total, size):
                exps = jnp.exp((held[here, at : at + size] - peak) * factor)
                summed += exps
                if windows[block].start == at:
                    fresh = exps.astype(jnp.bfloat16)
                    soft[here, at : at + size] = jnp.zeros((tok, size), jnp.bfloat16)
                else:
                    soft[here, at : at + size] = exps.astype(jnp.bfloat16)
            whole = jnp.sum(summed, axis=-1, keepdims=True)
            own = qkv[2, block * tok : (block + 1) * tok, cols]
            mixed = jnp.dot(fresh, own, preferred_element_type=jnp.float32)
            mixed += jnp.dot(
                soft[here, :], listed(text_v, 1, head), preferred_element_type=jnp.float32
            )
            outs[block][:, cols] = (mixed / whole).astype(jnp.bfloat16)


def attend(qkv, text_keys, text_values, arrays, stacks, groups, size):
    _, rows, width = qkv.shape
    tok = rows // groups
    total = text_keys.shape[0] + tok * sum(len(keys) for keys in stacks)
    many = tok * (2 if groups % 2 == 0 else 1)
    return pl.pallas_call(
        functools.partial(attend_kernel, groups, size, stacks),
        out_shape=[jax.ShapeDtypeStruct((tok, width), jnp.bfloat16)] * groups,
        in_specs=[VMEM] * (3 + len(arrays)),
        out_specs=[VMEM] * groups,
        scratch_shapes=[
            pltpu.VMEM((many, total), jnp.float32),
            pltpu.VMEM((many, total), jnp.float32),
            pltpu.VMEM((many, total), jnp.bfloat16),
            pltpu.VMEM((many, total), jnp.bfloat16),
        ],
        compiler_params=params(24),
        cost_estimate=pl.CostEstimate(
            flops=4 * rows * width * total,
            bytes_accessed=4 * total * width,
            transcendentals=rows * (width // size) * total,
        ),
    )(qkv, text_keys, text_values, *arrays)


def combine_kernel(hop, n_head, weight, *refs):
    pieces, out, rows = refs[:-2], refs[-2], refs[-1]
    wide = pieces[0].shape[1]
    for step, piece in enumerate(pieces):
        rows[:, column(group_at(step, len(pieces)), wide)] = piece[...]
    side = lax.rem(lax.axis_index("head") + hop, n_head)
    table = weight[:, column(side, out.shape[1])]
    out[...] = jnp.dot(rows[...], table, preferred_element_type=jnp.float32).astype(out.dtype)


def combine(pieces, hop, n_head, weight, share, kind):
    tok = pieces[0].shape[0]
    depth = weight.shape[0]
    return pl.pallas_call(
        functools.partial(combine_kernel, hop, n_head),
        out_shape=jax.ShapeDtypeStruct((tok, share), kind),
        in_specs=[VMEM] * (1 + len(pieces)),
        out_specs=VMEM,
        scratch_shapes=[pltpu.VMEM((tok, depth), jnp.bfloat16)],
        compiler_params=params(6),
        cost_estimate=pl.CostEstimate(
            flops=2 * tok * depth * share, bytes_accessed=2 * depth * share, transcendentals=0
        ),
    )(weight, *pieces)


def after(array, *others):
    return lax.optimization_barrier((array, *others))[0] if others else array


def per_device(
    groups,
    rest,
    n_head,
    hidden_states,
    shift_mod,
    scale_mod,
    gate_mod,
    qkv_weight,
    query_gain,
    key_gain,
    text_keys,
    text_values,
    stale_keys,
    stale_values,
    out_weight,
):
    tok, share = hidden_states.shape
    size = query_gain.shape[0]

    def turn(array, step):
        pairs = [(i, gray((gray(i) + step) % groups)) for i in range(groups)]
        return lax.ppermute(array, "group", pairs)

    def swap(array, bit):
        return lax.ppermute(array, "rest", [(i, i ^ bit) for i in range(rest)])

    def across(array, hop):
        return lax.ppermute(array, "head", [(i, (i + hop) % n_head) for i in range(n_head)])

    def finish(found, last, ready):
        bit = rest // 2
        while bit > 1:
            for (step, bits), piece in list(found.items()):
                if last is not None:
                    piece = after(piece, last)
                found[step, bits | bit] = last = swap(piece, bit)
            bit //= 2
        names = list(found)
        stacks = [[name] for name in names]
        arrays = [found[name][None] for name in names]
        if bit:
            early = [name for name in names[:-1] if name[0] < groups // 2]
            late = [name for name in names[:-1] if name[0] >= groups // 2]
            for cut in (early, late, names[-1:]):
                if not cut:
                    continue
                pieces = [found[name] for name in cut]
                stack = jnp.stack(pieces) if len(cut) > 1 else pieces[0][None]
                if cut[-1] == names[-1]:
                    stack = after(stack, *ready)
                arrays.append(swap(stack, bit))
                stacks.append([(step, bits | bit) for step, bits in cut])
        return arrays, stacks, last

    moving, last = hidden_states, None
    mods, hops, sides = [], [], []
    for step in range(groups):
        if step:
            moving = turn(after(moving, *sides[: step - 1]), 1)
            hops.append(moving)
        slices = [moving]
        for hop in range(1, n_head):
            last = across(moving if last is None else after(moving, last), hop)
            slices.append(last)
            sides.append(last)
        mods.append(modulate(slices, scale_mod, shift_mod))

    packed, pairs = pack(jnp.transpose(qkv_weight, (1, 0, 2)), stale_keys, stale_values, groups)
    rows, cached = {(0, 0): packed[0]}, {(0, 0): pairs[0]}
    before = []
    for step in range(1, groups):
        before = before + hops[step - 1 : step]
        rows[step, 0] = turn(after(packed[step], *before), step)
        before = [rows[step, 0]]
    for step in range(1, groups):
        before = [rows[min(step + 1, groups - 1), 0]] + (mods[:step] if step > 1 else [])
        cached[step, 0] = turn(after(pairs[step], *before), step)
    arrays, stacks, last = finish(rows, None, mods[-1:])
    qkv = project(mods, arrays, stacks, groups, rest, query_gain, key_gain)
    arrays, stacks, _ = finish(cached, last, [])
    attention = attend(qkv, text_keys, text_values, arrays, stacks, groups, size)
    pieces = [attention[0]] + [turn(attention[step], -step) for step in range(1, groups)]
    terms = []
    for hop in range(1, n_head):
        term = combine(pieces, hop, n_head, out_weight, share, jnp.bfloat16)
        terms.append(across(term, hop))
    summed = combine(pieces, 0, n_head, out_weight, share, jnp.float32)
    for term in terms:
        summed = summed + term.astype(jnp.float32)
    return (summed * gate_mod).astype(jnp.bfloat16)


def solution(mesh):
    n_patch, n_head = mesh.shape["patch"], mesh.shape["head"]

    def whole(*arrays):
        heads = arrays[4].shape[2] // n_head // arrays[5].shape[0]
        groups = math.gcd(math.gcd(4, heads), n_patch)
        rest = n_patch // groups
        cut = Mesh(mesh.devices.reshape(groups, rest, n_head), ("group", "rest", "head"))
        patch = ("group", "rest")
        placed = (
            P(patch, "head"),
            P(),
            P(),
            P("head"),
            P(patch, None, "head"),
            P(),
            P(),
            P(None, "head"),
            P(None, "head"),
            P(patch, "head"),
            P(patch, "head"),
            P("head", None),
        )
        return jax.shard_map(
            functools.partial(per_device, groups, rest, n_head),
            mesh=cut,
            in_specs=placed,
            out_specs=P(patch, "head"),
            check_vma=False,
        )(*arrays)

    return whole
```

time: 257 us -> 123 us (0.48)
  waiting for transfers between devices: 164 us -> 59.5 us
  starting transfers between devices: 0.12 us -> 45.7 us
  local copies, waits for them, and re-layouts: 36.6 us -> 3.23 us
  matrix products: 23.5 us -> 0 us
  between operations: 13.4 us -> 0.31 us
  blocking collectives: 13 us -> 0 us
  Pallas kernels: 0 us -> 12.9 us
  other arithmetic: 5.51 us -> 1.2 us
    all_gather x3 -> x0, waiting for transfers between devices: 147 us -> none  [the longest x1 92.5 us: per_device(): piece = lax.all_gather(qkv_weight, 'patch', axis=0, tiled=True)]
    ppermute x0 -> x31, waiting for transfers between devices: none -> 59.5 us  [the longest x12 29.4 us: turn(): return lax.ppermute(array, 'group', pairs)]
    ppermute x0 -> x31, starting transfers between devices: none -> 45.7 us  [the longest x12 28.9 us: turn(): return lax.ppermute(array, 'group', pairs)]
    all_gather x2 -> x0, local copies, waits for them, and re-layouts: 31.2 us -> none  [the longest x1 24.7 us: per_device(): piece = lax.all_gather(qkv_weight, 'patch', axis=0, tiled=True)]
    dot_general x6 -> x0, matrix products: 23.5 us -> none  [the longest x1 10.2 us: per_device(): jnp.dot(modulated, flat_piece, preferred_element_type=jnp.float32)]
    reduce_scatter x1 -> x0, waiting for transfers between devices: 15.8 us -> none  [per_device(): lax.psum_scatter(partial_terms.astype(jnp.bfloat16), 'head', scatter_dime...]
    all_gather x1 -> x0, blocking collectives: 13 us -> none  [per_device(): gathered = lax.all_gather(hidden_states, 'head', axis=1, tiled=True)]
    pallas_call x0 -> x9, Pallas kernels: none -> 12.9 us  [the longest x1 4.96 us: attend(): pl.pallas_call(functools.partial(attend_kernel, groups, size, stacks), ou...]
  transfers between devices with their start and end apart: 4 -> 31, of which waited for: 4 -> 18; matrix products, arithmetic and copies ran while one was open for 19% -> 0% of each run, Pallas kernels for 0% -> 6%
where the time goes in v1:
time: 123 us
  waiting for transfers between devices  59.5 us (48%)
  starting transfers between devices  45.7 us (37%)
  Pallas kernels  12.9 us (10%)
  local copies, waits for them, and re-layouts  3.23 us (3%)
    ppermute x12, waiting for transfers between devices, turn(): return lax.ppermute(array, 'group', pairs)  29.4 us
    ppermute x12, starting transfers between devices, turn(): return lax.ppermute(array, 'group', pairs)  28.9 us
    ppermute x5, waiting for transfers between devices, across(): lax.ppermute(array, 'head', [(i, (i + hop) % n_head) for i in range(n_hea...  16.5 us
    ppermute x14, waiting for transfers between devices, swap(): return lax.ppermute(array, 'rest', [(i, i ^ bit) for i in range(rest)])  13.7 us
    ppermute x14, starting transfers between devices, swap(): return lax.ppermute(array, 'rest', [(i, i ^ bit) for i in range(rest)])  8.51 us
    ppermute x5, starting transfers between devices, across(): lax.ppermute(array, 'head', [(i, (i + hop) % n_head) for i in range(n_hea...  8.31 us
    pallas_call x1, Pallas kernels, attend(): pl.pallas_call(functools.partial(attend_kernel, groups, size, stacks), ou...  4.96 us
    pallas_call x4, Pallas kernels, modulate(): pl.pallas_call(functools.partial(modulate_kernel, len(pieces)), out_shape...  3.29 us
  transfers between devices with their start and end apart: 31, of which 18 were waited for; matrix products, arithmetic and copies ran while one was open for 0% of the time, Pallas kernels for 6%

profile of v1, /device:TPU:0, one launch (start us, length us, event | category | flops | bytes accessed | tf_op | source)
XLA Modules:
  0.0 122.8 jit_solution(9396677150302301799)
XLA Ops:
  0.0 2.9 %collective-permute-start = (bf16[128,1536]{1,0:T(8,128)(2,1)}, bf16[128,1536]{1,0:T(8,128)(2,1)S(1)}, u32[]{:S(2)}, u32[]{:S(2)}) collective-permute-start(bf16[128,1536]{1,0:T(8,128)(2,1)} %refs_0_.1), channel_id=1, source_target_pairs={{0,1},{1,0},{2,3},{3,2},{4,5},{5,4},{6,7},{7,6},{8,9},{9,8},{10,11... | collective-permute-start | bytes 1179656 | tf_op jit(solution)/shard_map/ppermute | solution.py:295
  2.9 1.6 %collective-permute-start.1 = (bf16[128,1536]{1,0:T(8,128)(2,1)}, bf16[128,1536]{1,0:T(8,128)(2,1)S(1)}, u32[]{:S(2)}, u32[]{:S(2)}) collective-permute-start(bf16[128,1536]{1,0:T(8,128)(2,1)} %refs_0_.1), channel_id=1, source_target_pairs={{0,8},{8,24},{16,0},{24,16},{1,9},{9,25},{17,1},{25,17},{2,10},{10... | collective-permute-start | bytes 1179656 | tf_op jit(solution)/shard_map/ppermute | solution.py:289
  4.5 7.7 %collective-permute-done.refs_1_ = bf16[128,1536]{1,0:T(8,128)(2,1)S(1)} collective-permute-done((bf16[128,1536]{1,0:T(8,128)(2,1)}, bf16[128,1536]{1,0:T(8,128)(2,1)S(1)}, u32[]{:S(2)}, u32[]{:S(2)}) %collective-permute-start) | collective-permute-done | bytes 393248 | tf_op jit(solution)/shard_map/ppermute | solution.py:295
  12.3 2.4 %collective-permute-done.1.refs_0_ = bf16[128,1536]{1,0:T(8,128)(2,1)S(1)} collective-permute-done((bf16[128,1536]{1,0:T(8,128)(2,1)}, bf16[128,1536]{1,0:T(8,128)(2,1)S(1)}, u32[]{:S(2)}, u32[]{:S(2)}) %collective-permute-start.1) | collective-permute-done | bytes 393248 | tf_op jit(solution)/shard_map/ppermute | solution.py:289
  16.1 1.3 %copy-done = bf16[192,3,1024]{2,0,1:T(8,128)(2,1)S(1)} copy-done((bf16[192,3,1024]{2,0,1:T(8,128)(2,1)S(1)}, bf16[192,3,1024]{2,0,1:T(8,128)(2,1)}, u32[]{:S(2)}) %copy-start) | copy-done | bytes 1179672
  19.6 1.6 %collective-permute-start.10 = (bf16[3,192,256]{2,1,0:T(8,128)(2,1)S(1)}, bf16[3,192,256]{2,1,0:T(8,128)(2,1)S(1)}, u32[]{:S(2)}, u32[]{:S(2)}) collective-permute-start(bf16[3,192,256]{2,1,0:T(8,128)(2,1)S(1)} %get-tuple-element.39), channel_id=1, source_target_pairs={{0,4},{2,6},{4,0},{6,2},{1,5},{3,7},{5,1},{7,3},{8,12},{10,14},{12... | collective-permute-start | bytes 884744 | tf_op jit(solution)/shard_map/ppermute | solution.py:292
  21.2 3.3 %collective-permute-start.7 = (bf16[3,192,256]{2,1,0:T(8,128)(2,1)S(1)}, bf16[3,192,256]{2,1,0:T(8,128)(2,1)S(1)}, u32[]{:S(2)}, u32[]{:S(2)}) collective-permute-start(bf16[3,192,256]{2,1,0:T(8,128)(2,1)S(1)} %get-tuple-element.41), channel_id=1, source_target_pairs={{0,8},{8,24},{16,0},{24,16},{1,9},{9,25},{17,1},{25,17},{2,10},{10... | collective-permute-start | bytes 884744 | tf_op jit(solution)/shard_map/ppermute | solution.py:289
  24.5 3.6 %collective-permute-done.3.refs_0_ = bf16[128,1536]{1,0:T(8,128)(2,1)S(1)} collective-permute-done((bf16[128,1536]{1,0:T(8,128)(2,1)S(1)}, bf16[128,1536]{1,0:T(8,128)(2,1)S(1)}, u32[]{:S(2)}, u32[]{:S(2)}) %collective-permute-start.3) | collective-permute-done | bytes 393248 | tf_op jit(solution)/shard_map/ppermute | solution.py:289
  28.9 5.5 %collective-permute-done.7 = bf16[3,192,256]{2,1,0:T(8,128)(2,1)S(1)} collective-permute-done((bf16[3,192,256]{2,1,0:T(8,128)(2,1)S(1)}, bf16[3,192,256]{2,1,0:T(8,128)(2,1)S(1)}, u32[]{:S(2)}, u32[]{:S(2)}) %collective-permute-start.7) | collective-permute-done | bytes 294944 | tf_op jit(solution)/shard_map/ppermute | solution.py:289
  34.4 1.6 %collective-permute-start.11 = (bf16[3,192,256]{2,1,0:T(8,128)(2,1)S(1)}, bf16[3,192,256]{2,1,0:T(8,128)(2,1)S(1)}, u32[]{:S(2)}, u32[]{:S(2)}) collective-permute-start(bf16[3,192,256]{2,1,0:T(8,128)(2,1)S(1)} %collective-permute-done.7), channel_id=1, source_target_pairs={{0,4},{2,6},{4,0},{6,2},{1,5},{3,7},{5,1},{7,3},{8,12},{10,14},{12... | collective-permute-start | bytes 884744 | tf_op jit(solution)/shard_map/ppermute | solution.py:292
  36.0 3.6 %collective-permute-start.8 = (bf16[3,192,256]{2,1,0:T(8,128)(2,1)S(1)}, bf16[3,192,256]{2,1,0:T(8,128)(2,1)S(1)}, u32[]{:S(2)}, u32[]{:S(2)}) collective-permute-start(bf16[3,192,256]{2,1,0:T(8,128)(2,1)S(1)} %get-tuple-element.43), channel_id=1, source_target_pairs={{0,24},{8,16},{16,8},{24,0},{1,25},{9,17},{17,9},{25,1},{2,26},{10... | collective-permute-start | bytes 884744 | tf_op jit(solution)/shard_map/ppermute | solution.py:289
  39.6 1.5 %collective-permute-start.4 = (bf16[128,1536]{1,0:T(8,128)(2,1)S(1)}, bf16[128,1536]{1,0:T(8,128)(2,1)S(1)}, u32[]{:S(2)}, u32[]{:S(2)}) collective-permute-start(bf16[128,1536]{1,0:T(8,128)(2,1)S(1)} %collective-permute-done.3.refs_0_), channel_id=1, source_target_pairs={{0,1},{1,0},{2,3},{3,2},{4,5},{5,4},{6,7},{7,6},{8,9},{9,8},{10,11... | collective-permute-start | bytes 1179656 | tf_op jit(solution)/shard_map/ppermute | solution.py:295
  41.1 6.4 %collective-permute-done.8 = bf16[3,192,256]{2,1,0:T(8,128)(2,1)S(1)} collective-permute-done((bf16[3,192,256]{2,1,0:T(8,128)(2,1)S(1)}, bf16[3,192,256]{2,1,0:T(8,128)(2,1)S(1)}, u32[]{:S(2)}, u32[]{:S(2)}) %collective-permute-start.8) | collective-permute-done | bytes 294944 | tf_op jit(solution)/shard_map/ppermute | solution.py:289
  47.6 1.5 %collective-permute-start.12 = (bf16[3,192,256]{2,1,0:T(8,128)(2,1)S(1)}, bf16[3,192,256]{2,1,0:T(8,128)(2,1)S(1)}, u32[]{:S(2)}, u32[]{:S(2)}) collective-permute-start(bf16[3,192,256]{2,1,0:T(8,128)(2,1)S(1)} %collective-permute-done.8), channel_id=1, source_target_pairs={{0,4},{2,6},{4,0},{6,2},{1,5},{3,7},{5,1},{7,3},{8,12},{10,14},{12... | collective-permute-start | bytes 884744 | tf_op jit(solution)/shard_map/ppermute | solution.py:292
  49.2 7.9 %collective-permute-start.9 = (bf16[3,192,256]{2,1,0:T(8,128)(2,1)S(1)}, bf16[3,192,256]{2,1,0:T(8,128)(2,1)S(1)}, u32[]{:S(2)}, u32[]{:S(2)}) collective-permute-start(bf16[3,192,256]{2,1,0:T(8,128)(2,1)S(1)} %get-tuple-element.45), channel_id=1, source_target_pairs={{0,16},{8,0},{16,24},{24,8},{1,17},{9,1},{17,25},{25,9},{2,18},{10... | collective-permute-start | bytes 884744 | tf_op jit(solution)/shard_map/ppermute | solution.py:289
  57.3 4.0 %collective-permute-done.9 = bf16[3,192,256]{2,1,0:T(8,128)(2,1)S(1)} collective-permute-done((bf16[3,192,256]{2,1,0:T(8,128)(2,1)S(1)}, bf16[3,192,256]{2,1,0:T(8,128)(2,1)S(1)}, u32[]{:S(2)}, u32[]{:S(2)}) %collective-permute-start.9) | collective-permute-done | bytes 294944 | tf_op jit(solution)/shard_map/ppermute | solution.py:289
  62.0 1.6 %collective-permute-start.6 = (bf16[128,1536]{1,0:T(8,128)(2,1)S(1)}, bf16[128,1536]{1,0:T(8,128)(2,1)S(1)}, u32[]{:S(2)}, u32[]{:S(2)}) collective-permute-start(bf16[128,1536]{1,0:T(8,128)(2,1)S(1)} %collective-permute-done.5.refs_0_), channel_id=1, source_target_pairs={{0,1},{1,0},{2,3},{3,2},{4,5},{5,4},{6,7},{7,6},{8,9},{9,8},{10,11... | collective-permute-start | bytes 1179656 | tf_op jit(solution)/shard_map/ppermute | solution.py:295
  63.6 1.5 %collective-permute-start.17 = (bf16[2,128,256]{2,1,0:T(8,128)(2,1)S(1)}, bf16[2,128,256]{2,1,0:T(8,128)(2,1)S(1)}, u32[]{:S(2)}, u32[]{:S(2)}) collective-permute-start(bf16[2,128,256]{2,1,0:T(8,128)(2,1)S(1)} %get-tuple-element.52), channel_id=1, source_target_pairs={{0,8},{8,24},{16,0},{24,16},{1,9},{9,25},{17,1},{25,17},{2,10},{10... | collective-permute-start | bytes 393224 | tf_op jit(solution)/shard_map/ppermute | solution.py:289
  65.0 3.5 %collective-permute-done.13 = bf16[3,192,256]{2,1,0:T(8,128)(2,1)S(1)} collective-permute-done((bf16[3,192,256]{2,1,0:T(8,128)(2,1)S(1)}, bf16[3,192,256]{2,1,0:T(8,128)(2,1)S(1)}, u32[]{:S(2)}, u32[]{:S(2)}) %collective-permute-start.13) | collective-permute-done | bytes 294944 | tf_op jit(solution)/shard_map/ppermute | solution.py:292
  70.8 1.4 %collective-permute-start.18 = (bf16[2,128,256]{2,1,0:T(8,128)(2,1)S(1)}, bf16[2,128,256]{2,1,0:T(8,128)(2,1)S(1)}, u32[]{:S(2)}, u32[]{:S(2)}) collective-permute-start(bf16[2,128,256]{2,1,0:T(8,128)(2,1)S(1)} %get-tuple-element.54), channel_id=1, source_target_pairs={{0,24},{8,16},{16,8},{24,0},{1,25},{9,17},{17,9},{25,1},{2,26},{10... | collective-permute-start | bytes 393224 | tf_op jit(solution)/shard_map/ppermute | solution.py:289
  74.5 5.4 %collective-permute-start.19 = (bf16[2,128,256]{2,1,0:T(8,128)(2,1)S(1)}, bf16[2,128,256]{2,1,0:T(8,128)(2,1)S(1)}, u32[]{:S(2)}, u32[]{:S(2)}) collective-permute-start(bf16[2,128,256]{2,1,0:T(8,128)(2,1)S(1)} %get-tuple-element.56), channel_id=1, source_target_pairs={{0,16},{8,0},{16,24},{24,8},{1,17},{9,1},{17,25},{25,9},{2,18},{10... | collective-permute-start | bytes 393224 | tf_op jit(solution)/shard_map/ppermute | solution.py:289
  80.9 1.3 %collective-permute-start.22 = (bf16[2,128,256]{2,1,0:T(8,128)(2,1)S(1)}, bf16[2,128,256]{2,1,0:T(8,128)(2,1)S(1)}, u32[]{:S(2)}, u32[]{:S(2)}) collective-permute-start(bf16[2,128,256]{2,1,0:T(8,128)(2,1)S(1)} %collective-permute-done.18), channel_id=1, source_target_pairs={{0,4},{2,6},{4,0},{6,2},{1,5},{3,7},{5,1},{7,3},{8,12},{10,14},{12... | collective-permute-start | bytes 393224 | tf_op jit(solution)/shard_map/ppermute | solution.py:292
  82.5 4.3 %collective-permute-done.22 = bf16[2,128,256]{2,1,0:T(8,128)(2,1)S(1)} collective-permute-done((bf16[2,128,256]{2,1,0:T(8,128)(2,1)S(1)}, bf16[2,128,256]{2,1,0:T(8,128)(2,1)S(1)}, u32[]{:S(2)}, u32[]{:S(2)}) %collective-permute-start.22) | collective-permute-done | bytes 131104 | tf_op jit(solution)/shard_map/ppermute | solution.py:292
  86.9 1.3 %collective-permute-start.23 = (bf16[2,128,256]{2,1,0:T(8,128)(2,1)S(1)}, bf16[2,128,256]{2,1,0:T(8,128)(2,1)S(1)}, u32[]{:S(2)}, u32[]{:S(2)}) collective-permute-start(bf16[2,128,256]{2,1,0:T(8,128)(2,1)S(1)} %collective-permute-done.19), channel_id=1, source_target_pairs={{0,4},{2,6},{4,0},{6,2},{1,5},{3,7},{5,1},{7,3},{8,12},{10,14},{12... | collective-permute-start | bytes 393224 | tf_op jit(solution)/shard_map/ppermute | solution.py:292
  88.2 4.6 %collective-permute-done.23 = bf16[2,128,256]{2,1,0:T(8,128)(2,1)S(1)} collective-permute-done((bf16[2,128,256]{2,1,0:T(8,128)(2,1)S(1)}, bf16[2,128,256]{2,1,0:T(8,128)(2,1)S(1)}, u32[]{:S(2)}, u32[]{:S(2)}) %collective-permute-start.23) | collective-permute-done | bytes 131104 | tf_op jit(solution)/shard_map/ppermute | solution.py:292
  92.9 3.0 %shard_map.123.qkv = bf16[3,512,256]{2,1,0:T(8,128)(2,1)S(1)} custom-call(f32[1,128]{1,0:T(1,128)S(1)} %bitcast.64, f32[1,128]{1,0:T(1,128)S(1)} %bitcast.65, bf16[128,3072]{1,0:T(8,128)(2,1)S(1)} %shard_map.118.refs_0_, bf16[128,3072]{1,0:T(8,128)(2,1)S(1)} %shard_map.119.refs_1_, bf16[128,3072]{1,0:T(8,128)(2,1)S(1)} %shard_map.120.refs_2_, ...), custom_call_target="tpu_custom_call" | custom-call | flops 2415919104 | bytes 7864320 | tf_op jit(solution)/shard_map/pallas_call | solution.py:125
  96.0 5.0 %shard_map.124 = (bf16[128,256]{1,0:T(8,128)(2,1)S(1)}, bf16[128,256]{1,0:T(8,128)(2,1)S(1)}, bf16[128,256]{1,0:T(8,128)(2,1)S(1)}, bf16[128,256]{1,0:T(8,128)(2,1)S(1)}) custom-call(bf16[3,512,256]{2,1,0:T(8,128)(2,1)S(1)} %shard_map.123.qkv, bf16[512,1024]{1,0:T(8,128)(2,1)S(1)} %copy-done.1, bf16[512,1024]{1,0:T(8,128)(2,1)S(1)} %copy-done.2, ...), custom_call_target="tpu_custom_call" | custom-call | flops 1342177280 | bytes 2621440 | tf_op jit(solution)/shard_map/pallas_call | solution.py:217
  100.9 1.4 %collective-permute-start.27 = (bf16[128,256]{1,0:T(8,128)(2,1)S(1)}, bf16[128,256]{1,0:T(8,128)(2,1)S(1)}, u32[]{:S(2)}, u32[]{:S(2)}) collective-permute-start(bf16[128,256]{1,0:T(8,128)(2,1)S(1)} %get-tuple-element.62), channel_id=1, source_target_pairs={{0,16},{8,0},{16,24},{24,8},{1,17},{9,1},{17,25},{25,9},{2,18},{10... | collective-permute-start | bytes 196616 | tf_op jit(solution)/shard_map/ppermute | solution.py:289
  103.5 1.9 %collective-permute-done.27.refs_1_ = bf16[128,256]{1,0:T(8,128)(2,1)S(1)} collective-permute-done((bf16[128,256]{1,0:T(8,128)(2,1)S(1)}, bf16[128,256]{1,0:T(8,128)(2,1)S(1)}, u32[]{:S(2)}, u32[]{:S(2)}) %collective-permute-start.27) | collective-permute-done | bytes 65568 | tf_op jit(solution)/shard_map/ppermute | solution.py:289
  105.5 3.5 %collective-permute-done.28.refs_2_ = bf16[128,256]{1,0:T(8,128)(2,1)S(1)} collective-permute-done((bf16[128,256]{1,0:T(8,128)(2,1)S(1)}, bf16[128,256]{1,0:T(8,128)(2,1)S(1)}, u32[]{:S(2)}, u32[]{:S(2)}) %collective-permute-start.28) | collective-permute-done | bytes 65568 | tf_op jit(solution)/shard_map/ppermute | solution.py:289
  110.8 1.8 %collective-permute-start.30 = (bf16[128,1536]{1,0:T(8,128)(2,1)S(1)}, bf16[128,1536]{1,0:T(8,128)(2,1)S(1)}, u32[]{:S(2)}, u32[]{:S(2)}) collective-permute-start(bf16[128,1536]{1,0:T(8,128)(2,1)S(1)} %shard_map.126), channel_id=1, source_target_pairs={{0,1},{1,0},{2,3},{3,2},{4,5},{5,4},{6,7},{7,6},{8,9},{9,8},{10,11... | collective-permute-start | bytes 1179656 | tf_op jit(solution)/shard_map/ppermute | solution.py:295
  113.3 8.7 %collective-permute-done.30 = bf16[128,1536]{1,0:T(8,128)(2,1)S(1)} collective-permute-done((bf16[128,1536]{1,0:T(8,128)(2,1)S(1)}, bf16[128,1536]{1,0:T(8,128)(2,1)S(1)}, u32[]{:S(2)}, u32[]{:S(2)}) %collective-permute-start.30) | collective-permute-done | bytes 393248 | tf_op jit(solution)/shard_map/ppermute | solution.py:295
  (71 shorter events, 16.0 us)
Async XLA Ops:
  0.0 12.3 %collective-permute-start = (bf16[128,1536]{1,0:T(8,128)(2,1)}, bf16[128,1536]{1,0:T(8,128)(2,1)S(1)}, u32[]{:S(2)}, u32[]{:S(2)}) collective-permute-start(bf16[128,1536]{1,0:T(8,128)(2,1)} %refs_0_.1), channel_id=1, source_target_pairs={{0,1},{1,0},{2,3},{3,2},{4,5},{5,4},{6,7},{7,6},{8,9},{9,8},{10,11... | collective-permute-start | bytes 1179656 | tf_op jit(solution)/shard_map/ppermute | solution.py:295
  2.9 11.7 %collective-permute-start.1 = (bf16[128,1536]{1,0:T(8,128)(2,1)}, bf16[128,1536]{1,0:T(8,128)(2,1)S(1)}, u32[]{:S(2)}, u32[]{:S(2)}) collective-permute-start(bf16[128,1536]{1,0:T(8,128)(2,1)} %refs_0_.1), channel_id=1, source_target_pairs={{0,8},{8,24},{16,0},{24,16},{1,9},{9,25},{17,1},{25,17},{2,10},{10... | collective-permute-start | bytes 1179656 | tf_op jit(solution)/shard_map/ppermute | solution.py:289
  14.6 9.8 %collective-permute-start.2 = (bf16[128,1536]{1,0:T(8,128)(2,1)S(1)}, bf16[128,1536]{1,0:T(8,128)(2,1)S(1)}, u32[]{:S(2)}, u32[]{:S(2)}) collective-permute-start(bf16[128,1536]{1,0:T(8,128)(2,1)S(1)} %collective-permute-done.1.refs_0_), channel_id=1, source_target_pairs={{0,1},{1,0},{2,3},{3,2},{4,5},{5,4},{6,7},{7,6},{8,9},{9,8},{10,11... | collective-permute-start | bytes 1179656 | tf_op jit(solution)/shard_map/ppermute | solution.py:295
  15.1 12.9 %collective-permute-start.3 = (bf16[128,1536]{1,0:T(8,128)(2,1)S(1)}, bf16[128,1536]{1,0:T(8,128)(2,1)S(1)}, u32[]{:S(2)}, u32[]{:S(2)}) collective-permute-start(bf16[128,1536]{1,0:T(8,128)(2,1)S(1)} %collective-permute-done.1.refs_0_), channel_id=1, source_target_pairs={{0,8},{8,24},{16,0},{24,16},{1,9},{9,25},{17,1},{25,17},{2,10},{10... | collective-permute-start | bytes 1179656 | tf_op jit(solution)/shard_map/ppermute | solution.py:289
  19.6 9.3 %collective-permute-start.10 = (bf16[3,192,256]{2,1,0:T(8,128)(2,1)S(1)}, bf16[3,192,256]{2,1,0:T(8,128)(2,1)S(1)}, u32[]{:S(2)}, u32[]{:S(2)}) collective-permute-start(bf16[3,192,256]{2,1,0:T(8,128)(2,1)S(1)} %get-tuple-element.39), channel_id=1, source_target_pairs={{0,4},{2,6},{4,0},{6,2},{1,5},{3,7},{5,1},{7,3},{8,12},{10,14},{12... | collective-permute-start | bytes 884744 | tf_op jit(solution)/shard_map/ppermute | solution.py:292
  21.2 13.2 %collective-permute-start.7 = (bf16[3,192,256]{2,1,0:T(8,128)(2,1)S(1)}, bf16[3,192,256]{2,1,0:T(8,128)(2,1)S(1)}, u32[]{:S(2)}, u32[]{:S(2)}) collective-permute-start(bf16[3,192,256]{2,1,0:T(8,128)(2,1)S(1)} %get-tuple-element.41), channel_id=1, source_target_pairs={{0,8},{8,24},{16,0},{24,16},{1,9},{9,25},{17,1},{25,17},{2,10},{10... | collective-permute-start | bytes 884744 | tf_op jit(solution)/shard_map/ppermute | solution.py:289
  28.1 21.1 %collective-permute-start.5 = (bf16[128,1536]{1,0:T(8,128)(2,1)S(1)}, bf16[128,1536]{1,0:T(8,128)(2,1)S(1)}, u32[]{:S(2)}, u32[]{:S(2)}) collective-permute-start(bf16[128,1536]{1,0:T(8,128)(2,1)S(1)} %collective-permute-done.3.refs_0_), channel_id=1, source_target_pairs={{0,8},{8,24},{16,0},{24,16},{1,9},{9,25},{17,1},{25,17},{2,10},{10... | collective-permute-start | bytes 1179656 | tf_op jit(solution)/shard_map/ppermute | solution.py:289
  34.4 6.7 %collective-permute-start.11 = (bf16[3,192,256]{2,1,0:T(8,128)(2,1)S(1)}, bf16[3,192,256]{2,1,0:T(8,128)(2,1)S(1)}, u32[]{:S(2)}, u32[]{:S(2)}) collective-permute-start(bf16[3,192,256]{2,1,0:T(8,128)(2,1)S(1)} %collective-permute-done.7), channel_id=1, source_target_pairs={{0,4},{2,6},{4,0},{6,2},{1,5},{3,7},{5,1},{7,3},{8,12},{10,14},{12... | collective-permute-start | bytes 884744 | tf_op jit(solution)/shard_map/ppermute | solution.py:292
  36.0 11.6 %collective-permute-start.8 = (bf16[3,192,256]{2,1,0:T(8,128)(2,1)S(1)}, bf16[3,192,256]{2,1,0:T(8,128)(2,1)S(1)}, u32[]{:S(2)}, u32[]{:S(2)}) collective-permute-start(bf16[3,192,256]{2,1,0:T(8,128)(2,1)S(1)} %get-tuple-element.43), channel_id=1, source_target_pairs={{0,24},{8,16},{16,8},{24,0},{1,25},{9,17},{17,9},{25,1},{2,26},{10... | collective-permute-start | bytes 884744 | tf_op jit(solution)/shard_map/ppermute | solution.py:289
  39.6 22.4 %collective-permute-start.4 = (bf16[128,1536]{1,0:T(8,128)(2,1)S(1)}, bf16[128,1536]{1,0:T(8,128)(2,1)S(1)}, u32[]{:S(2)}, u32[]{:S(2)}) collective-permute-start(bf16[128,1536]{1,0:T(8,128)(2,1)S(1)} %collective-permute-done.3.refs_0_), channel_id=1, source_target_pairs={{0,1},{1,0},{2,3},{3,2},{4,5},{5,4},{6,7},{7,6},{8,9},{9,8},{10,11... | collective-permute-start | bytes 1179656 | tf_op jit(solution)/shard_map/ppermute | solution.py:295
  47.6 9.8 %collective-permute-start.12 = (bf16[3,192,256]{2,1,0:T(8,128)(2,1)S(1)}, bf16[3,192,256]{2,1,0:T(8,128)(2,1)S(1)}, u32[]{:S(2)}, u32[]{:S(2)}) collective-permute-start(bf16[3,192,256]{2,1,0:T(8,128)(2,1)S(1)} %collective-permute-done.8), channel_id=1, source_target_pairs={{0,4},{2,6},{4,0},{6,2},{1,5},{3,7},{5,1},{7,3},{8,12},{10,14},{12... | collective-permute-start | bytes 884744 | tf_op jit(solution)/shard_map/ppermute | solution.py:292
  49.2 12.1 %collective-permute-start.9 = (bf16[3,192,256]{2,1,0:T(8,128)(2,1)S(1)}, bf16[3,192,256]{2,1,0:T(8,128)(2,1)S(1)}, u32[]{:S(2)}, u32[]{:S(2)}) collective-permute-start(bf16[3,192,256]{2,1,0:T(8,128)(2,1)S(1)} %get-tuple-element.45), channel_id=1, source_target_pairs={{0,16},{8,0},{16,24},{24,8},{1,17},{9,1},{17,25},{25,9},{2,18},{10... | collective-permute-start | bytes 884744 | tf_op jit(solution)/shard_map/ppermute | solution.py:289
  57.2 35.6 %collective-permute-start.14 = (bf16[4,3,192,256]{3,2,1,0:T(8,128)(2,1)S(1)}, bf16[4,3,192,256]{3,2,1,0:T(8,128)(2,1)S(1)}, u32[]{:S(2)}, u32[]{:S(2)}) collective-permute-start(bf16[4,3,192,256]{3,2,1,0:T(8,128)(2,1)S(1)} %pad_maximum_fusion), channel_id=1, source_target_pairs={{0,2},{2,0},{4,6},{6,4},{1,3},{3,1},{5,7},{7,5},{8,10},{10,8},{12,... | collective-permute-start | bytes 3538952 | tf_op jit(solution)/shard_map/ppermute | solution.py:292
  61.3 7.2 %collective-permute-start.13 = (bf16[3,192,256]{2,1,0:T(8,128)(2,1)S(1)}, bf16[3,192,256]{2,1,0:T(8,128)(2,1)S(1)}, u32[]{:S(2)}, u32[]{:S(2)}) collective-permute-start(bf16[3,192,256]{2,1,0:T(8,128)(2,1)S(1)} %collective-permute-done.9), channel_id=1, source_target_pairs={{0,4},{2,6},{4,0},{6,2},{1,5},{3,7},{5,1},{7,3},{8,12},{10,14},{12... | collective-permute-start | bytes 884744 | tf_op jit(solution)/shard_map/ppermute | solution.py:292
  61.9 30.9 %collective-permute-start.15 = (bf16[3,3,192,256]{3,2,1,0:T(8,128)(2,1)S(1)}, bf16[3,3,192,256]{3,2,1,0:T(8,128)(2,1)S(1)}, u32[]{:S(2)}, u32[]{:S(2)}) collective-permute-start(bf16[3,3,192,256]{3,2,1,0:T(8,128)(2,1)S(1)} %pad_maximum_fusion.1), channel_id=1, source_target_pairs={{0,2},{2,0},{4,6},{6,4},{1,3},{3,1},{5,7},{7,5},{8,10},{10,8},{12,... | collective-permute-start | bytes 2654216 | tf_op jit(solution)/shard_map/ppermute | solution.py:292
  62.0 12.5 %collective-permute-start.6 = (bf16[128,1536]{1,0:T(8,128)(2,1)S(1)}, bf16[128,1536]{1,0:T(8,128)(2,1)S(1)}, u32[]{:S(2)}, u32[]{:S(2)}) collective-permute-start(bf16[128,1536]{1,0:T(8,128)(2,1)S(1)} %collective-permute-done.5.refs_0_), channel_id=1, source_target_pairs={{0,1},{1,0},{2,3},{3,2},{4,5},{5,4},{6,7},{7,6},{8,9},{9,8},{10,11... | collective-permute-start | bytes 1179656 | tf_op jit(solution)/shard_map/ppermute | solution.py:295
  63.6 7.2 %collective-permute-start.17 = (bf16[2,128,256]{2,1,0:T(8,128)(2,1)S(1)}, bf16[2,128,256]{2,1,0:T(8,128)(2,1)S(1)}, u32[]{:S(2)}, u32[]{:S(2)}) collective-permute-start(bf16[2,128,256]{2,1,0:T(8,128)(2,1)S(1)} %get-tuple-element.52), channel_id=1, source_target_pairs={{0,8},{8,24},{16,0},{24,16},{1,9},{9,25},{17,1},{25,17},{2,10},{10... | collective-permute-start | bytes 393224 | tf_op jit(solution)/shard_map/ppermute | solution.py:289
  68.5 5.0 %collective-permute-start.20 = (bf16[2,128,256]{2,1,0:T(8,128)(2,1)S(1)}, bf16[2,128,256]{2,1,0:T(8,128)(2,1)S(1)}, u32[]{:S(2)}, u32[]{:S(2)}) collective-permute-start(bf16[2,128,256]{2,1,0:T(8,128)(2,1)S(1)} %get-tuple-element.57), channel_id=1, source_target_pairs={{0,4},{2,6},{4,0},{6,2},{1,5},{3,7},{5,1},{7,3},{8,12},{10,14},{12... | collective-permute-start | bytes 393224 | tf_op jit(solution)/shard_map/ppermute | solution.py:292
  70.8 10.0 %collective-permute-start.18 = (bf16[2,128,256]{2,1,0:T(8,128)(2,1)S(1)}, bf16[2,128,256]{2,1,0:T(8,128)(2,1)S(1)}, u32[]{:S(2)}, u32[]{:S(2)}) collective-permute-start(bf16[2,128,256]{2,1,0:T(8,128)(2,1)S(1)} %get-tuple-element.54), channel_id=1, source_target_pairs={{0,24},{8,16},{16,8},{24,0},{1,25},{9,17},{17,9},{25,1},{2,26},{10... | collective-permute-start | bytes 393224 | tf_op jit(solution)/shard_map/ppermute | solution.py:289
  73.5 7.4 %collective-permute-start.21 = (bf16[2,128,256]{2,1,0:T(8,128)(2,1)S(1)}, bf16[2,128,256]{2,1,0:T(8,128)(2,1)S(1)}, u32[]{:S(2)}, u32[]{:S(2)}) collective-permute-start(bf16[2,128,256]{2,1,0:T(8,128)(2,1)S(1)} %collective-permute-done.17), channel_id=1, source_target_pairs={{0,4},{2,6},{4,0},{6,2},{1,5},{3,7},{5,1},{7,3},{8,12},{10,14},{12... | collective-permute-start | bytes 393224 | tf_op jit(solution)/shard_map/ppermute | solution.py:292
  74.5 7.9 %collective-permute-start.19 = (bf16[2,128,256]{2,1,0:T(8,128)(2,1)S(1)}, bf16[2,128,256]{2,1,0:T(8,128)(2,1)S(1)}, u32[]{:S(2)}, u32[]{:S(2)}) collective-permute-start(bf16[2,128,256]{2,1,0:T(8,128)(2,1)S(1)} %get-tuple-element.56), channel_id=1, source_target_pairs={{0,16},{8,0},{16,24},{24,8},{1,17},{9,1},{17,25},{25,9},{2,18},{10... | collective-permute-start | bytes 393224 | tf_op jit(solution)/shard_map/ppermute | solution.py:289
  80.8 6.1 %collective-permute-start.16 = (bf16[1,3,192,256]{3,2,1,0:T(8,128)(2,1)S(1)}, bf16[1,3,192,256]{3,2,1,0:T(8,128)(2,1)S(1)}, u32[]{:S(2)}, u32[]{:S(2)}) collective-permute-start(bf16[1,3,192,256]{3,2,1,0:T(8,128)(2,1)S(1)} %bitcast.62), channel_id=1, source_target_pairs={{0,2},{2,0},{4,6},{6,4},{1,3},{3,1},{5,7},{7,5},{8,10},{10,8},{12,... | collective-permute-start | bytes 884744 | tf_op jit(solution)/shard_map/ppermute | solution.py:292
  80.9 5.9 %collective-permute-start.22 = (bf16[2,128,256]{2,1,0:T(8,128)(2,1)S(1)}, bf16[2,128,256]{2,1,0:T(8,128)(2,1)S(1)}, u32[]{:S(2)}, u32[]{:S(2)}) collective-permute-start(bf16[2,128,256]{2,1,0:T(8,128)(2,1)S(1)} %collective-permute-done.18), channel_id=1, source_target_pairs={{0,4},{2,6},{4,0},{6,2},{1,5},{3,7},{5,1},{7,3},{8,12},{10,14},{12... | collective-permute-start | bytes 393224 | tf_op jit(solution)/shard_map/ppermute | solution.py:292
  82.4 13.5 %collective-permute-start.24 = (bf16[4,2,128,256]{3,2,1,0:T(8,128)(2,1)S(1)}, bf16[4,2,128,256]{3,2,1,0:T(8,128)(2,1)S(1)}, u32[]{:S(2)}, u32[]{:S(2)}) collective-permute-start(bf16[4,2,128,256]{3,2,1,0:T(8,128)(2,1)S(1)} %pad_maximum_fusion.2), channel_id=1, source_target_pairs={{0,2},{2,0},{4,6},{6,4},{1,3},{3,1},{5,7},{7,5},{8,10},{10,8},{12,... | collective-permute-start | bytes 1572872 | tf_op jit(solution)/shard_map/ppermute | solution.py:292
  86.8 9.1 %collective-permute-start.25 = (bf16[3,2,128,256]{3,2,1,0:T(8,128)(2,1)S(1)}, bf16[3,2,128,256]{3,2,1,0:T(8,128)(2,1)S(1)}, u32[]{:S(2)}, u32[]{:S(2)}) collective-permute-start(bf16[3,2,128,256]{3,2,1,0:T(8,128)(2,1)S(1)} %pad_maximum_fusion.3), channel_id=1, source_target_pairs={{0,2},{2,0},{4,6},{6,4},{1,3},{3,1},{5,7},{7,5},{8,10},{10,8},{12,... | collective-permute-start | bytes 1179656 | tf_op jit(solution)/shard_map/ppermute | solution.py:292
  86.9 5.9 %collective-permute-start.23 = (bf16[2,128,256]{2,1,0:T(8,128)(2,1)S(1)}, bf16[2,128,256]{2,1,0:T(8,128)(2,1)S(1)}, u32[]{:S(2)}, u32[]{:S(2)}) collective-permute-start(bf16[2,128,256]{2,1,0:T(8,128)(2,1)S(1)} %collective-permute-done.19), channel_id=1, source_target_pairs={{0,4},{2,6},{4,0},{6,2},{1,5},{3,7},{5,1},{7,3},{8,12},{10,14},{12... | collective-permute-start | bytes 393224 | tf_op jit(solution)/shard_map/ppermute | solution.py:292
  92.8 3.1 %collective-permute-start.26 = (bf16[1,2,128,256]{3,2,1,0:T(8,128)(2,1)S(1)}, bf16[1,2,128,256]{3,2,1,0:T(8,128)(2,1)S(1)}, u32[]{:S(2)}, u32[]{:S(2)}) collective-permute-start(bf16[1,2,128,256]{3,2,1,0:T(8,128)(2,1)S(1)} %bitcast.60), channel_id=1, source_target_pairs={{0,2},{2,0},{4,6},{6,4},{1,3},{3,1},{5,7},{7,5},{8,10},{10,8},{12,... | collective-permute-start | bytes 393224 | tf_op jit(solution)/shard_map/ppermute | solution.py:292
  92.8 17.4 %slice-start = ((s8[6291456]{0:T(1024)(128)(4,1)}), s8[4194304]{0:T(1024)(128)(4,1)S(1)}, s32[]{:S(2)}) async-start(s8[6291456]{0:T(1024)(128)(4,1)} %bitcast.21), calls=%async_computation | async-start | bytes 8388608
  100.9 4.6 %collective-permute-start.27 = (bf16[128,256]{1,0:T(8,128)(2,1)S(1)}, bf16[128,256]{1,0:T(8,128)(2,1)S(1)}, u32[]{:S(2)}, u32[]{:S(2)}) collective-permute-start(bf16[128,256]{1,0:T(8,128)(2,1)S(1)} %get-tuple-element.62), channel_id=1, source_target_pairs={{0,16},{8,0},{16,24},{24,8},{1,17},{9,1},{17,25},{25,9},{2,18},{10... | collective-permute-start | bytes 196616 | tf_op jit(solution)/shard_map/ppermute | solution.py:289
  102.3 6.7 %collective-permute-start.28 = (bf16[128,256]{1,0:T(8,128)(2,1)S(1)}, bf16[128,256]{1,0:T(8,128)(2,1)S(1)}, u32[]{:S(2)}, u32[]{:S(2)}) collective-permute-start(bf16[128,256]{1,0:T(8,128)(2,1)S(1)} %get-tuple-element.63), channel_id=1, source_target_pairs={{0,24},{8,16},{16,8},{24,0},{1,25},{9,17},{17,9},{25,1},{2,26},{10... | collective-permute-start | bytes 196616 | tf_op jit(solution)/shard_map/ppermute | solution.py:289
  103.5 6.7 %collective-permute-start.29 = (bf16[128,256]{1,0:T(8,128)(2,1)S(1)}, bf16[128,256]{1,0:T(8,128)(2,1)S(1)}, u32[]{:S(2)}, u32[]{:S(2)}) collective-permute-start(bf16[128,256]{1,0:T(8,128)(2,1)S(1)} %get-tuple-element.64), channel_id=1, source_target_pairs={{0,8},{8,24},{16,0},{24,16},{1,9},{9,25},{17,1},{25,17},{2,10},{10... | collective-permute-start | bytes 196616 | tf_op jit(solution)/shard_map/ppermute | solution.py:289
  110.8 11.2 %collective-permute-start.30 = (bf16[128,1536]{1,0:T(8,128)(2,1)S(1)}, bf16[128,1536]{1,0:T(8,128)(2,1)S(1)}, u32[]{:S(2)}, u32[]{:S(2)}) collective-permute-start(bf16[128,1536]{1,0:T(8,128)(2,1)S(1)} %shard_map.126), channel_id=1, source_target_pairs={{0,1},{1,0},{2,3},{3,2},{4,5},{5,4},{6,7},{7,6},{8,9},{9,8},{10,11... | collective-permute-start | bytes 1179656 | tf_op jit(solution)/shard_map/ppermute | solution.py:295
  (12 other events, 96.0 us)

commit v2 on v1

--- a/solution.py
+++ b/solution.py
@@ -12,6 +12,7 @@
 ANY = pl.BlockSpec(memory_space=pl.ANY)
 VMEM = pl.BlockSpec(memory_space=pltpu.VMEM)
 MIB = 1024 * 1024
+NO_COST = pl.CostEstimate(flops=0, bytes_accessed=0, transcendentals=0)
 ACROSS = (((1,), (1,)), ((), ()))
 
 
@@ -59,11 +60,32 @@
         out_specs=[ANY] * (2 * groups),
         scratch_shapes=[pltpu.SemaphoreType.DMA((groups, 3))],
         compiler_params=params(4),
-        cost_estimate=pl.CostEstimate(
-            flops=0, bytes_accessed=4 * full * (parts * depth + 2 * tok), transcendentals=0
-        ),
+        cost_estimate=NO_COST,
     )(weight, keys, values)
     return outs[:groups], outs[groups:]
+
+
+def stack_kernel(*refs):
+    pieces, out, sems = refs[:-2], refs[-2], refs[-1]
+    started = []
+    for index, piece in enumerate(pieces):
+        started.append(pltpu.make_async_copy(piece, out.at[index], sems.at[index]))
+        started[-1].start()
+    for copy in started:
+        copy.wait()
+
+
+def stack(pieces):
+    shape = (len(pieces), *pieces[0].shape)
+    return pl.pallas_call(
+        stack_kernel,
+        out_shape=jax.ShapeDtypeStruct(shape, pieces[0].dtype),
+        in_specs=[ANY] * len(pieces),
+        out_specs=ANY,
+        scratch_shapes=[pltpu.SemaphoreType.DMA((len(pieces),))],
+        compiler_params=params(4),
+        cost_estimate=NO_COST,
+    )(*pieces)
 
 
 def modulate_kernel(n_head, scale, shift, *refs):
@@ -89,9 +111,7 @@
         out_specs=VMEM,
         scratch_shapes=[pltpu.VMEM((rows, full), jnp.float32)],
         compiler_params=params(12),
-        cost_estimate=pl.CostEstimate(
-            flops=10 * rows * full, bytes_accessed=4 * rows * full, transcendentals=rows
-        ),
+        cost_estimate=NO_COST,
     )(scale_mod.reshape(1, full), shift_mod.reshape(1, full), *pieces)
 
 
@@ -129,11 +149,7 @@
         out_specs=VMEM,
         scratch_shapes=[pltpu.VMEM((3, full, width), jnp.bfloat16)],
         compiler_params=params(16),
-        cost_estimate=pl.CostEstimate(
-            flops=6 * rows * full * width,
-            bytes_accessed=2 * rows * full + 6 * full * width,
-            transcendentals=0,
-        ),
+        cost_estimate=NO_COST,
     )(query_gain.reshape(1, size), key_gain.reshape(1, size), *mods, *arrays)
 
 
@@ -226,11 +242,7 @@
             pltpu.VMEM((many, total), jnp.bfloat16),
         ],
         compiler_params=params(24),
-        cost_estimate=pl.CostEstimate(
-            flops=4 * rows * width * total,
-            bytes_accessed=4 * total * width,
-            transcendentals=rows * (width // size) * total,
-        ),
+        cost_estimate=NO_COST,
     )(qkv, text_keys, text_values, *arrays)
 
 
@@ -254,9 +266,7 @@
         out_specs=VMEM,
         scratch_shapes=[pltpu.VMEM((tok, depth), jnp.bfloat16)],
         compiler_params=params(6),
-        cost_estimate=pl.CostEstimate(
-            flops=2 * tok * depth * share, bytes_accessed=2 * depth * share, transcendentals=0
-        ),
+        cost_estimate=NO_COST,
     )(weight, *pieces)
 
 
@@ -294,57 +304,69 @@
     def across(array, hop):
         return lax.ppermute(array, "head", [(i, (i + hop) % n_head) for i in range(n_head)])
 
-    def finish(found, last, ready):
+    def spread(found, step, *ready):
         bit = rest // 2
         while bit > 1:
-            for (step, bits), piece in list(found.items()):
-                if last is not None:
-                    piece = after(piece, last)
-                found[step, bits | bit] = last = swap(piece, bit)
+            for (mark, bits), piece in list(found.items()):
+                if mark == step:
+                    found[step, bits | bit] = swap(after(piece, *ready), bit)
             bit //= 2
+        return found[step, max(bits for mark, bits in found if mark == step)]
+
+    def finish(found, last_step, early_waits, late_waits):
         names = list(found)
         stacks = [[name] for name in names]
         arrays = [found[name][None] for name in names]
-        if bit:
-            early = [name for name in names[:-1] if name[0] < groups // 2]
-            late = [name for name in names[:-1] if name[0] >= groups // 2]
-            for cut in (early, late, names[-1:]):
-                if not cut:
+        if rest % 2 == 0:
+            early = [name for name in names if name[0] != last_step]
+            late = [name for name in names if name[0] == last_step]
+            for part, waits in ((early, early_waits), (late, late_waits)):
+                if not part:
                     continue
-                pieces = [found[name] for name in cut]
-                stack = jnp.stack(pieces) if len(cut) > 1 else pieces[0][None]
-                if cut[-1] == names[-1]:
-                    stack = after(stack, *ready)
-                arrays.append(swap(stack, bit))
-                stacks.append([(step, bits | bit) for step, bits in cut])
-        return arrays, stacks, last
-
-    moving, last = hidden_states, None
-    mods, hops, sides = [], [], []
-    for step in range(groups):
-        if step:
-            moving = turn(after(moving, *sides[: step - 1]), 1)
-            hops.append(moving)
-        slices = [moving]
+                pieces = [found[name] for name in part]
+                pieces[0] = after(pieces[0], *waits)
+                joined = stack(pieces) if len(part) > 1 else pieces[0][None]
+                arrays.append(swap(joined, 1))
+                stacks.append([(step, bits | 1) for step, bits in part])
+        return arrays, stacks
+
+    packed, pairs = pack(jnp.transpose(qkv_weight, (1, 0, 2)), stale_keys, stale_values, groups)
+    found, cached = {(0, 0): packed[0]}, {(0, 0): pairs[0]}
+    mods, hops, crossed, swapped = [], [], [], []
+
+    def cross(piece, *ready):
+        slices = [piece]
         for hop in range(1, n_head):
-            last = across(moving if last is None else after(moving, last), hop)
-            slices.append(last)
-            sides.append(last)
+            slices.append(across(after(piece, *ready), hop))
+            crossed.append(slices[-1])
         mods.append(modulate(slices, scale_mod, shift_mod))
 
-    packed, pairs = pack(jnp.transpose(qkv_weight, (1, 0, 2)), stale_keys, stale_values, groups)
-    rows, cached = {(0, 0): packed[0]}, {(0, 0): pairs[0]}
-    before = []
-    for step in range(1, groups):
-        before = before + hops[step - 1 : step]
-        rows[step, 0] = turn(after(packed[step], *before), step)
-        before = [rows[step, 0]]
-    for step in range(1, groups):
-        before = [rows[min(step + 1, groups - 1), 0]] + (mods[:step] if step > 1 else [])
-        cached[step, 0] = turn(after(pairs[step], *before), step)
-    arrays, stacks, last = finish(rows, None, mods[-1:])
+    cross(hidden_states)
+    swapped.append(spread(found, 0))
+    order = [1, *range(groups - 1, 1, -1)][: groups - 1]
+    for index, step in enumerate(order):
+        ready = [found[order[0], 0]] if index > 1 else crossed[:1]
+        hops.append(turn(after(hops[-1], *ready) if hops else hidden_states, 1))
+        ready = [found[order[0], 0]] if index > 1 else []
+        found[step, 0] = turn(after(packed[step], *hops[:1], *crossed[:1], *ready), step)
+        cross(hops[-1], *crossed[-1:], *packed[:1])
+    for index, step in enumerate(order):
+        ready = hops[1:2] if index == 0 else []
+        ready += crossed[: (index + 2) * (n_head - 1)] if index < 2 else []
+        swapped.append(spread(found, step, *swapped[-1:], *ready))
+    for index, step in enumerate(order):
+        ready = [found[order[min(1, groups - 2)], 0], *swapped[1:2]]
+        ready += [] if index == 0 else hops[-1:]
+        cached[step, 0] = turn(after(pairs[step], *ready), step)
+    spread(cached, 0, *swapped[2:3])
+    for step in order:
+        spread(cached, step, *swapped[2:3])
+    last_step = order[-1] if order else 0
+    waits = [found[step, 0] for step in order] + [cached[step, 0] for step in order[:1]]
+    waits += crossed[: 1 - n_head] + swapped[:-1] + hops[-1:]
+    arrays, stacks = finish(found, last_step, waits, mods + [cached[last_step, 0]])
     qkv = project(mods, arrays, stacks, groups, rest, query_gain, key_gain)
-    arrays, stacks, _ = finish(cached, last, [])
+    arrays, stacks = finish(cached, last_step, [], [])
     attention = attend(qkv, text_keys, text_values, arrays, stacks, groups, size)
     pieces = [attention[0]] + [turn(attention[step], -step) for step in range(1, groups)]
     terms = []

time: 123 us -> 124 us (level)
  Pallas kernels: 12.9 us -> 14.8 us
    ppermute x14 -> x12, waiting for transfers between devices: 13.7 us -> 8.93 us  [swap(): return lax.ppermute(array, 'rest', [(i, i ^ bit) for i in range(rest)])]
    ppermute x12, waiting for transfers between devices: 29.4 us -> 33.2 us  [turn(): return lax.ppermute(array, 'group', pairs)]
    pallas_call x0 -> x4, Pallas kernels: none -> 1.94 us  [stack(): pl.pallas_call(stack_kernel, out_shape=jax.ShapeDtypeStruct(shape, pieces...]
    ppermute x14 -> x12, starting transfers between devices: 8.51 us -> 9.18 us  [swap(): return lax.ppermute(array, 'rest', [(i, i ^ bit) for i in range(rest)])]
  transfers between devices with their start and end apart: 31 -> 29, of which waited for: 18 -> 16; matrix products, arithmetic and copies ran while one was open for 0% -> 0% of each run, Pallas kernels for 6% -> 7%
where the time goes in v2:
time: 124 us; the launch traced here: 123 us
  waiting for transfers between devices  59 us (48%)
  starting transfers between devices  45.3 us (37%)
  Pallas kernels  14.8 us (12%)
  local copies, waits for them, and re-layouts  3.23 us (3%)
    ppermute x12, waiting for transfers between devices, turn(): return lax.ppermute(array, 'group', pairs)  33.2 us
    ppermute x12, starting transfers between devices, turn(): return lax.ppermute(array, 'group', pairs)  28.4 us
    ppermute x5, waiting for transfers between devices, across(): lax.ppermute(array, 'head', [(i, (i + hop) % n_head) for i in range(n_hea...  16.8 us
    ppermute x12, starting transfers between devices, swap(): return lax.ppermute(array, 'rest', [(i, i ^ bit) for i in range(rest)])  9.18 us
    ppermute x12, waiting for transfers between devices, swap(): return lax.ppermute(array, 'rest', [(i, i ^ bit) for i in range(rest)])  8.93 us
    ppermute x5, starting transfers between devices, across(): lax.ppermute(array, 'head', [(i, (i + hop) % n_head) for i in range(n_hea...  7.68 us
    pallas_call x1, Pallas kernels, attend(): pl.pallas_call(functools.partial(attend_kernel, groups, size, stacks), ou...  4.97 us
    pallas_call x4, Pallas kernels, modulate(): pl.pallas_call(functools.partial(modulate_kernel, len(pieces)), out_shape...  3.3 us
  transfers between devices with their start and end apart: 29, of which 16 were waited for; matrix products, arithmetic and copies ran while one was open for 0% of the time, Pallas kernels for 7%

profile of v2, /device:TPU:0, one launch (start us, length us, event | category | flops | bytes accessed | tf_op | source)
XLA Modules:
  0.0 123.4 jit_solution(15351517768232560747)
XLA Ops:
  0.0 2.9 %collective-permute-start = (bf16[128,1536]{1,0:T(8,128)(2,1)}, bf16[128,1536]{1,0:T(8,128)(2,1)S(1)}, u32[]{:S(2)}, u32[]{:S(2)}) collective-permute-start(bf16[128,1536]{1,0:T(8,128)(2,1)} %refs_0_.1), channel_id=1, source_target_pairs={{0,1},{1,0},{2,3},{3,2},{4,5},{5,4},{6,7},{7,6},{8,9},{9,8},{10,11... | collective-permute-start | bytes 1179656 | tf_op jit(solution)/shard_map/ppermute | solution.py:305
  2.9 1.6 %collective-permute-start.1 = (bf16[128,1536]{1,0:T(8,128)(2,1)}, bf16[128,1536]{1,0:T(8,128)(2,1)S(1)}, u32[]{:S(2)}, u32[]{:S(2)}) collective-permute-start(bf16[128,1536]{1,0:T(8,128)(2,1)} %refs_0_.1), channel_id=1, source_target_pairs={{0,8},{8,24},{16,0},{24,16},{1,9},{9,25},{17,1},{25,17},{2,10},{10... | collective-permute-start | bytes 1179656 | tf_op jit(solution)/shard_map/ppermute | solution.py:299
  8.1 4.2 %collective-permute-done.refs_1_ = bf16[128,1536]{1,0:T(8,128)(2,1)S(1)} collective-permute-done((bf16[128,1536]{1,0:T(8,128)(2,1)}, bf16[128,1536]{1,0:T(8,128)(2,1)S(1)}, u32[]{:S(2)}, u32[]{:S(2)}) %collective-permute-start) | collective-permute-done | bytes 393248 | tf_op jit(solution)/shard_map/ppermute | solution.py:305
  12.3 2.4 %collective-permute-done.1.refs_0_ = bf16[128,1536]{1,0:T(8,128)(2,1)S(1)} collective-permute-done((bf16[128,1536]{1,0:T(8,128)(2,1)}, bf16[128,1536]{1,0:T(8,128)(2,1)S(1)}, u32[]{:S(2)}, u32[]{:S(2)}) %collective-permute-start.1) | collective-permute-done | bytes 393248 | tf_op jit(solution)/shard_map/ppermute | solution.py:299
  16.1 1.5 %collective-permute-start.8 = (bf16[3,192,256]{2,1,0:T(8,128)(2,1)S(1)}, bf16[3,192,256]{2,1,0:T(8,128)(2,1)S(1)}, u32[]{:S(2)}, u32[]{:S(2)}) collective-permute-start(bf16[3,192,256]{2,1,0:T(8,128)(2,1)S(1)} %get-tuple-element.54.refs_0_), channel_id=1, source_target_pairs={{0,4},{2,6},{4,0},{6,2},{1,5},{3,7},{5,1},{7,3},{8,12},{10,14},{12... | collective-permute-start | bytes 884744 | tf_op jit(solution)/shard_map/ppermute | solution.py:302
  17.6 3.3 %collective-permute-start.5 = (bf16[3,192,256]{2,1,0:T(8,128)(2,1)S(1)}, bf16[3,192,256]{2,1,0:T(8,128)(2,1)S(1)}, u32[]{:S(2)}, u32[]{:S(2)}) collective-permute-start(bf16[3,192,256]{2,1,0:T(8,128)(2,1)S(1)} %get-tuple-element.42), channel_id=1, source_target_pairs={{0,8},{8,24},{16,0},{24,16},{1,9},{9,25},{17,1},{25,17},{2,10},{10... | collective-permute-start | bytes 884744 | tf_op jit(solution)/shard_map/ppermute | solution.py:299
  20.8 3.5 %collective-permute-done.2.refs_1_ = bf16[128,1536]{1,0:T(8,128)(2,1)S(1)} collective-permute-done((bf16[128,1536]{1,0:T(8,128)(2,1)S(1)}, bf16[128,1536]{1,0:T(8,128)(2,1)S(1)}, u32[]{:S(2)}, u32[]{:S(2)}) %collective-permute-start.2) | collective-permute-done | bytes 393248 | tf_op jit(solution)/shard_map/ppermute | solution.py:305
  24.3 3.9 %collective-permute-done.3.refs_0_ = bf16[128,1536]{1,0:T(8,128)(2,1)S(1)} collective-permute-done((bf16[128,1536]{1,0:T(8,128)(2,1)S(1)}, bf16[128,1536]{1,0:T(8,128)(2,1)S(1)}, u32[]{:S(2)}, u32[]{:S(2)}) %collective-permute-start.3) | collective-permute-done | bytes 393248 | tf_op jit(solution)/shard_map/ppermute | solution.py:299
  28.2 1.5 %collective-permute-start.4 = (bf16[128,1536]{1,0:T(8,128)(2,1)S(1)}, bf16[128,1536]{1,0:T(8,128)(2,1)S(1)}, u32[]{:S(2)}, u32[]{:S(2)}) collective-permute-start(bf16[128,1536]{1,0:T(8,128)(2,1)S(1)} %collective-permute-done.3.refs_0_), channel_id=1, source_target_pairs={{0,1},{1,0},{2,3},{3,2},{4,5},{5,4},{6,7},{7,6},{8,9},{9,8},{10,11... | collective-permute-start | bytes 1179656 | tf_op jit(solution)/shard_map/ppermute | solution.py:305
  30.8 3.0 %collective-permute-done.5.refs_2_ = bf16[3,192,256]{2,1,0:T(8,128)(2,1)S(1)} collective-permute-done((bf16[3,192,256]{2,1,0:T(8,128)(2,1)S(1)}, bf16[3,192,256]{2,1,0:T(8,128)(2,1)S(1)}, u32[]{:S(2)}, u32[]{:S(2)}) %collective-permute-start.5) | collective-permute-done | bytes 294944 | tf_op jit(solution)/shard_map/ppermute | solution.py:299
  34.9 6.4 %collective-permute-start.6 = (bf16[128,1536]{1,0:T(8,128)(2,1)S(1)}, bf16[128,1536]{1,0:T(8,128)(2,1)S(1)}, u32[]{:S(2)}, u32[]{:S(2)}) collective-permute-start(bf16[128,1536]{1,0:T(8,128)(2,1)S(1)} %collective-permute-done.3.refs_0_), channel_id=1, source_target_pairs={{0,8},{8,24},{16,0},{24,16},{1,9},{9,25},{17,1},{25,17},{2,10},{10... | collective-permute-start | bytes 1179656 | tf_op jit(solution)/shard_map/ppermute | solution.py:299
  41.3 3.2 %collective-permute-start.10 = (bf16[3,192,256]{2,1,0:T(8,128)(2,1)S(1)}, bf16[3,192,256]{2,1,0:T(8,128)(2,1)S(1)}, u32[]{:S(2)}, u32[]{:S(2)}) collective-permute-start(bf16[3,192,256]{2,1,0:T(8,128)(2,1)S(1)} %get-tuple-element.48), channel_id=1, source_target_pairs={{0,24},{8,16},{16,8},{24,0},{1,25},{9,17},{17,9},{25,1},{2,26},{10... | collective-permute-start | bytes 884744 | tf_op jit(solution)/shard_map/ppermute | solution.py:299
  44.6 3.5 %collective-permute-start.14 = (bf16[2,128,256]{2,1,0:T(8,128)(2,1)S(1)}, bf16[2,128,256]{2,1,0:T(8,128)(2,1)S(1)}, u32[]{:S(2)}, u32[]{:S(2)}) collective-permute-start(bf16[2,128,256]{2,1,0:T(8,128)(2,1)S(1)} %get-tuple-element.53), channel_id=1, source_target_pairs={{0,8},{8,24},{16,0},{24,16},{1,9},{9,25},{17,1},{25,17},{2,10},{10... | collective-permute-start | bytes 393224 | tf_op jit(solution)/shard_map/ppermute | solution.py:299
  48.1 7.3 %collective-permute-done.10.refs_0_ = bf16[3,192,256]{2,1,0:T(8,128)(2,1)S(1)} collective-permute-done((bf16[3,192,256]{2,1,0:T(8,128)(2,1)S(1)}, bf16[3,192,256]{2,1,0:T(8,128)(2,1)S(1)}, u32[]{:S(2)}, u32[]{:S(2)}) %collective-permute-start.10) | collective-permute-done | bytes 294944 | tf_op jit(solution)/shard_map/ppermute | solution.py:299
  55.4 7.0 %collective-permute-done.14.refs_1_ = bf16[2,128,256]{2,1,0:T(8,128)(2,1)S(1)} collective-permute-done((bf16[2,128,256]{2,1,0:T(8,128)(2,1)S(1)}, bf16[2,128,256]{2,1,0:T(8,128)(2,1)S(1)}, u32[]{:S(2)}, u32[]{:S(2)}) %collective-permute-start.14) | collective-permute-done | bytes 131104 | tf_op jit(solution)/shard_map/ppermute | solution.py:299
  63.9 1.5 %collective-permute-start.19 = (bf16[2,128,256]{2,1,0:T(8,128)(2,1)S(1)}, bf16[2,128,256]{2,1,0:T(8,128)(2,1)S(1)}, u32[]{:S(2)}, u32[]{:S(2)}) collective-permute-start(bf16[2,128,256]{2,1,0:T(8,128)(2,1)S(1)} %get-tuple-element.61.refs_0_), channel_id=1, source_target_pairs={{0,4},{2,6},{4,0},{6,2},{1,5},{3,7},{5,1},{7,3},{8,12},{10,14},{12... | collective-permute-start | bytes 393224 | tf_op jit(solution)/shard_map/ppermute | solution.py:302
  65.4 1.5 %collective-permute-start.7 = (bf16[128,1536]{1,0:T(8,128)(2,1)S(1)}, bf16[128,1536]{1,0:T(8,128)(2,1)S(1)}, u32[]{:S(2)}, u32[]{:S(2)}) collective-permute-start(bf16[128,1536]{1,0:T(8,128)(2,1)S(1)} %collective-permute-done.6.refs_0_), channel_id=1, source_target_pairs={{0,1},{1,0},{2,3},{3,2},{4,5},{5,4},{6,7},{7,6},{8,9},{9,8},{10,11... | collective-permute-start | bytes 1179656 | tf_op jit(solution)/shard_map/ppermute | solution.py:305
  67.4 1.4 %collective-permute-done.18.refs_2_ = bf16[2,128,256]{2,1,0:T(8,128)(2,1)S(1)} collective-permute-done((bf16[2,128,256]{2,1,0:T(8,128)(2,1)S(1)}, bf16[2,128,256]{2,1,0:T(8,128)(2,1)S(1)}, u32[]{:S(2)}, u32[]{:S(2)}) %collective-permute-start.18) | collective-permute-done | bytes 131104 | tf_op jit(solution)/shard_map/ppermute | solution.py:299
  68.8 1.3 %collective-permute-start.21 = (bf16[2,128,256]{2,1,0:T(8,128)(2,1)S(1)}, bf16[2,128,256]{2,1,0:T(8,128)(2,1)S(1)}, u32[]{:S(2)}, u32[]{:S(2)}) collective-permute-start(bf16[2,128,256]{2,1,0:T(8,128)(2,1)S(1)} %collective-permute-done.18.refs_2_), channel_id=1, source_target_pairs={{0,4},{2,6},{4,0},{6,2},{1,5},{3,7},{5,1},{7,3},{8,12},{10,14},{12... | collective-permute-start | bytes 393224 | tf_op jit(solution)/shard_map/ppermute | solution.py:302
  70.1 1.7 %collective-permute-start.13 = (bf16[3,192,256]{2,1,0:T(8,128)(2,1)S(1)}, bf16[3,192,256]{2,1,0:T(8,128)(2,1)S(1)}, u32[]{:S(2)}, u32[]{:S(2)}) collective-permute-start(bf16[3,192,256]{2,1,0:T(8,128)(2,1)S(1)} %collective-permute-done.10.refs_0_), channel_id=1, source_target_pairs={{0,4},{2,6},{4,0},{6,2},{1,5},{3,7},{5,1},{7,3},{8,12},{10,14},{12... | collective-permute-start | bytes 884744 | tf_op jit(solution)/shard_map/ppermute | solution.py:302
  71.7 1.5 %collective-permute-done.20.refs_4_ = bf16[2,128,256]{2,1,0:T(8,128)(2,1)S(1)} collective-permute-done((bf16[2,128,256]{2,1,0:T(8,128)(2,1)S(1)}, bf16[2,128,256]{2,1,0:T(8,128)(2,1)S(1)}, u32[]{:S(2)}, u32[]{:S(2)}) %collective-permute-start.20) | collective-permute-done | bytes 131104 | tf_op jit(solution)/shard_map/ppermute | solution.py:302
  73.3 2.8 %collective-permute-done.21.refs_5_ = bf16[2,128,256]{2,1,0:T(8,128)(2,1)S(1)} collective-permute-done((bf16[2,128,256]{2,1,0:T(8,128)(2,1)S(1)}, bf16[2,128,256]{2,1,0:T(8,128)(2,1)S(1)}, u32[]{:S(2)}, u32[]{:S(2)}) %collective-permute-start.21) | collective-permute-done | bytes 131104 | tf_op jit(solution)/shard_map/ppermute | solution.py:302
  77.2 2.4 %collective-permute-start.16 = (bf16[2,128,256]{2,1,0:T(8,128)(2,1)S(1)}, bf16[2,128,256]{2,1,0:T(8,128)(2,1)S(1)}, u32[]{:S(2)}, u32[]{:S(2)}) collective-permute-start(bf16[2,128,256]{2,1,0:T(8,128)(2,1)S(1)} %get-tuple-element.56), channel_id=1, source_target_pairs={{0,24},{8,16},{16,8},{24,0},{1,25},{9,17},{17,9},{25,1},{2,26},{10... | collective-permute-start | bytes 393224 | tf_op jit(solution)/shard_map/ppermute | solution.py:299
  83.0 2.0 %collective-permute-done.16.refs_0_ = bf16[2,128,256]{2,1,0:T(8,128)(2,1)S(1)} collective-permute-done((bf16[2,128,256]{2,1,0:T(8,128)(2,1)S(1)}, bf16[2,128,256]{2,1,0:T(8,128)(2,1)S(1)}, u32[]{:S(2)}, u32[]{:S(2)}) %collective-permute-start.16) | collective-permute-done | bytes 131104 | tf_op jit(solution)/shard_map/ppermute | solution.py:299
  85.3 1.3 %collective-permute-start.22 = (bf16[2,128,256]{2,1,0:T(8,128)(2,1)S(1)}, bf16[2,128,256]{2,1,0:T(8,128)(2,1)S(1)}, u32[]{:S(2)}, u32[]{:S(2)}) collective-permute-start(bf16[2,128,256]{2,1,0:T(8,128)(2,1)S(1)} %collective-permute-done.16.refs_0_), channel_id=1, source_target_pairs={{0,4},{2,6},{4,0},{6,2},{1,5},{3,7},{5,1},{7,3},{8,12},{10,14},{12... | collective-permute-start | bytes 393224 | tf_op jit(solution)/shard_map/ppermute | solution.py:302
  86.6 4.6 %collective-permute-done.22.refs_1_ = bf16[2,128,256]{2,1,0:T(8,128)(2,1)S(1)} collective-permute-done((bf16[2,128,256]{2,1,0:T(8,128)(2,1)S(1)}, bf16[2,128,256]{2,1,0:T(8,128)(2,1)S(1)}, u32[]{:S(2)}, u32[]{:S(2)}) %collective-permute-start.22) | collective-permute-done | bytes 131104 | tf_op jit(solution)/shard_map/ppermute | solution.py:302
  91.7 3.0 %shard_map.125.qkv = bf16[3,512,256]{2,1,0:T(8,128)(2,1)S(1)} custom-call(f32[1,128]{1,0:T(1,128)S(1)} %bitcast.48, f32[1,128]{1,0:T(1,128)S(1)} %bitcast.49, bf16[128,3072]{1,0:T(8,128)(2,1)S(1)} %shard_map.118.refs_0_, bf16[128,3072]{1,0:T(8,128)(2,1)S(1)} %shard_map.120.refs_1_, bf16[128,3072]{1,0:T(8,128)(2,1)S(1)} %shard_map.121.refs_2_, ...), custom_call_target="tpu_custom_call" | custom-call | tf_op jit(solution)/shard_map/pallas_call | solution.py:145
  94.7 5.0 %shard_map.128 = (bf16[128,256]{1,0:T(8,128)(2,1)S(1)}, bf16[128,256]{1,0:T(8,128)(2,1)S(1)}, bf16[128,256]{1,0:T(8,128)(2,1)S(1)}, bf16[128,256]{1,0:T(8,128)(2,1)S(1)}) custom-call(bf16[3,512,256]{2,1,0:T(8,128)(2,1)S(1)} %shard_map.125.qkv, bf16[512,1024]{1,0:T(8,128)(2,1)S(1)} %copy-done.1, bf16[512,1024]{1,0:T(8,128)(2,1)S(1)} %copy-done.2, ...), custom_call_target="tpu_custom_call" | custom-call | tf_op jit(solution)/shard_map/pallas_call | solution.py:233
  99.7 3.9 %collective-permute-start.25 = (bf16[128,256]{1,0:T(8,128)(2,1)S(1)}, bf16[128,256]{1,0:T(8,128)(2,1)S(1)}, u32[]{:S(2)}, u32[]{:S(2)}) collective-permute-start(bf16[128,256]{1,0:T(8,128)(2,1)S(1)} %get-tuple-element.66), channel_id=1, source_target_pairs={{0,16},{8,0},{16,24},{24,8},{1,17},{9,1},{17,25},{25,9},{2,18},{10... | collective-permute-start | bytes 196616 | tf_op jit(solution)/shard_map/ppermute | solution.py:299
  104.7 1.3 %collective-permute-done.25.refs_1_ = bf16[128,256]{1,0:T(8,128)(2,1)S(1)} collective-permute-done((bf16[128,256]{1,0:T(8,128)(2,1)S(1)}, bf16[128,256]{1,0:T(8,128)(2,1)S(1)}, u32[]{:S(2)}, u32[]{:S(2)}) %collective-permute-start.25) | collective-permute-done | bytes 65568 | tf_op jit(solution)/shard_map/ppermute | solution.py:299
  106.0 4.2 %collective-permute-done.26.refs_2_ = bf16[128,256]{1,0:T(8,128)(2,1)S(1)} collective-permute-done((bf16[128,256]{1,0:T(8,128)(2,1)S(1)}, bf16[128,256]{1,0:T(8,128)(2,1)S(1)}, u32[]{:S(2)}, u32[]{:S(2)}) %collective-permute-start.26) | collective-permute-done | bytes 65568 | tf_op jit(solution)/shard_map/ppermute | solution.py:299
  113.5 9.1 %collective-permute-done.28 = bf16[128,1536]{1,0:T(8,128)(2,1)S(1)} collective-permute-done((bf16[128,1536]{1,0:T(8,128)(2,1)S(1)}, bf16[128,1536]{1,0:T(8,128)(2,1)S(1)}, u32[]{:S(2)}, u32[]{:S(2)}) %collective-permute-start.28) | collective-permute-done | bytes 393248 | tf_op jit(solution)/shard_map/ppermute | solution.py:305
  (67 shorter events, 19.4 us)
Async XLA Ops:
  0.0 12.3 %collective-permute-start = (bf16[128,1536]{1,0:T(8,128)(2,1)}, bf16[128,1536]{1,0:T(8,128)(2,1)S(1)}, u32[]{:S(2)}, u32[]{:S(2)}) collective-permute-start(bf16[128,1536]{1,0:T(8,128)(2,1)} %refs_0_.1), channel_id=1, source_target_pairs={{0,1},{1,0},{2,3},{3,2},{4,5},{5,4},{6,7},{7,6},{8,9},{9,8},{10,11... | collective-permute-start | bytes 1179656 | tf_op jit(solution)/shard_map/ppermute | solution.py:305
  2.9 11.7 %collective-permute-start.1 = (bf16[128,1536]{1,0:T(8,128)(2,1)}, bf16[128,1536]{1,0:T(8,128)(2,1)S(1)}, u32[]{:S(2)}, u32[]{:S(2)}) collective-permute-start(bf16[128,1536]{1,0:T(8,128)(2,1)} %refs_0_.1), channel_id=1, source_target_pairs={{0,8},{8,24},{16,0},{24,16},{1,9},{9,25},{17,1},{25,17},{2,10},{10... | collective-permute-start | bytes 1179656 | tf_op jit(solution)/shard_map/ppermute | solution.py:299
  14.6 9.7 %collective-permute-start.2 = (bf16[128,1536]{1,0:T(8,128)(2,1)S(1)}, bf16[128,1536]{1,0:T(8,128)(2,1)S(1)}, u32[]{:S(2)}, u32[]{:S(2)}) collective-permute-start(bf16[128,1536]{1,0:T(8,128)(2,1)S(1)} %collective-permute-done.1.refs_0_), channel_id=1, source_target_pairs={{0,1},{1,0},{2,3},{3,2},{4,5},{5,4},{6,7},{7,6},{8,9},{9,8},{10,11... | collective-permute-start | bytes 1179656 | tf_op jit(solution)/shard_map/ppermute | solution.py:305
  15.1 13.0 %collective-permute-start.3 = (bf16[128,1536]{1,0:T(8,128)(2,1)S(1)}, bf16[128,1536]{1,0:T(8,128)(2,1)S(1)}, u32[]{:S(2)}, u32[]{:S(2)}) collective-permute-start(bf16[128,1536]{1,0:T(8,128)(2,1)S(1)} %collective-permute-done.1.refs_0_), channel_id=1, source_target_pairs={{0,8},{8,24},{16,0},{24,16},{1,9},{9,25},{17,1},{25,17},{2,10},{10... | collective-permute-start | bytes 1179656 | tf_op jit(solution)/shard_map/ppermute | solution.py:299
  16.1 14.8 %collective-permute-start.8 = (bf16[3,192,256]{2,1,0:T(8,128)(2,1)S(1)}, bf16[3,192,256]{2,1,0:T(8,128)(2,1)S(1)}, u32[]{:S(2)}, u32[]{:S(2)}) collective-permute-start(bf16[3,192,256]{2,1,0:T(8,128)(2,1)S(1)} %get-tuple-element.54.refs_0_), channel_id=1, source_target_pairs={{0,4},{2,6},{4,0},{6,2},{1,5},{3,7},{5,1},{7,3},{8,12},{10,14},{12... | collective-permute-start | bytes 884744 | tf_op jit(solution)/shard_map/ppermute | solution.py:302
  17.6 16.3 %collective-permute-start.5 = (bf16[3,192,256]{2,1,0:T(8,128)(2,1)S(1)}, bf16[3,192,256]{2,1,0:T(8,128)(2,1)S(1)}, u32[]{:S(2)}, u32[]{:S(2)}) collective-permute-start(bf16[3,192,256]{2,1,0:T(8,128)(2,1)S(1)} %get-tuple-element.42), channel_id=1, source_target_pairs={{0,8},{8,24},{16,0},{24,16},{1,9},{9,25},{17,1},{25,17},{2,10},{10... | collective-permute-start | bytes 884744 | tf_op jit(solution)/shard_map/ppermute | solution.py:299
  28.2 16.3 %collective-permute-start.4 = (bf16[128,1536]{1,0:T(8,128)(2,1)S(1)}, bf16[128,1536]{1,0:T(8,128)(2,1)S(1)}, u32[]{:S(2)}, u32[]{:S(2)}) collective-permute-start(bf16[128,1536]{1,0:T(8,128)(2,1)S(1)} %collective-permute-done.3.refs_0_), channel_id=1, source_target_pairs={{0,1},{1,0},{2,3},{3,2},{4,5},{5,4},{6,7},{7,6},{8,9},{9,8},{10,11... | collective-permute-start | bytes 1179656 | tf_op jit(solution)/shard_map/ppermute | solution.py:305
  29.7 14.7 %collective-permute-start.9 = (bf16[3,192,256]{2,1,0:T(8,128)(2,1)S(1)}, bf16[3,192,256]{2,1,0:T(8,128)(2,1)S(1)}, u32[]{:S(2)}, u32[]{:S(2)}) collective-permute-start(bf16[3,192,256]{2,1,0:T(8,128)(2,1)S(1)} %get-tuple-element.46), channel_id=1, source_target_pairs={{0,16},{8,0},{16,24},{24,8},{1,17},{9,1},{17,25},{25,9},{2,18},{10... | collective-permute-start | bytes 884744 | tf_op jit(solution)/shard_map/ppermute | solution.py:299
  33.9 10.6 %collective-permute-start.11 = (bf16[3,192,256]{2,1,0:T(8,128)(2,1)S(1)}, bf16[3,192,256]{2,1,0:T(8,128)(2,1)S(1)}, u32[]{:S(2)}, u32[]{:S(2)}) collective-permute-start(bf16[3,192,256]{2,1,0:T(8,128)(2,1)S(1)} %collective-permute-done.5.refs_2_), channel_id=1, source_target_pairs={{0,4},{2,6},{4,0},{6,2},{1,5},{3,7},{5,1},{7,3},{8,12},{10,14},{12... | collective-permute-start | bytes 884744 | tf_op jit(solution)/shard_map/ppermute | solution.py:302
  34.9 20.5 %collective-permute-start.6 = (bf16[128,1536]{1,0:T(8,128)(2,1)S(1)}, bf16[128,1536]{1,0:T(8,128)(2,1)S(1)}, u32[]{:S(2)}, u32[]{:S(2)}) collective-permute-start(bf16[128,1536]{1,0:T(8,128)(2,1)S(1)} %collective-permute-done.3.refs_0_), channel_id=1, source_target_pairs={{0,8},{8,24},{16,0},{24,16},{1,9},{9,25},{17,1},{25,17},{2,10},{10... | collective-permute-start | bytes 1179656 | tf_op jit(solution)/shard_map/ppermute | solution.py:299
  41.3 14.1 %collective-permute-start.10 = (bf16[3,192,256]{2,1,0:T(8,128)(2,1)S(1)}, bf16[3,192,256]{2,1,0:T(8,128)(2,1)S(1)}, u32[]{:S(2)}, u32[]{:S(2)}) collective-permute-start(bf16[3,192,256]{2,1,0:T(8,128)(2,1)S(1)} %get-tuple-element.48), channel_id=1, source_target_pairs={{0,24},{8,16},{16,8},{24,0},{1,25},{9,17},{17,9},{25,1},{2,26},{10... | collective-permute-start | bytes 884744 | tf_op jit(solution)/shard_map/ppermute | solution.py:299
  44.5 17.9 %collective-permute-start.12 = (bf16[3,192,256]{2,1,0:T(8,128)(2,1)S(1)}, bf16[3,192,256]{2,1,0:T(8,128)(2,1)S(1)}, u32[]{:S(2)}, u32[]{:S(2)}) collective-permute-start(bf16[3,192,256]{2,1,0:T(8,128)(2,1)S(1)} %collective-permute-done.9.refs_3_), channel_id=1, source_target_pairs={{0,4},{2,6},{4,0},{6,2},{1,5},{3,7},{5,1},{7,3},{8,12},{10,14},{12... | collective-permute-start | bytes 884744 | tf_op jit(solution)/shard_map/ppermute | solution.py:302
  44.6 35.1 %copy-start.3 = (bf16[128,1536]{1,0:T(8,128)(2,1)S(1)}, bf16[128,1536]{1,0:T(8,128)(2,1)}, u32[]{:S(2)}) copy-start(bf16[128,1536]{1,0:T(8,128)(2,1)} %refs_0_.1) | copy-start | bytes 1179652
  44.6 35.1 %copy-start.6 = (f32[3072]{0:T(1024)S(1)}, f32[3072]{0:T(1024)}, u32[]{:S(2)}) copy-start(f32[3072]{0:T(1024)} %param.14) | copy-start | bytes 36868
  44.6 35.0 %copy-start.7 = (f32[3072]{0:T(1024)S(1)}, f32[3072]{0:T(1024)}, u32[]{:S(2)}) copy-start(f32[3072]{0:T(1024)} %param.13) | copy-start | bytes 36868
  44.6 17.8 %collective-permute-start.14 = (bf16[2,128,256]{2,1,0:T(8,128)(2,1)S(1)}, bf16[2,128,256]{2,1,0:T(8,128)(2,1)S(1)}, u32[]{:S(2)}, u32[]{:S(2)}) collective-permute-start(bf16[2,128,256]{2,1,0:T(8,128)(2,1)S(1)} %get-tuple-element.53), channel_id=1, source_target_pairs={{0,8},{8,24},{16,0},{24,16},{1,9},{9,25},{17,1},{25,17},{2,10},{10... | collective-permute-start | bytes 393224 | tf_op jit(solution)/shard_map/ppermute | solution.py:299
  62.8 28.8 %collective-permute-start.15 = (bf16[6,3,192,256]{3,2,1,0:T(8,128)(2,1)S(1)}, bf16[6,3,192,256]{3,2,1,0:T(8,128)(2,1)S(1)}, u32[]{:S(2)}, u32[]{:S(2)}) collective-permute-start(bf16[6,3,192,256]{3,2,1,0:T(8,128)(2,1)S(1)} %shard_map.123), channel_id=1, source_target_pairs={{0,2},{2,0},{4,6},{6,4},{1,3},{3,1},{5,7},{7,5},{8,10},{10,8},{12,... | collective-permute-start | bytes 5308424 | tf_op jit(solution)/shard_map/ppermute | solution.py:302
  62.9 5.9 %collective-permute-start.18 = (bf16[2,128,256]{2,1,0:T(8,128)(2,1)S(1)}, bf16[2,128,256]{2,1,0:T(8,128)(2,1)S(1)}, u32[]{:S(2)}, u32[]{:S(2)}) collective-permute-start(bf16[2,128,256]{2,1,0:T(8,128)(2,1)S(1)} %get-tuple-element.60), channel_id=1, source_target_pairs={{0,16},{8,0},{16,24},{24,8},{1,17},{9,1},{17,25},{25,9},{2,18},{10... | collective-permute-start | bytes 393224 | tf_op jit(solution)/shard_map/ppermute | solution.py:299
  63.9 6.2 %collective-permute-start.19 = (bf16[2,128,256]{2,1,0:T(8,128)(2,1)S(1)}, bf16[2,128,256]{2,1,0:T(8,128)(2,1)S(1)}, u32[]{:S(2)}, u32[]{:S(2)}) collective-permute-start(bf16[2,128,256]{2,1,0:T(8,128)(2,1)S(1)} %get-tuple-element.61.refs_0_), channel_id=1, source_target_pairs={{0,4},{2,6},{4,0},{6,2},{1,5},{3,7},{5,1},{7,3},{8,12},{10,14},{12... | collective-permute-start | bytes 393224 | tf_op jit(solution)/shard_map/ppermute | solution.py:302
  65.4 16.7 %collective-permute-start.7 = (bf16[128,1536]{1,0:T(8,128)(2,1)S(1)}, bf16[128,1536]{1,0:T(8,128)(2,1)S(1)}, u32[]{:S(2)}, u32[]{:S(2)}) collective-permute-start(bf16[128,1536]{1,0:T(8,128)(2,1)S(1)} %collective-permute-done.6.refs_0_), channel_id=1, source_target_pairs={{0,1},{1,0},{2,3},{3,2},{4,5},{5,4},{6,7},{7,6},{8,9},{9,8},{10,11... | collective-permute-start | bytes 1179656 | tf_op jit(solution)/shard_map/ppermute | solution.py:305
  66.9 6.4 %collective-permute-start.20 = (bf16[2,128,256]{2,1,0:T(8,128)(2,1)S(1)}, bf16[2,128,256]{2,1,0:T(8,128)(2,1)S(1)}, u32[]{:S(2)}, u32[]{:S(2)}) collective-permute-start(bf16[2,128,256]{2,1,0:T(8,128)(2,1)S(1)} %collective-permute-done.14.refs_1_), channel_id=1, source_target_pairs={{0,4},{2,6},{4,0},{6,2},{1,5},{3,7},{5,1},{7,3},{8,12},{10,14},{12... | collective-permute-start | bytes 393224 | tf_op jit(solution)/shard_map/ppermute | solution.py:302
  68.8 7.3 %collective-permute-start.21 = (bf16[2,128,256]{2,1,0:T(8,128)(2,1)S(1)}, bf16[2,128,256]{2,1,0:T(8,128)(2,1)S(1)}, u32[]{:S(2)}, u32[]{:S(2)}) collective-permute-start(bf16[2,128,256]{2,1,0:T(8,128)(2,1)S(1)} %collective-permute-done.18.refs_2_), channel_id=1, source_target_pairs={{0,4},{2,6},{4,0},{6,2},{1,5},{3,7},{5,1},{7,3},{8,12},{10,14},{12... | collective-permute-start | bytes 393224 | tf_op jit(solution)/shard_map/ppermute | solution.py:302
  70.1 14.9 %collective-permute-start.13 = (bf16[3,192,256]{2,1,0:T(8,128)(2,1)S(1)}, bf16[3,192,256]{2,1,0:T(8,128)(2,1)S(1)}, u32[]{:S(2)}, u32[]{:S(2)}) collective-permute-start(bf16[3,192,256]{2,1,0:T(8,128)(2,1)S(1)} %collective-permute-done.10.refs_0_), channel_id=1, source_target_pairs={{0,4},{2,6},{4,0},{6,2},{1,5},{3,7},{5,1},{7,3},{8,12},{10,14},{12... | collective-permute-start | bytes 884744 | tf_op jit(solution)/shard_map/ppermute | solution.py:302
  77.1 17.6 %collective-permute-start.23 = (bf16[6,2,128,256]{3,2,1,0:T(8,128)(2,1)S(1)}, bf16[6,2,128,256]{3,2,1,0:T(8,128)(2,1)S(1)}, u32[]{:S(2)}, u32[]{:S(2)}) collective-permute-start(bf16[6,2,128,256]{3,2,1,0:T(8,128)(2,1)S(1)} %shard_map.126), channel_id=1, source_target_pairs={{0,2},{2,0},{4,6},{6,4},{1,3},{3,1},{5,7},{7,5},{8,10},{10,8},{12,... | collective-permute-start | bytes 2359304 | tf_op jit(solution)/shard_map/ppermute | solution.py:302
  77.2 7.8 %collective-permute-start.16 = (bf16[2,128,256]{2,1,0:T(8,128)(2,1)S(1)}, bf16[2,128,256]{2,1,0:T(8,128)(2,1)S(1)}, u32[]{:S(2)}, u32[]{:S(2)}) collective-permute-start(bf16[2,128,256]{2,1,0:T(8,128)(2,1)S(1)} %get-tuple-element.56), channel_id=1, source_target_pairs={{0,24},{8,16},{16,8},{24,0},{1,25},{9,17},{17,9},{25,1},{2,26},{10... | collective-permute-start | bytes 393224 | tf_op jit(solution)/shard_map/ppermute | solution.py:299
  85.2 6.4 %collective-permute-start.17 = (bf16[2,3,192,256]{3,2,1,0:T(8,128)(2,1)S(1)}, bf16[2,3,192,256]{3,2,1,0:T(8,128)(2,1)S(1)}, u32[]{:S(2)}, u32[]{:S(2)}) collective-permute-start(bf16[2,3,192,256]{3,2,1,0:T(8,128)(2,1)S(1)} %shard_map.124), channel_id=1, source_target_pairs={{0,2},{2,0},{4,6},{6,4},{1,3},{3,1},{5,7},{7,5},{8,10},{10,8},{12,... | collective-permute-start | bytes 1769480 | tf_op jit(solution)/shard_map/ppermute | solution.py:302
  85.3 5.9 %collective-permute-start.22 = (bf16[2,128,256]{2,1,0:T(8,128)(2,1)S(1)}, bf16[2,128,256]{2,1,0:T(8,128)(2,1)S(1)}, u32[]{:S(2)}, u32[]{:S(2)}) collective-permute-start(bf16[2,128,256]{2,1,0:T(8,128)(2,1)S(1)} %collective-permute-done.16.refs_0_), channel_id=1, source_target_pairs={{0,4},{2,6},{4,0},{6,2},{1,5},{3,7},{5,1},{7,3},{8,12},{10,14},{12... | collective-permute-start | bytes 393224 | tf_op jit(solution)/shard_map/ppermute | solution.py:302
  91.5 3.2 %collective-permute-start.24 = (bf16[2,2,128,256]{3,2,1,0:T(8,128)(2,1)S(1)}, bf16[2,2,128,256]{3,2,1,0:T(8,128)(2,1)S(1)}, u32[]{:S(2)}, u32[]{:S(2)}) collective-permute-start(bf16[2,2,128,256]{3,2,1,0:T(8,128)(2,1)S(1)} %shard_map.127), channel_id=1, source_target_pairs={{0,2},{2,0},{4,6},{6,4},{1,3},{3,1},{5,7},{7,5},{8,10},{10,8},{12,... | collective-permute-start | bytes 786440 | tf_op jit(solution)/shard_map/ppermute | solution.py:302
  99.7 6.3 %collective-permute-start.25 = (bf16[128,256]{1,0:T(8,128)(2,1)S(1)}, bf16[128,256]{1,0:T(8,128)(2,1)S(1)}, u32[]{:S(2)}, u32[]{:S(2)}) collective-permute-start(bf16[128,256]{1,0:T(8,128)(2,1)S(1)} %get-tuple-element.66), channel_id=1, source_target_pairs={{0,16},{8,0},{16,24},{24,8},{1,17},{9,1},{17,25},{25,9},{2,18},{10... | collective-permute-start | bytes 196616 | tf_op jit(solution)/shard_map/ppermute | solution.py:299
  103.6 6.7 %collective-permute-start.26 = (bf16[128,256]{1,0:T(8,128)(2,1)S(1)}, bf16[128,256]{1,0:T(8,128)(2,1)S(1)}, u32[]{:S(2)}, u32[]{:S(2)}) collective-permute-start(bf16[128,256]{1,0:T(8,128)(2,1)S(1)} %get-tuple-element.67), channel_id=1, source_target_pairs={{0,24},{8,16},{16,8},{24,0},{1,25},{9,17},{17,9},{25,1},{2,26},{10... | collective-permute-start | bytes 196616 | tf_op jit(solution)/shard_map/ppermute | solution.py:299
  104.7 6.2 %collective-permute-start.27 = (bf16[128,256]{1,0:T(8,128)(2,1)S(1)}, bf16[128,256]{1,0:T(8,128)(2,1)S(1)}, u32[]{:S(2)}, u32[]{:S(2)}) collective-permute-start(bf16[128,256]{1,0:T(8,128)(2,1)S(1)} %get-tuple-element.68), channel_id=1, source_target_pairs={{0,8},{8,24},{16,0},{24,16},{1,9},{9,25},{17,1},{25,17},{2,10},{10... | collective-permute-start | bytes 196616 | tf_op jit(solution)/shard_map/ppermute | solution.py:299
  111.6 11.0 %collective-permute-start.28 = (bf16[128,1536]{1,0:T(8,128)(2,1)S(1)}, bf16[128,1536]{1,0:T(8,128)(2,1)S(1)}, u32[]{:S(2)}, u32[]{:S(2)}) collective-permute-start(bf16[128,1536]{1,0:T(8,128)(2,1)S(1)} %shard_map.130), channel_id=1, source_target_pairs={{0,1},{1,0},{2,3},{3,2},{4,5},{5,4},{6,7},{7,6},{8,9},{9,8},{10,11... | collective-permute-start | bytes 1179656 | tf_op jit(solution)/shard_map/ppermute | solution.py:305
  (10 other events, 78.5 us)

commit v3 on v2

--- a/solution.py
+++ b/solution.py
@@ -343,30 +343,34 @@
 
     cross(hidden_states)
     swapped.append(spread(found, 0))
+    ahead = []
     order = [1, *range(groups - 1, 1, -1)][: groups - 1]
     for index, step in enumerate(order):
         ready = [found[order[0], 0]] if index > 1 else crossed[:1]
         hops.append(turn(after(hops[-1], *ready) if hops else hidden_states, 1))
         ready = [found[order[0], 0]] if index > 1 else []
-        found[step, 0] = turn(after(packed[step], *hops[:1], *crossed[:1], *ready), step)
-        cross(hops[-1], *crossed[-1:], *packed[:1])
+        ready += [*hops[:1], *crossed[:1]] if index else []
+        found[step, 0] = turn(after(packed[step], *ready), step)
+        if index == len(order) - 1:
+            ahead = [spread(cached, 0, *hops[1:2])]
+        cross(hops[-1], *crossed[-1:], *packed[:1], *ahead)
     for index, step in enumerate(order):
         ready = hops[1:2] if index == 0 else []
-        ready += crossed[: (index + 2) * (n_head - 1)] if index < 2 else []
+        ready += crossed[: (index + 2) * (n_head - 1)] if index < 2 else [cached[order[0], 0]]
         swapped.append(spread(found, step, *swapped[-1:], *ready))
-    for index, step in enumerate(order):
-        ready = [found[order[min(1, groups - 2)], 0], *swapped[1:2]]
-        ready += [] if index == 0 else hops[-1:]
+        if index == 0:
+            ready = [found[order[min(1, groups - 2)], 0], swapped[-1]]
+            cached[step, 0] = turn(after(pairs[step], *ready), step)
+    for step in order[1:]:
+        ready = [found[order[1], 0], *swapped[1:2], *hops[-1:]]
         cached[step, 0] = turn(after(pairs[step], *ready), step)
-    spread(cached, 0, *swapped[2:3])
-    for step in order:
-        spread(cached, step, *swapped[2:3])
+    ahead += [spread(cached, step, *swapped[2:3]) for step in order]
     last_step = order[-1] if order else 0
-    waits = [found[step, 0] for step in order] + [cached[step, 0] for step in order[:1]]
-    waits += crossed[: 1 - n_head] + swapped[:-1] + hops[-1:]
+    waits = [array[step, 0] for array in (found, cached) for step in order]
+    waits += crossed + swapped + ahead
     arrays, stacks = finish(found, last_step, waits, mods + [cached[last_step, 0]])
     qkv = project(mods, arrays, stacks, groups, rest, query_gain, key_gain)
-    arrays, stacks = finish(cached, last_step, [], [])
+    arrays, stacks = finish(cached, last_step, [cached[last_step, 0]], [])
     attention = attend(qkv, text_keys, text_values, arrays, stacks, groups, size)
     pieces = [attention[0]] + [turn(attention[step], -step) for step in range(1, groups)]
     terms = []

time: 124 us -> 118 us (0.952)
  waiting for transfers between devices: 59 us -> 50.7 us
  starting transfers between devices: 45.3 us -> 47.7 us
    ppermute x12, waiting for transfers between devices: 33.2 us -> 25.5 us  [turn(): return lax.ppermute(array, 'group', pairs)]
    ppermute x12, starting transfers between devices: 28.4 us -> 30.7 us  [turn(): return lax.ppermute(array, 'group', pairs)]
  transfers between devices with their start and end apart: 29 -> 29, of which waited for: 16 -> 17; matrix products, arithmetic and copies ran while one was open for 0% -> 0% of each run, Pallas kernels for 7% -> 8%
where the time goes in v3:
time: 118 us
  waiting for transfers between devices  50.7 us (43%)
  starting transfers between devices  47.7 us (40%)
  Pallas kernels  14.9 us (13%)
  local copies, waits for them, and re-layouts  3.22 us (3%)
    ppermute x12, starting transfers between devices, turn(): return lax.ppermute(array, 'group', pairs)  30.7 us
    ppermute x12, waiting for transfers between devices, turn(): return lax.ppermute(array, 'group', pairs)  25.5 us
    ppermute x5, waiting for transfers between devices, across(): lax.ppermute(array, 'head', [(i, (i + hop) % n_head) for i in range(n_hea...  16.3 us
    ppermute x12, starting transfers between devices, swap(): return lax.ppermute(array, 'rest', [(i, i ^ bit) for i in range(rest)])  9.16 us
    ppermute x12, waiting for transfers between devices, swap(): return lax.ppermute(array, 'rest', [(i, i ^ bit) for i in range(rest)])  8.93 us
    ppermute x5, starting transfers between devices, across(): lax.ppermute(array, 'head', [(i, (i + hop) % n_head) for i in range(n_hea...  7.9 us
    pallas_call x1, Pallas kernels, attend(): pl.pallas_call(functools.partial(attend_kernel, groups, size, stacks), ou...  4.98 us
    pallas_call x4, Pallas kernels, modulate(): pl.pallas_call(functools.partial(modulate_kernel, len(pieces)), out_shape...  3.3 us
  transfers between devices with their start and end apart: 29, of which 17 were waited for; matrix products, arithmetic and copies ran while one was open for 0% of the time, Pallas kernels for 8%

profile of v3, /device:TPU:0, one launch (start us, length us, event | category | flops | bytes accessed | tf_op | source)
XLA Modules:
  0.0 117.6 jit_solution(139440101576222534)
XLA Ops:
  0.0 2.9 %collective-permute-start = (bf16[128,1536]{1,0:T(8,128)(2,1)}, bf16[128,1536]{1,0:T(8,128)(2,1)S(1)}, u32[]{:S(2)}, u32[]{:S(2)}) collective-permute-start(bf16[128,1536]{1,0:T(8,128)(2,1)} %refs_0_.1), channel_id=1, source_target_pairs={{0,1},{1,0},{2,3},{3,2},{4,5},{5,4},{6,7},{7,6},{8,9},{9,8},{10,11... | collective-permute-start | bytes 1179656 | tf_op jit(solution)/shard_map/ppermute | solution.py:305
  2.9 1.6 %collective-permute-start.1 = (bf16[128,1536]{1,0:T(8,128)(2,1)}, bf16[128,1536]{1,0:T(8,128)(2,1)S(1)}, u32[]{:S(2)}, u32[]{:S(2)}) collective-permute-start(bf16[128,1536]{1,0:T(8,128)(2,1)} %refs_0_.1), channel_id=1, source_target_pairs={{0,8},{8,24},{16,0},{24,16},{1,9},{9,25},{17,1},{25,17},{2,10},{10... | collective-permute-start | bytes 1179656 | tf_op jit(solution)/shard_map/ppermute | solution.py:299
  4.5 1.3 %copy-done = bf16[192,3,1024]{2,0,1:T(8,128)(2,1)S(1)} copy-done((bf16[192,3,1024]{2,0,1:T(8,128)(2,1)S(1)}, bf16[192,3,1024]{2,0,1:T(8,128)(2,1)}, u32[]{:S(2)}) %copy-start) | copy-done | bytes 1179672
  8.1 4.2 %collective-permute-done.refs_1_ = bf16[128,1536]{1,0:T(8,128)(2,1)S(1)} collective-permute-done((bf16[128,1536]{1,0:T(8,128)(2,1)}, bf16[128,1536]{1,0:T(8,128)(2,1)S(1)}, u32[]{:S(2)}, u32[]{:S(2)}) %collective-permute-start) | collective-permute-done | bytes 393248 | tf_op jit(solution)/shard_map/ppermute | solution.py:305
  12.3 2.4 %collective-permute-done.1.refs_0_ = bf16[128,1536]{1,0:T(8,128)(2,1)S(1)} collective-permute-done((bf16[128,1536]{1,0:T(8,128)(2,1)}, bf16[128,1536]{1,0:T(8,128)(2,1)S(1)}, u32[]{:S(2)}, u32[]{:S(2)}) %collective-permute-start.1) | collective-permute-done | bytes 393248 | tf_op jit(solution)/shard_map/ppermute | solution.py:299
  16.1 3.3 %collective-permute-start.5 = (bf16[3,192,256]{2,1,0:T(8,128)(2,1)S(1)}, bf16[3,192,256]{2,1,0:T(8,128)(2,1)S(1)}, u32[]{:S(2)}, u32[]{:S(2)}) collective-permute-start(bf16[3,192,256]{2,1,0:T(8,128)(2,1)S(1)} %get-tuple-element.41), channel_id=1, source_target_pairs={{0,8},{8,24},{16,0},{24,16},{1,9},{9,25},{17,1},{25,17},{2,10},{10... | collective-permute-start | bytes 884744 | tf_op jit(solution)/shard_map/ppermute | solution.py:299
  19.3 1.5 %collective-permute-start.9 = (bf16[3,192,256]{2,1,0:T(8,128)(2,1)S(1)}, bf16[3,192,256]{2,1,0:T(8,128)(2,1)S(1)}, u32[]{:S(2)}, u32[]{:S(2)}) collective-permute-start(bf16[3,192,256]{2,1,0:T(8,128)(2,1)S(1)} %get-tuple-element.62.refs_0_), channel_id=1, source_target_pairs={{0,4},{2,6},{4,0},{6,2},{1,5},{3,7},{5,1},{7,3},{8,12},{10,14},{12... | collective-permute-start | bytes 884744 | tf_op jit(solution)/shard_map/ppermute | solution.py:302
  20.8 3.5 %collective-permute-done.2.refs_1_ = bf16[128,1536]{1,0:T(8,128)(2,1)S(1)} collective-permute-done((bf16[128,1536]{1,0:T(8,128)(2,1)S(1)}, bf16[128,1536]{1,0:T(8,128)(2,1)S(1)}, u32[]{:S(2)}, u32[]{:S(2)}) %collective-permute-start.2) | collective-permute-done | bytes 393248 | tf_op jit(solution)/shard_map/ppermute | solution.py:305
  24.3 3.9 %collective-permute-done.3.refs_0_ = bf16[128,1536]{1,0:T(8,128)(2,1)S(1)} collective-permute-done((bf16[128,1536]{1,0:T(8,128)(2,1)S(1)}, bf16[128,1536]{1,0:T(8,128)(2,1)S(1)}, u32[]{:S(2)}, u32[]{:S(2)}) %collective-permute-start.3) | collective-permute-done | bytes 393248 | tf_op jit(solution)/shard_map/ppermute | solution.py:299
  28.2 1.5 %collective-permute-start.4 = (bf16[128,1536]{1,0:T(8,128)(2,1)S(1)}, bf16[128,1536]{1,0:T(8,128)(2,1)S(1)}, u32[]{:S(2)}, u32[]{:S(2)}) collective-permute-start(bf16[128,1536]{1,0:T(8,128)(2,1)S(1)} %collective-permute-done.3.refs_0_), channel_id=1, source_target_pairs={{0,1},{1,0},{2,3},{3,2},{4,5},{5,4},{6,7},{7,6},{8,9},{9,8},{10,11... | collective-permute-start | bytes 1179656 | tf_op jit(solution)/shard_map/ppermute | solution.py:305
  30.8 3.0 %collective-permute-done.5.refs_2_ = bf16[3,192,256]{2,1,0:T(8,128)(2,1)S(1)} collective-permute-done((bf16[3,192,256]{2,1,0:T(8,128)(2,1)S(1)}, bf16[3,192,256]{2,1,0:T(8,128)(2,1)S(1)}, u32[]{:S(2)}, u32[]{:S(2)}) %collective-permute-start.5) | collective-permute-done | bytes 294944 | tf_op jit(solution)/shard_map/ppermute | solution.py:299
  34.9 6.4 %collective-permute-start.6 = (bf16[128,1536]{1,0:T(8,128)(2,1)S(1)}, bf16[128,1536]{1,0:T(8,128)(2,1)S(1)}, u32[]{:S(2)}, u32[]{:S(2)}) collective-permute-start(bf16[128,1536]{1,0:T(8,128)(2,1)S(1)} %collective-permute-done.3.refs_0_), channel_id=1, source_target_pairs={{0,8},{8,24},{16,0},{24,16},{1,9},{9,25},{17,1},{25,17},{2,10},{10... | collective-permute-start | bytes 1179656 | tf_op jit(solution)/shard_map/ppermute | solution.py:299
  41.3 3.2 %collective-permute-start.11 = (bf16[3,192,256]{2,1,0:T(8,128)(2,1)S(1)}, bf16[3,192,256]{2,1,0:T(8,128)(2,1)S(1)}, u32[]{:S(2)}, u32[]{:S(2)}) collective-permute-start(bf16[3,192,256]{2,1,0:T(8,128)(2,1)S(1)} %get-tuple-element.49), channel_id=1, source_target_pairs={{0,24},{8,16},{16,8},{24,0},{1,25},{9,17},{17,9},{25,1},{2,26},{10... | collective-permute-start | bytes 884744 | tf_op jit(solution)/shard_map/ppermute | solution.py:299
  44.6 2.0 %collective-permute-start.7 = (bf16[2,128,256]{2,1,0:T(8,128)(2,1)S(1)}, bf16[2,128,256]{2,1,0:T(8,128)(2,1)S(1)}, u32[]{:S(2)}, u32[]{:S(2)}) collective-permute-start(bf16[2,128,256]{2,1,0:T(8,128)(2,1)S(1)} %get-tuple-element.64.refs_0_), channel_id=1, source_target_pairs={{0,4},{2,6},{4,0},{6,2},{1,5},{3,7},{5,1},{7,3},{8,12},{10,14},{12... | collective-permute-start | bytes 393224 | tf_op jit(solution)/shard_map/ppermute | solution.py:302
  46.6 3.2 %collective-permute-start.14 = (bf16[2,128,256]{2,1,0:T(8,128)(2,1)S(1)}, bf16[2,128,256]{2,1,0:T(8,128)(2,1)S(1)}, u32[]{:S(2)}, u32[]{:S(2)}) collective-permute-start(bf16[2,128,256]{2,1,0:T(8,128)(2,1)S(1)} %get-tuple-element.53), channel_id=1, source_target_pairs={{0,8},{8,24},{16,0},{24,16},{1,9},{9,25},{17,1},{25,17},{2,10},{10... | collective-permute-start | bytes 393224 | tf_op jit(solution)/shard_map/ppermute | solution.py:299
  49.8 2.9 %collective-permute-done.7.refs_1_ = bf16[2,128,256]{2,1,0:T(8,128)(2,1)S(1)} collective-permute-done((bf16[2,128,256]{2,1,0:T(8,128)(2,1)S(1)}, bf16[2,128,256]{2,1,0:T(8,128)(2,1)S(1)}, u32[]{:S(2)}, u32[]{:S(2)}) %collective-permute-start.7) | collective-permute-done | bytes 131104 | tf_op jit(solution)/shard_map/ppermute | solution.py:302
  52.7 1.4 %collective-permute-start.8 = (bf16[128,1536]{1,0:T(8,128)(2,1)S(1)}, bf16[128,1536]{1,0:T(8,128)(2,1)S(1)}, u32[]{:S(2)}, u32[]{:S(2)}) collective-permute-start(bf16[128,1536]{1,0:T(8,128)(2,1)S(1)} %collective-permute-done.6.refs_0_), channel_id=1, source_target_pairs={{0,1},{1,0},{2,3},{3,2},{4,5},{5,4},{6,7},{7,6},{8,9},{9,8},{10,11... | collective-permute-start | bytes 1179656 | tf_op jit(solution)/shard_map/ppermute | solution.py:305
  54.1 1.3 %collective-permute-done.11.refs_0_ = bf16[3,192,256]{2,1,0:T(8,128)(2,1)S(1)} collective-permute-done((bf16[3,192,256]{2,1,0:T(8,128)(2,1)S(1)}, bf16[3,192,256]{2,1,0:T(8,128)(2,1)S(1)}, u32[]{:S(2)}, u32[]{:S(2)}) %collective-permute-start.11) | collective-permute-done | bytes 294944 | tf_op jit(solution)/shard_map/ppermute | solution.py:299
  55.4 7.0 %collective-permute-done.14.refs_2_ = bf16[2,128,256]{2,1,0:T(8,128)(2,1)S(1)} collective-permute-done((bf16[2,128,256]{2,1,0:T(8,128)(2,1)S(1)}, bf16[2,128,256]{2,1,0:T(8,128)(2,1)S(1)}, u32[]{:S(2)}, u32[]{:S(2)}) %collective-permute-start.14) | collective-permute-done | bytes 131104 | tf_op jit(solution)/shard_map/ppermute | solution.py:299
  62.4 1.3 %collective-permute-start.15 = (bf16[3,192,256]{2,1,0:T(8,128)(2,1)S(1)}, bf16[3,192,256]{2,1,0:T(8,128)(2,1)S(1)}, u32[]{:S(2)}, u32[]{:S(2)}) collective-permute-start(bf16[3,192,256]{2,1,0:T(8,128)(2,1)S(1)} %collective-permute-done.11.refs_0_), channel_id=1, source_target_pairs={{0,4},{2,6},{4,0},{6,2},{1,5},{3,7},{5,1},{7,3},{8,12},{10,14},{12... | collective-permute-start | bytes 884744 | tf_op jit(solution)/shard_map/ppermute | solution.py:302
  64.8 5.5 %collective-permute-start.17 = (bf16[2,128,256]{2,1,0:T(8,128)(2,1)S(1)}, bf16[2,128,256]{2,1,0:T(8,128)(2,1)S(1)}, u32[]{:S(2)}, u32[]{:S(2)}) collective-permute-start(bf16[2,128,256]{2,1,0:T(8,128)(2,1)S(1)} %get-tuple-element.58), channel_id=1, source_target_pairs={{0,24},{8,16},{16,8},{24,0},{1,25},{9,17},{17,9},{25,1},{2,26},{10... | collective-permute-start | bytes 393224 | tf_op jit(solution)/shard_map/ppermute | solution.py:299
  70.3 2.0 %collective-permute-start.19 = (bf16[2,128,256]{2,1,0:T(8,128)(2,1)S(1)}, bf16[2,128,256]{2,1,0:T(8,128)(2,1)S(1)}, u32[]{:S(2)}, u32[]{:S(2)}) collective-permute-start(bf16[2,128,256]{2,1,0:T(8,128)(2,1)S(1)} %collective-permute-done.16.refs_3_), channel_id=1, source_target_pairs={{0,4},{2,6},{4,0},{6,2},{1,5},{3,7},{5,1},{7,3},{8,12},{10,14},{12... | collective-permute-start | bytes 393224 | tf_op jit(solution)/shard_map/ppermute | solution.py:302
  72.3 2.3 %collective-permute-done.17.refs_0_ = bf16[2,128,256]{2,1,0:T(8,128)(2,1)S(1)} collective-permute-done((bf16[2,128,256]{2,1,0:T(8,128)(2,1)S(1)}, bf16[2,128,256]{2,1,0:T(8,128)(2,1)S(1)}, u32[]{:S(2)}, u32[]{:S(2)}) %collective-permute-start.17) | collective-permute-done | bytes 131104 | tf_op jit(solution)/shard_map/ppermute | solution.py:299
  75.3 1.4 %collective-permute-done.19.refs_5_ = bf16[2,128,256]{2,1,0:T(8,128)(2,1)S(1)} collective-permute-done((bf16[2,128,256]{2,1,0:T(8,128)(2,1)S(1)}, bf16[2,128,256]{2,1,0:T(8,128)(2,1)S(1)}, u32[]{:S(2)}, u32[]{:S(2)}) %collective-permute-start.19) | collective-permute-done | bytes 131104 | tf_op jit(solution)/shard_map/ppermute | solution.py:302
  76.7 3.0 %collective-permute-done.20.refs_1_ = bf16[2,128,256]{2,1,0:T(8,128)(2,1)S(1)} collective-permute-done((bf16[2,128,256]{2,1,0:T(8,128)(2,1)S(1)}, bf16[2,128,256]{2,1,0:T(8,128)(2,1)S(1)}, u32[]{:S(2)}, u32[]{:S(2)}) %collective-permute-start.20) | collective-permute-done | bytes 131104 | tf_op jit(solution)/shard_map/ppermute | solution.py:302
  87.4 3.0 %shard_map.125.qkv = bf16[3,512,256]{2,1,0:T(8,128)(2,1)S(1)} custom-call(f32[1,128]{1,0:T(1,128)S(1)} %bitcast.48, f32[1,128]{1,0:T(1,128)S(1)} %bitcast.49, bf16[128,3072]{1,0:T(8,128)(2,1)S(1)} %shard_map.118.refs_0_, bf16[128,3072]{1,0:T(8,128)(2,1)S(1)} %shard_map.120.refs_1_, bf16[128,3072]{1,0:T(8,128)(2,1)S(1)} %shard_map.121.refs_2_, ...), custom_call_target="tpu_custom_call" | custom-call | tf_op jit(solution)/shard_map/pallas_call | solution.py:145
  90.5 5.0 %shard_map.128 = (bf16[128,256]{1,0:T(8,128)(2,1)S(1)}, bf16[128,256]{1,0:T(8,128)(2,1)S(1)}, bf16[128,256]{1,0:T(8,128)(2,1)S(1)}, bf16[128,256]{1,0:T(8,128)(2,1)S(1)}) custom-call(bf16[3,512,256]{2,1,0:T(8,128)(2,1)S(1)} %shard_map.125.qkv, bf16[512,1024]{1,0:T(8,128)(2,1)S(1)} %copy-done.1, bf16[512,1024]{1,0:T(8,128)(2,1)S(1)} %copy-done.2, ...), custom_call_target="tpu_custom_call" | custom-call | tf_op jit(solution)/shard_map/pallas_call | solution.py:233
  95.4 2.6 %collective-permute-start.25 = (bf16[128,256]{1,0:T(8,128)(2,1)S(1)}, bf16[128,256]{1,0:T(8,128)(2,1)S(1)}, u32[]{:S(2)}, u32[]{:S(2)}) collective-permute-start(bf16[128,256]{1,0:T(8,128)(2,1)S(1)} %get-tuple-element.66), channel_id=1, source_target_pairs={{0,16},{8,0},{16,24},{24,8},{1,17},{9,1},{17,25},{25,9},{2,18},{10... | collective-permute-start | bytes 196616 | tf_op jit(solution)/shard_map/ppermute | solution.py:299
  98.0 1.7 %collective-permute-start.26 = (bf16[128,256]{1,0:T(8,128)(2,1)S(1)}, bf16[128,256]{1,0:T(8,128)(2,1)S(1)}, u32[]{:S(2)}, u32[]{:S(2)}) collective-permute-start(bf16[128,256]{1,0:T(8,128)(2,1)S(1)} %get-tuple-element.67), channel_id=1, source_target_pairs={{0,24},{8,16},{16,8},{24,0},{1,25},{9,17},{17,9},{25,1},{2,26},{10... | collective-permute-start | bytes 196616 | tf_op jit(solution)/shard_map/ppermute | solution.py:299
  100.0 4.4 %collective-permute-done.26.refs_2_ = bf16[128,256]{1,0:T(8,128)(2,1)S(1)} collective-permute-done((bf16[128,256]{1,0:T(8,128)(2,1)S(1)}, bf16[128,256]{1,0:T(8,128)(2,1)S(1)}, u32[]{:S(2)}, u32[]{:S(2)}) %collective-permute-start.26) | collective-permute-done | bytes 65568 | tf_op jit(solution)/shard_map/ppermute | solution.py:299
  106.0 1.5 %collective-permute-start.28 = (bf16[128,1536]{1,0:T(8,128)(2,1)S(1)}, bf16[128,1536]{1,0:T(8,128)(2,1)S(1)}, u32[]{:S(2)}, u32[]{:S(2)}) collective-permute-start(bf16[128,1536]{1,0:T(8,128)(2,1)S(1)} %shard_map.130), channel_id=1, source_target_pairs={{0,1},{1,0},{2,3},{3,2},{4,5},{5,4},{6,7},{7,6},{8,9},{9,8},{10,11... | collective-permute-start | bytes 1179656 | tf_op jit(solution)/shard_map/ppermute | solution.py:305
  108.1 8.6 %collective-permute-done.28 = bf16[128,1536]{1,0:T(8,128)(2,1)S(1)} collective-permute-done((bf16[128,1536]{1,0:T(8,128)(2,1)S(1)}, bf16[128,1536]{1,0:T(8,128)(2,1)S(1)}, u32[]{:S(2)}, u32[]{:S(2)}) %collective-permute-start.28) | collective-permute-done | bytes 393248 | tf_op jit(solution)/shard_map/ppermute | solution.py:305
  (67 shorter events, 18.6 us)
Async XLA Ops:
  0.0 12.3 %collective-permute-start = (bf16[128,1536]{1,0:T(8,128)(2,1)}, bf16[128,1536]{1,0:T(8,128)(2,1)S(1)}, u32[]{:S(2)}, u32[]{:S(2)}) collective-permute-start(bf16[128,1536]{1,0:T(8,128)(2,1)} %refs_0_.1), channel_id=1, source_target_pairs={{0,1},{1,0},{2,3},{3,2},{4,5},{5,4},{6,7},{7,6},{8,9},{9,8},{10,11... | collective-permute-start | bytes 1179656 | tf_op jit(solution)/shard_map/ppermute | solution.py:305
  2.9 11.7 %collective-permute-start.1 = (bf16[128,1536]{1,0:T(8,128)(2,1)}, bf16[128,1536]{1,0:T(8,128)(2,1)S(1)}, u32[]{:S(2)}, u32[]{:S(2)}) collective-permute-start(bf16[128,1536]{1,0:T(8,128)(2,1)} %refs_0_.1), channel_id=1, source_target_pairs={{0,8},{8,24},{16,0},{24,16},{1,9},{9,25},{17,1},{25,17},{2,10},{10... | collective-permute-start | bytes 1179656 | tf_op jit(solution)/shard_map/ppermute | solution.py:299
  14.6 9.7 %collective-permute-start.2 = (bf16[128,1536]{1,0:T(8,128)(2,1)S(1)}, bf16[128,1536]{1,0:T(8,128)(2,1)S(1)}, u32[]{:S(2)}, u32[]{:S(2)}) collective-permute-start(bf16[128,1536]{1,0:T(8,128)(2,1)S(1)} %collective-permute-done.1.refs_0_), channel_id=1, source_target_pairs={{0,1},{1,0},{2,3},{3,2},{4,5},{5,4},{6,7},{7,6},{8,9},{9,8},{10,11... | collective-permute-start | bytes 1179656 | tf_op jit(solution)/shard_map/ppermute | solution.py:305
  15.1 13.0 %collective-permute-start.3 = (bf16[128,1536]{1,0:T(8,128)(2,1)S(1)}, bf16[128,1536]{1,0:T(8,128)(2,1)S(1)}, u32[]{:S(2)}, u32[]{:S(2)}) collective-permute-start(bf16[128,1536]{1,0:T(8,128)(2,1)S(1)} %collective-permute-done.1.refs_0_), channel_id=1, source_target_pairs={{0,8},{8,24},{16,0},{24,16},{1,9},{9,25},{17,1},{25,17},{2,10},{10... | collective-permute-start | bytes 1179656 | tf_op jit(solution)/shard_map/ppermute | solution.py:299
  16.1 17.8 %collective-permute-start.5 = (bf16[3,192,256]{2,1,0:T(8,128)(2,1)S(1)}, bf16[3,192,256]{2,1,0:T(8,128)(2,1)S(1)}, u32[]{:S(2)}, u32[]{:S(2)}) collective-permute-start(bf16[3,192,256]{2,1,0:T(8,128)(2,1)S(1)} %get-tuple-element.41), channel_id=1, source_target_pairs={{0,8},{8,24},{16,0},{24,16},{1,9},{9,25},{17,1},{25,17},{2,10},{10... | collective-permute-start | bytes 884744 | tf_op jit(solution)/shard_map/ppermute | solution.py:299
  19.3 14.5 %collective-permute-start.9 = (bf16[3,192,256]{2,1,0:T(8,128)(2,1)S(1)}, bf16[3,192,256]{2,1,0:T(8,128)(2,1)S(1)}, u32[]{:S(2)}, u32[]{:S(2)}) collective-permute-start(bf16[3,192,256]{2,1,0:T(8,128)(2,1)S(1)} %get-tuple-element.62.refs_0_), channel_id=1, source_target_pairs={{0,4},{2,6},{4,0},{6,2},{1,5},{3,7},{5,1},{7,3},{8,12},{10,14},{12... | collective-permute-start | bytes 884744 | tf_op jit(solution)/shard_map/ppermute | solution.py:302
  28.2 16.3 %collective-permute-start.4 = (bf16[128,1536]{1,0:T(8,128)(2,1)S(1)}, bf16[128,1536]{1,0:T(8,128)(2,1)S(1)}, u32[]{:S(2)}, u32[]{:S(2)}) collective-permute-start(bf16[128,1536]{1,0:T(8,128)(2,1)S(1)} %collective-permute-done.3.refs_0_), channel_id=1, source_target_pairs={{0,1},{1,0},{2,3},{3,2},{4,5},{5,4},{6,7},{7,6},{8,9},{9,8},{10,11... | collective-permute-start | bytes 1179656 | tf_op jit(solution)/shard_map/ppermute | solution.py:305
  29.7 14.8 %collective-permute-start.10 = (bf16[3,192,256]{2,1,0:T(8,128)(2,1)S(1)}, bf16[3,192,256]{2,1,0:T(8,128)(2,1)S(1)}, u32[]{:S(2)}, u32[]{:S(2)}) collective-permute-start(bf16[3,192,256]{2,1,0:T(8,128)(2,1)S(1)} %get-tuple-element.47), channel_id=1, source_target_pairs={{0,16},{8,0},{16,24},{24,8},{1,17},{9,1},{17,25},{25,9},{2,18},{10... | collective-permute-start | bytes 884744 | tf_op jit(solution)/shard_map/ppermute | solution.py:299
  33.9 10.6 %collective-permute-start.12 = (bf16[3,192,256]{2,1,0:T(8,128)(2,1)S(1)}, bf16[3,192,256]{2,1,0:T(8,128)(2,1)S(1)}, u32[]{:S(2)}, u32[]{:S(2)}) collective-permute-start(bf16[3,192,256]{2,1,0:T(8,128)(2,1)S(1)} %collective-permute-done.5.refs_2_), channel_id=1, source_target_pairs={{0,4},{2,6},{4,0},{6,2},{1,5},{3,7},{5,1},{7,3},{8,12},{10,14},{12... | collective-permute-start | bytes 884744 | tf_op jit(solution)/shard_map/ppermute | solution.py:302
  34.9 17.8 %collective-permute-start.6 = (bf16[128,1536]{1,0:T(8,128)(2,1)S(1)}, bf16[128,1536]{1,0:T(8,128)(2,1)S(1)}, u32[]{:S(2)}, u32[]{:S(2)}) collective-permute-start(bf16[128,1536]{1,0:T(8,128)(2,1)S(1)} %collective-permute-done.3.refs_0_), channel_id=1, source_target_pairs={{0,8},{8,24},{16,0},{24,16},{1,9},{9,25},{17,1},{25,17},{2,10},{10... | collective-permute-start | bytes 1179656 | tf_op jit(solution)/shard_map/ppermute | solution.py:299
  41.3 14.1 %collective-permute-start.11 = (bf16[3,192,256]{2,1,0:T(8,128)(2,1)S(1)}, bf16[3,192,256]{2,1,0:T(8,128)(2,1)S(1)}, u32[]{:S(2)}, u32[]{:S(2)}) collective-permute-start(bf16[3,192,256]{2,1,0:T(8,128)(2,1)S(1)} %get-tuple-element.49), channel_id=1, source_target_pairs={{0,24},{8,16},{16,8},{24,0},{1,25},{9,17},{17,9},{25,1},{2,26},{10... | collective-permute-start | bytes 884744 | tf_op jit(solution)/shard_map/ppermute | solution.py:299
  44.5 17.9 %collective-permute-start.13 = (bf16[3,192,256]{2,1,0:T(8,128)(2,1)S(1)}, bf16[3,192,256]{2,1,0:T(8,128)(2,1)S(1)}, u32[]{:S(2)}, u32[]{:S(2)}) collective-permute-start(bf16[3,192,256]{2,1,0:T(8,128)(2,1)S(1)} %collective-permute-done.10.refs_3_), channel_id=1, source_target_pairs={{0,4},{2,6},{4,0},{6,2},{1,5},{3,7},{5,1},{7,3},{8,12},{10,14},{12... | collective-permute-start | bytes 884744 | tf_op jit(solution)/shard_map/ppermute | solution.py:302
  44.6 8.1 %collective-permute-start.7 = (bf16[2,128,256]{2,1,0:T(8,128)(2,1)S(1)}, bf16[2,128,256]{2,1,0:T(8,128)(2,1)S(1)}, u32[]{:S(2)}, u32[]{:S(2)}) collective-permute-start(bf16[2,128,256]{2,1,0:T(8,128)(2,1)S(1)} %get-tuple-element.64.refs_0_), channel_id=1, source_target_pairs={{0,4},{2,6},{4,0},{6,2},{1,5},{3,7},{5,1},{7,3},{8,12},{10,14},{12... | collective-permute-start | bytes 393224 | tf_op jit(solution)/shard_map/ppermute | solution.py:302
  46.6 15.8 %collective-permute-start.14 = (bf16[2,128,256]{2,1,0:T(8,128)(2,1)S(1)}, bf16[2,128,256]{2,1,0:T(8,128)(2,1)S(1)}, u32[]{:S(2)}, u32[]{:S(2)}) collective-permute-start(bf16[2,128,256]{2,1,0:T(8,128)(2,1)S(1)} %get-tuple-element.53), channel_id=1, source_target_pairs={{0,8},{8,24},{16,0},{24,16},{1,9},{9,25},{17,1},{25,17},{2,10},{10... | collective-permute-start | bytes 393224 | tf_op jit(solution)/shard_map/ppermute | solution.py:299
  52.7 22.0 %collective-permute-start.8 = (bf16[128,1536]{1,0:T(8,128)(2,1)S(1)}, bf16[128,1536]{1,0:T(8,128)(2,1)S(1)}, u32[]{:S(2)}, u32[]{:S(2)}) collective-permute-start(bf16[128,1536]{1,0:T(8,128)(2,1)S(1)} %collective-permute-done.6.refs_0_), channel_id=1, source_target_pairs={{0,1},{1,0},{2,3},{3,2},{4,5},{5,4},{6,7},{7,6},{8,9},{9,8},{10,11... | collective-permute-start | bytes 1179656 | tf_op jit(solution)/shard_map/ppermute | solution.py:305
  62.4 17.3 %collective-permute-start.15 = (bf16[3,192,256]{2,1,0:T(8,128)(2,1)S(1)}, bf16[3,192,256]{2,1,0:T(8,128)(2,1)S(1)}, u32[]{:S(2)}, u32[]{:S(2)}) collective-permute-start(bf16[3,192,256]{2,1,0:T(8,128)(2,1)S(1)} %collective-permute-done.11.refs_0_), channel_id=1, source_target_pairs={{0,4},{2,6},{4,0},{6,2},{1,5},{3,7},{5,1},{7,3},{8,12},{10,14},{12... | collective-permute-start | bytes 884744 | tf_op jit(solution)/shard_map/ppermute | solution.py:302
  63.7 6.7 %collective-permute-start.16 = (bf16[2,128,256]{2,1,0:T(8,128)(2,1)S(1)}, bf16[2,128,256]{2,1,0:T(8,128)(2,1)S(1)}, u32[]{:S(2)}, u32[]{:S(2)}) collective-permute-start(bf16[2,128,256]{2,1,0:T(8,128)(2,1)S(1)} %get-tuple-element.56), channel_id=1, source_target_pairs={{0,16},{8,0},{16,24},{24,8},{1,17},{9,1},{17,25},{25,9},{2,18},{10... | collective-permute-start | bytes 393224 | tf_op jit(solution)/shard_map/ppermute | solution.py:299
  64.8 16.9 %copy-start.7 = (f32[3072]{0:T(1024)S(1)}, f32[3072]{0:T(1024)}, u32[]{:S(2)}) copy-start(f32[3072]{0:T(1024)} %param.13) | copy-start | bytes 36868
  64.8 9.8 %collective-permute-start.17 = (bf16[2,128,256]{2,1,0:T(8,128)(2,1)S(1)}, bf16[2,128,256]{2,1,0:T(8,128)(2,1)S(1)}, u32[]{:S(2)}, u32[]{:S(2)}) collective-permute-start(bf16[2,128,256]{2,1,0:T(8,128)(2,1)S(1)} %get-tuple-element.58), channel_id=1, source_target_pairs={{0,24},{8,16},{16,8},{24,0},{1,25},{9,17},{17,9},{25,1},{2,26},{10... | collective-permute-start | bytes 393224 | tf_op jit(solution)/shard_map/ppermute | solution.py:299
  70.3 5.0 %collective-permute-start.18 = (bf16[2,128,256]{2,1,0:T(8,128)(2,1)S(1)}, bf16[2,128,256]{2,1,0:T(8,128)(2,1)S(1)}, u32[]{:S(2)}, u32[]{:S(2)}) collective-permute-start(bf16[2,128,256]{2,1,0:T(8,128)(2,1)S(1)} %collective-permute-done.14.refs_2_), channel_id=1, source_target_pairs={{0,4},{2,6},{4,0},{6,2},{1,5},{3,7},{5,1},{7,3},{8,12},{10,14},{12... | collective-permute-start | bytes 393224 | tf_op jit(solution)/shard_map/ppermute | solution.py:302
  70.3 6.3 %collective-permute-start.19 = (bf16[2,128,256]{2,1,0:T(8,128)(2,1)S(1)}, bf16[2,128,256]{2,1,0:T(8,128)(2,1)S(1)}, u32[]{:S(2)}, u32[]{:S(2)}) collective-permute-start(bf16[2,128,256]{2,1,0:T(8,128)(2,1)S(1)} %collective-permute-done.16.refs_3_), channel_id=1, source_target_pairs={{0,4},{2,6},{4,0},{6,2},{1,5},{3,7},{5,1},{7,3},{8,12},{10,14},{12... | collective-permute-start | bytes 393224 | tf_op jit(solution)/shard_map/ppermute | solution.py:302
  74.7 5.0 %collective-permute-start.20 = (bf16[2,128,256]{2,1,0:T(8,128)(2,1)S(1)}, bf16[2,128,256]{2,1,0:T(8,128)(2,1)S(1)}, u32[]{:S(2)}, u32[]{:S(2)}) collective-permute-start(bf16[2,128,256]{2,1,0:T(8,128)(2,1)S(1)} %collective-permute-done.17.refs_0_), channel_id=1, source_target_pairs={{0,4},{2,6},{4,0},{6,2},{1,5},{3,7},{5,1},{7,3},{8,12},{10,14},{12... | collective-permute-start | bytes 393224 | tf_op jit(solution)/shard_map/ppermute | solution.py:302
  80.1 7.3 %collective-permute-start.21 = (bf16[6,3,192,256]{3,2,1,0:T(8,128)(2,1)S(1)}, bf16[6,3,192,256]{3,2,1,0:T(8,128)(2,1)S(1)}, u32[]{:S(2)}, u32[]{:S(2)}) collective-permute-start(bf16[6,3,192,256]{3,2,1,0:T(8,128)(2,1)S(1)} %shard_map.123), channel_id=1, source_target_pairs={{0,2},{2,0},{4,6},{6,4},{1,3},{3,1},{5,7},{7,5},{8,10},{10,8},{12,... | collective-permute-start | bytes 5308424 | tf_op jit(solution)/shard_map/ppermute | solution.py:302
  81.2 9.2 %collective-permute-start.23 = (bf16[6,2,128,256]{3,2,1,0:T(8,128)(2,1)S(1)}, bf16[6,2,128,256]{3,2,1,0:T(8,128)(2,1)S(1)}, u32[]{:S(2)}, u32[]{:S(2)}) collective-permute-start(bf16[6,2,128,256]{3,2,1,0:T(8,128)(2,1)S(1)} %shard_map.126), channel_id=1, source_target_pairs={{0,2},{2,0},{4,6},{6,4},{1,3},{3,1},{5,7},{7,5},{8,10},{10,8},{12,... | collective-permute-start | bytes 2359304 | tf_op jit(solution)/shard_map/ppermute | solution.py:302
  85.3 2.1 %collective-permute-start.22 = (bf16[2,3,192,256]{3,2,1,0:T(8,128)(2,1)S(1)}, bf16[2,3,192,256]{3,2,1,0:T(8,128)(2,1)S(1)}, u32[]{:S(2)}, u32[]{:S(2)}) collective-permute-start(bf16[2,3,192,256]{3,2,1,0:T(8,128)(2,1)S(1)} %shard_map.124), channel_id=1, source_target_pairs={{0,2},{2,0},{4,6},{6,4},{1,3},{3,1},{5,7},{7,5},{8,10},{10,8},{12,... | collective-permute-start | bytes 1769480 | tf_op jit(solution)/shard_map/ppermute | solution.py:302
  85.4 20.0 %slice-start = ((s8[6291456]{0:T(1024)(128)(4,1)}), s8[4194304]{0:T(1024)(128)(4,1)S(1)}, s32[]{:S(2)}) async-start(s8[6291456]{0:T(1024)(128)(4,1)} %bitcast.21), calls=%async_computation | async-start | bytes 8388608
  85.7 4.7 %collective-permute-start.24 = (bf16[2,2,128,256]{3,2,1,0:T(8,128)(2,1)S(1)}, bf16[2,2,128,256]{3,2,1,0:T(8,128)(2,1)S(1)}, u32[]{:S(2)}, u32[]{:S(2)}) collective-permute-start(bf16[2,2,128,256]{3,2,1,0:T(8,128)(2,1)S(1)} %shard_map.127), channel_id=1, source_target_pairs={{0,2},{2,0},{4,6},{6,4},{1,3},{3,1},{5,7},{7,5},{8,10},{10,8},{12,... | collective-permute-start | bytes 786440 | tf_op jit(solution)/shard_map/ppermute | solution.py:302
  87.4 18.0 %slice-start.1 = ((s8[6291456]{0:T(1024)(128)(4,1)}), s8[2097152]{0:T(1024)(128)(4,1)S(1)}, s32[]{:S(2)}) async-start(s8[6291456]{0:T(1024)(128)(4,1)} %bitcast.21), calls=%async_computation.1 | async-start | bytes 4194304
  95.4 4.5 %collective-permute-start.25 = (bf16[128,256]{1,0:T(8,128)(2,1)S(1)}, bf16[128,256]{1,0:T(8,128)(2,1)S(1)}, u32[]{:S(2)}, u32[]{:S(2)}) collective-permute-start(bf16[128,256]{1,0:T(8,128)(2,1)S(1)} %get-tuple-element.66), channel_id=1, source_target_pairs={{0,16},{8,0},{16,24},{24,8},{1,17},{9,1},{17,25},{25,9},{2,18},{10... | collective-permute-start | bytes 196616 | tf_op jit(solution)/shard_map/ppermute | solution.py:299
  98.0 6.3 %collective-permute-start.26 = (bf16[128,256]{1,0:T(8,128)(2,1)S(1)}, bf16[128,256]{1,0:T(8,128)(2,1)S(1)}, u32[]{:S(2)}, u32[]{:S(2)}) collective-permute-start(bf16[128,256]{1,0:T(8,128)(2,1)S(1)} %get-tuple-element.67), channel_id=1, source_target_pairs={{0,24},{8,16},{16,8},{24,0},{1,25},{9,17},{17,9},{25,1},{2,26},{10... | collective-permute-start | bytes 196616 | tf_op jit(solution)/shard_map/ppermute | solution.py:299
  99.8 5.6 %collective-permute-start.27 = (bf16[128,256]{1,0:T(8,128)(2,1)S(1)}, bf16[128,256]{1,0:T(8,128)(2,1)S(1)}, u32[]{:S(2)}, u32[]{:S(2)}) collective-permute-start(bf16[128,256]{1,0:T(8,128)(2,1)S(1)} %get-tuple-element.68), channel_id=1, source_target_pairs={{0,8},{8,24},{16,0},{24,16},{1,9},{9,25},{17,1},{25,17},{2,10},{10... | collective-permute-start | bytes 196616 | tf_op jit(solution)/shard_map/ppermute | solution.py:299
  106.0 10.7 %collective-permute-start.28 = (bf16[128,1536]{1,0:T(8,128)(2,1)S(1)}, bf16[128,1536]{1,0:T(8,128)(2,1)S(1)}, u32[]{:S(2)}, u32[]{:S(2)}) collective-permute-start(bf16[128,1536]{1,0:T(8,128)(2,1)S(1)} %shard_map.130), channel_id=1, source_target_pairs={{0,1},{1,0},{2,3},{3,2},{4,5},{5,4},{6,7},{7,6},{8,9},{9,8},{10,11... | collective-permute-start | bytes 1179656 | tf_op jit(solution)/shard_map/ppermute | solution.py:305
  (10 other events, 60.1 us)

commit v4 on v3

--- a/solution.py
+++ b/solution.py
@@ -352,7 +352,7 @@
         ready += [*hops[:1], *crossed[:1]] if index else []
         found[step, 0] = turn(after(packed[step], *ready), step)
         if index == len(order) - 1:
-            ahead = [spread(cached, 0, *hops[1:2])]
+            ahead = [spread(cached, 0, *hops[1:2], *mods[:2])]
         cross(hops[-1], *crossed[-1:], *packed[:1], *ahead)
     for index, step in enumerate(order):
         ready = hops[1:2] if index == 0 else []
@@ -372,7 +372,9 @@
     qkv = project(mods, arrays, stacks, groups, rest, query_gain, key_gain)
     arrays, stacks = finish(cached, last_step, [cached[last_step, 0]], [])
     attention = attend(qkv, text_keys, text_values, arrays, stacks, groups, size)
-    pieces = [attention[0]] + [turn(attention[step], -step) for step in range(1, groups)]
+    pieces = [attention[0]] * groups
+    for step in sorted(range(1, groups), key=lambda step: -min(step, groups - step)):
+        pieces[step] = turn(attention[step], -step)
     terms = []
     for hop in range(1, n_head):
         term = combine(pieces, hop, n_head, out_weight, share, jnp.bfloat16)

time: 118 us -> 116 us (0.983)
  waiting for transfers between devices: 50.7 us -> 47 us
  local copies, waits for them, and re-layouts: 3.22 us -> 4.63 us
    ppermute x12, waiting for transfers between devices: 8.93 us -> 6.2 us  [swap(): return lax.ppermute(array, 'rest', [(i, i ^ bit) for i in range(rest)])]
    unnamed x26, local copies, waits for them, and re-layouts: 3.22 us -> 4.63 us
  transfers between devices with their start and end apart: 29 -> 29, of which waited for: 17 -> 16; matrix products, arithmetic and copies ran while one was open for 0% -> 0% of each run, Pallas kernels for 8% -> 8%
where the time goes in v4:
time: 116 us
  starting transfers between devices  48.5 us (42%)
  waiting for transfers between devices  47 us (41%)
  Pallas kernels  14.9 us (13%)
  local copies, waits for them, and re-layouts  4.63 us (4%)
    ppermute x12, starting transfers between devices, turn(): return lax.ppermute(array, 'group', pairs)  30.6 us
    ppermute x12, waiting for transfers between devices, turn(): return lax.ppermute(array, 'group', pairs)  24.6 us
    ppermute x5, waiting for transfers between devices, across(): lax.ppermute(array, 'head', [(i, (i + hop) % n_head) for i in range(n_hea...  16.3 us
    ppermute x12, starting transfers between devices, swap(): return lax.ppermute(array, 'rest', [(i, i ^ bit) for i in range(rest)])  9.23 us
    ppermute x5, starting transfers between devices, across(): lax.ppermute(array, 'head', [(i, (i + hop) % n_head) for i in range(n_hea...  8.66 us
    ppermute x12, waiting for transfers between devices, swap(): return lax.ppermute(array, 'rest', [(i, i ^ bit) for i in range(rest)])  6.2 us
    pallas_call x1, Pallas kernels, attend(): pl.pallas_call(functools.partial(attend_kernel, groups, size, stacks), ou...  4.98 us
    unnamed x26, local copies, waits for them, and re-layouts  4.63 us
  transfers between devices with their start and end apart: 29, of which 16 were waited for; matrix products, arithmetic and copies ran while one was open for 0% of the time, Pallas kernels for 8%

profile of v4, /device:TPU:0, one launch (start us, length us, event | category | flops | bytes accessed | tf_op | source)
XLA Modules:
  0.0 116.0 jit_solution(3646928382070241984)
XLA Ops:
  0.0 2.9 %collective-permute-start = (bf16[128,1536]{1,0:T(8,128)(2,1)}, bf16[128,1536]{1,0:T(8,128)(2,1)S(1)}, u32[]{:S(2)}, u32[]{:S(2)}) collective-permute-start(bf16[128,1536]{1,0:T(8,128)(2,1)} %refs_0_.1), channel_id=1, source_target_pairs={{0,1},{1,0},{2,3},{3,2},{4,5},{5,4},{6,7},{7,6},{8,9},{9,8},{10,11... | collective-permute-start | bytes 1179656 | tf_op jit(solution)/shard_map/ppermute | solution.py:305
  2.9 1.6 %collective-permute-start.1 = (bf16[128,1536]{1,0:T(8,128)(2,1)}, bf16[128,1536]{1,0:T(8,128)(2,1)S(1)}, u32[]{:S(2)}, u32[]{:S(2)}) collective-permute-start(bf16[128,1536]{1,0:T(8,128)(2,1)} %refs_0_.1), channel_id=1, source_target_pairs={{0,8},{8,24},{16,0},{24,16},{1,9},{9,25},{17,1},{25,17},{2,10},{10... | collective-permute-start | bytes 1179656 | tf_op jit(solution)/shard_map/ppermute | solution.py:299
  4.5 1.3 %copy-done = bf16[192,3,1024]{2,0,1:T(8,128)(2,1)S(1)} copy-done((bf16[192,3,1024]{2,0,1:T(8,128)(2,1)S(1)}, bf16[192,3,1024]{2,0,1:T(8,128)(2,1)}, u32[]{:S(2)}) %copy-start) | copy-done | bytes 1179672
  8.1 4.2 %collective-permute-done.refs_1_ = bf16[128,1536]{1,0:T(8,128)(2,1)S(1)} collective-permute-done((bf16[128,1536]{1,0:T(8,128)(2,1)}, bf16[128,1536]{1,0:T(8,128)(2,1)S(1)}, u32[]{:S(2)}, u32[]{:S(2)}) %collective-permute-start) | collective-permute-done | bytes 393248 | tf_op jit(solution)/shard_map/ppermute | solution.py:305
  12.3 2.4 %collective-permute-done.1.refs_0_ = bf16[128,1536]{1,0:T(8,128)(2,1)S(1)} collective-permute-done((bf16[128,1536]{1,0:T(8,128)(2,1)}, bf16[128,1536]{1,0:T(8,128)(2,1)S(1)}, u32[]{:S(2)}, u32[]{:S(2)}) %collective-permute-start.1) | collective-permute-done | bytes 393248 | tf_op jit(solution)/shard_map/ppermute | solution.py:299
  16.1 3.3 %collective-permute-start.5 = (bf16[3,192,256]{2,1,0:T(8,128)(2,1)S(1)}, bf16[3,192,256]{2,1,0:T(8,128)(2,1)S(1)}, u32[]{:S(2)}, u32[]{:S(2)}) collective-permute-start(bf16[3,192,256]{2,1,0:T(8,128)(2,1)S(1)} %get-tuple-element.41), channel_id=1, source_target_pairs={{0,8},{8,24},{16,0},{24,16},{1,9},{9,25},{17,1},{25,17},{2,10},{10... | collective-permute-start | bytes 884744 | tf_op jit(solution)/shard_map/ppermute | solution.py:299
  19.3 1.5 %collective-permute-start.9 = (bf16[3,192,256]{2,1,0:T(8,128)(2,1)S(1)}, bf16[3,192,256]{2,1,0:T(8,128)(2,1)S(1)}, u32[]{:S(2)}, u32[]{:S(2)}) collective-permute-start(bf16[3,192,256]{2,1,0:T(8,128)(2,1)S(1)} %get-tuple-element.62.refs_0_), channel_id=1, source_target_pairs={{0,4},{2,6},{4,0},{6,2},{1,5},{3,7},{5,1},{7,3},{8,12},{10,14},{12... | collective-permute-start | bytes 884744 | tf_op jit(solution)/shard_map/ppermute | solution.py:302
  20.8 3.5 %collective-permute-done.2.refs_1_ = bf16[128,1536]{1,0:T(8,128)(2,1)S(1)} collective-permute-done((bf16[128,1536]{1,0:T(8,128)(2,1)S(1)}, bf16[128,1536]{1,0:T(8,128)(2,1)S(1)}, u32[]{:S(2)}, u32[]{:S(2)}) %collective-permute-start.2) | collective-permute-done | bytes 393248 | tf_op jit(solution)/shard_map/ppermute | solution.py:305
  24.3 3.9 %collective-permute-done.3.refs_0_ = bf16[128,1536]{1,0:T(8,128)(2,1)S(1)} collective-permute-done((bf16[128,1536]{1,0:T(8,128)(2,1)S(1)}, bf16[128,1536]{1,0:T(8,128)(2,1)S(1)}, u32[]{:S(2)}, u32[]{:S(2)}) %collective-permute-start.3) | collective-permute-done | bytes 393248 | tf_op jit(solution)/shard_map/ppermute | solution.py:299
  28.2 1.5 %collective-permute-start.4 = (bf16[128,1536]{1,0:T(8,128)(2,1)S(1)}, bf16[128,1536]{1,0:T(8,128)(2,1)S(1)}, u32[]{:S(2)}, u32[]{:S(2)}) collective-permute-start(bf16[128,1536]{1,0:T(8,128)(2,1)S(1)} %collective-permute-done.3.refs_0_), channel_id=1, source_target_pairs={{0,1},{1,0},{2,3},{3,2},{4,5},{5,4},{6,7},{7,6},{8,9},{9,8},{10,11... | collective-permute-start | bytes 1179656 | tf_op jit(solution)/shard_map/ppermute | solution.py:305
  30.8 3.0 %collective-permute-done.5.refs_2_ = bf16[3,192,256]{2,1,0:T(8,128)(2,1)S(1)} collective-permute-done((bf16[3,192,256]{2,1,0:T(8,128)(2,1)S(1)}, bf16[3,192,256]{2,1,0:T(8,128)(2,1)S(1)}, u32[]{:S(2)}, u32[]{:S(2)}) %collective-permute-start.5) | collective-permute-done | bytes 294944 | tf_op jit(solution)/shard_map/ppermute | solution.py:299
  34.9 6.4 %collective-permute-start.6 = (bf16[128,1536]{1,0:T(8,128)(2,1)S(1)}, bf16[128,1536]{1,0:T(8,128)(2,1)S(1)}, u32[]{:S(2)}, u32[]{:S(2)}) collective-permute-start(bf16[128,1536]{1,0:T(8,128)(2,1)S(1)} %collective-permute-done.3.refs_0_), channel_id=1, source_target_pairs={{0,8},{8,24},{16,0},{24,16},{1,9},{9,25},{17,1},{25,17},{2,10},{10... | collective-permute-start | bytes 1179656 | tf_op jit(solution)/shard_map/ppermute | solution.py:299
  41.3 3.2 %collective-permute-start.11 = (bf16[3,192,256]{2,1,0:T(8,128)(2,1)S(1)}, bf16[3,192,256]{2,1,0:T(8,128)(2,1)S(1)}, u32[]{:S(2)}, u32[]{:S(2)}) collective-permute-start(bf16[3,192,256]{2,1,0:T(8,128)(2,1)S(1)} %get-tuple-element.49), channel_id=1, source_target_pairs={{0,24},{8,16},{16,8},{24,0},{1,25},{9,17},{17,9},{25,1},{2,26},{10... | collective-permute-start | bytes 884744 | tf_op jit(solution)/shard_map/ppermute | solution.py:299
  47.7 2.0 %collective-permute-start.7 = (bf16[2,128,256]{2,1,0:T(8,128)(2,1)S(1)}, bf16[2,128,256]{2,1,0:T(8,128)(2,1)S(1)}, u32[]{:S(2)}, u32[]{:S(2)}) collective-permute-start(bf16[2,128,256]{2,1,0:T(8,128)(2,1)S(1)} %get-tuple-element.64.refs_0_), channel_id=1, source_target_pairs={{0,4},{2,6},{4,0},{6,2},{1,5},{3,7},{5,1},{7,3},{8,12},{10,14},{12... | collective-permute-start | bytes 393224 | tf_op jit(solution)/shard_map/ppermute | solution.py:302
  49.7 3.2 %collective-permute-start.14 = (bf16[2,128,256]{2,1,0:T(8,128)(2,1)S(1)}, bf16[2,128,256]{2,1,0:T(8,128)(2,1)S(1)}, u32[]{:S(2)}, u32[]{:S(2)}) collective-permute-start(bf16[2,128,256]{2,1,0:T(8,128)(2,1)S(1)} %get-tuple-element.53), channel_id=1, source_target_pairs={{0,8},{8,24},{16,0},{24,16},{1,9},{9,25},{17,1},{25,17},{2,10},{10... | collective-permute-start | bytes 393224 | tf_op jit(solution)/shard_map/ppermute | solution.py:299
  53.0 2.2 %collective-permute-start.8 = (bf16[128,1536]{1,0:T(8,128)(2,1)S(1)}, bf16[128,1536]{1,0:T(8,128)(2,1)S(1)}, u32[]{:S(2)}, u32[]{:S(2)}) collective-permute-start(bf16[128,1536]{1,0:T(8,128)(2,1)S(1)} %collective-permute-done.6.refs_0_), channel_id=1, source_target_pairs={{0,1},{1,0},{2,3},{3,2},{4,5},{5,4},{6,7},{7,6},{8,9},{9,8},{10,11... | collective-permute-start | bytes 1179656 | tf_op jit(solution)/shard_map/ppermute | solution.py:305
  55.4 7.0 %collective-permute-done.14.refs_2_ = bf16[2,128,256]{2,1,0:T(8,128)(2,1)S(1)} collective-permute-done((bf16[2,128,256]{2,1,0:T(8,128)(2,1)S(1)}, bf16[2,128,256]{2,1,0:T(8,128)(2,1)S(1)}, u32[]{:S(2)}, u32[]{:S(2)}) %collective-permute-start.14) | collective-permute-done | bytes 131104 | tf_op jit(solution)/shard_map/ppermute | solution.py:299
  62.4 1.3 %collective-permute-start.15 = (bf16[3,192,256]{2,1,0:T(8,128)(2,1)S(1)}, bf16[3,192,256]{2,1,0:T(8,128)(2,1)S(1)}, u32[]{:S(2)}, u32[]{:S(2)}) collective-permute-start(bf16[3,192,256]{2,1,0:T(8,128)(2,1)S(1)} %collective-permute-done.11.refs_0_), channel_id=1, source_target_pairs={{0,4},{2,6},{4,0},{6,2},{1,5},{3,7},{5,1},{7,3},{8,12},{10,14},{12... | collective-permute-start | bytes 884744 | tf_op jit(solution)/shard_map/ppermute | solution.py:302
  63.7 1.1 collective-permute-start.16
  64.8 5.4 %collective-permute-start.17 = (bf16[2,128,256]{2,1,0:T(8,128)(2,1)S(1)}, bf16[2,128,256]{2,1,0:T(8,128)(2,1)S(1)}, u32[]{:S(2)}, u32[]{:S(2)}) collective-permute-start(bf16[2,128,256]{2,1,0:T(8,128)(2,1)S(1)} %get-tuple-element.58), channel_id=1, source_target_pairs={{0,24},{8,16},{16,8},{24,0},{1,25},{9,17},{17,9},{25,1},{2,26},{10... | collective-permute-start | bytes 393224 | tf_op jit(solution)/shard_map/ppermute | solution.py:299
  70.3 2.0 %collective-permute-start.19 = (bf16[2,128,256]{2,1,0:T(8,128)(2,1)S(1)}, bf16[2,128,256]{2,1,0:T(8,128)(2,1)S(1)}, u32[]{:S(2)}, u32[]{:S(2)}) collective-permute-start(bf16[2,128,256]{2,1,0:T(8,128)(2,1)S(1)} %collective-permute-done.16.refs_3_), channel_id=1, source_target_pairs={{0,4},{2,6},{4,0},{6,2},{1,5},{3,7},{5,1},{7,3},{8,12},{10,14},{12... | collective-permute-start | bytes 393224 | tf_op jit(solution)/shard_map/ppermute | solution.py:302
  72.3 2.4 %collective-permute-done.17.refs_0_ = bf16[2,128,256]{2,1,0:T(8,128)(2,1)S(1)} collective-permute-done((bf16[2,128,256]{2,1,0:T(8,128)(2,1)S(1)}, bf16[2,128,256]{2,1,0:T(8,128)(2,1)S(1)}, u32[]{:S(2)}, u32[]{:S(2)}) %collective-permute-start.17) | collective-permute-done | bytes 131104 | tf_op jit(solution)/shard_map/ppermute | solution.py:299
  75.2 1.4 %collective-permute-done.19.refs_5_ = bf16[2,128,256]{2,1,0:T(8,128)(2,1)S(1)} collective-permute-done((bf16[2,128,256]{2,1,0:T(8,128)(2,1)S(1)}, bf16[2,128,256]{2,1,0:T(8,128)(2,1)S(1)}, u32[]{:S(2)}, u32[]{:S(2)}) %collective-permute-start.19) | collective-permute-done | bytes 131104 | tf_op jit(solution)/shard_map/ppermute | solution.py:302
  76.6 3.0 %collective-permute-done.20.refs_1_ = bf16[2,128,256]{2,1,0:T(8,128)(2,1)S(1)} collective-permute-done((bf16[2,128,256]{2,1,0:T(8,128)(2,1)S(1)}, bf16[2,128,256]{2,1,0:T(8,128)(2,1)S(1)}, u32[]{:S(2)}, u32[]{:S(2)}) %collective-permute-start.20) | collective-permute-done | bytes 131104 | tf_op jit(solution)/shard_map/ppermute | solution.py:302
  84.6 1.2 %collective-permute-done.22.refs_13_ = bf16[2,3,192,256]{3,2,1,0:T(8,128)(2,1)S(1)} collective-permute-done((bf16[2,3,192,256]{3,2,1,0:T(8,128)(2,1)S(1)}, bf16[2,3,192,256]{3,2,1,0:T(8,128)(2,1)S(1)}, u32[]{:S(2)}, u32[]{:S(2)}) %collective-permute-start.22) | collective-permute-done | bytes 589856 | tf_op jit(solution)/shard_map/ppermute | solution.py:302
  85.8 3.0 %shard_map.125.qkv = bf16[3,512,256]{2,1,0:T(8,128)(2,1)S(1)} custom-call(f32[1,128]{1,0:T(1,128)S(1)} %bitcast.48, f32[1,128]{1,0:T(1,128)S(1)} %bitcast.49, bf16[128,3072]{1,0:T(8,128)(2,1)S(1)} %shard_map.118.refs_0_, bf16[128,3072]{1,0:T(8,128)(2,1)S(1)} %shard_map.120.refs_1_, bf16[128,3072]{1,0:T(8,128)(2,1)S(1)} %shard_map.121.refs_2_, ...), custom_call_target="tpu_custom_call" | custom-call | tf_op jit(solution)/shard_map/pallas_call | solution.py:145
  88.9 5.0 %shard_map.128 = (bf16[128,256]{1,0:T(8,128)(2,1)S(1)}, bf16[128,256]{1,0:T(8,128)(2,1)S(1)}, bf16[128,256]{1,0:T(8,128)(2,1)S(1)}, bf16[128,256]{1,0:T(8,128)(2,1)S(1)}) custom-call(bf16[3,512,256]{2,1,0:T(8,128)(2,1)S(1)} %shard_map.125.qkv, bf16[512,1024]{1,0:T(8,128)(2,1)S(1)} %copy-done.1, bf16[512,1024]{1,0:T(8,128)(2,1)S(1)} %copy-done.2, ...), custom_call_target="tpu_custom_call" | custom-call | tf_op jit(solution)/shard_map/pallas_call | solution.py:233
  93.9 2.6 %collective-permute-start.25 = (bf16[128,256]{1,0:T(8,128)(2,1)S(1)}, bf16[128,256]{1,0:T(8,128)(2,1)S(1)}, u32[]{:S(2)}, u32[]{:S(2)}) collective-permute-start(bf16[128,256]{1,0:T(8,128)(2,1)S(1)} %get-tuple-element.66), channel_id=1, source_target_pairs={{0,16},{8,0},{16,24},{24,8},{1,17},{9,1},{17,25},{25,9},{2,18},{10... | collective-permute-start | bytes 196616 | tf_op jit(solution)/shard_map/ppermute | solution.py:299
  96.5 1.7 %collective-permute-start.26 = (bf16[128,256]{1,0:T(8,128)(2,1)S(1)}, bf16[128,256]{1,0:T(8,128)(2,1)S(1)}, u32[]{:S(2)}, u32[]{:S(2)}) collective-permute-start(bf16[128,256]{1,0:T(8,128)(2,1)S(1)} %get-tuple-element.67), channel_id=1, source_target_pairs={{0,24},{8,16},{16,8},{24,0},{1,25},{9,17},{17,9},{25,1},{2,26},{10... | collective-permute-start | bytes 196616 | tf_op jit(solution)/shard_map/ppermute | solution.py:299
  98.5 4.4 %collective-permute-done.26.refs_2_ = bf16[128,256]{1,0:T(8,128)(2,1)S(1)} collective-permute-done((bf16[128,256]{1,0:T(8,128)(2,1)S(1)}, bf16[128,256]{1,0:T(8,128)(2,1)S(1)}, u32[]{:S(2)}, u32[]{:S(2)}) %collective-permute-start.26) | collective-permute-done | bytes 65568 | tf_op jit(solution)/shard_map/ppermute | solution.py:299
  104.5 1.5 %collective-permute-start.28 = (bf16[128,1536]{1,0:T(8,128)(2,1)S(1)}, bf16[128,1536]{1,0:T(8,128)(2,1)S(1)}, u32[]{:S(2)}, u32[]{:S(2)}) collective-permute-start(bf16[128,1536]{1,0:T(8,128)(2,1)S(1)} %shard_map.130), channel_id=1, source_target_pairs={{0,1},{1,0},{2,3},{3,2},{4,5},{5,4},{6,7},{7,6},{8,9},{9,8},{10,11... | collective-permute-start | bytes 1179656 | tf_op jit(solution)/shard_map/ppermute | solution.py:305
  106.6 8.6 %collective-permute-done.28 = bf16[128,1536]{1,0:T(8,128)(2,1)S(1)} collective-permute-done((bf16[128,1536]{1,0:T(8,128)(2,1)S(1)}, bf16[128,1536]{1,0:T(8,128)(2,1)S(1)}, u32[]{:S(2)}, u32[]{:S(2)}) %collective-permute-start.28) | collective-permute-done | bytes 393248 | tf_op jit(solution)/shard_map/ppermute | solution.py:305
  (67 shorter events, 18.1 us)
Async XLA Ops:
  0.0 12.3 %collective-permute-start = (bf16[128,1536]{1,0:T(8,128)(2,1)}, bf16[128,1536]{1,0:T(8,128)(2,1)S(1)}, u32[]{:S(2)}, u32[]{:S(2)}) collective-permute-start(bf16[128,1536]{1,0:T(8,128)(2,1)} %refs_0_.1), channel_id=1, source_target_pairs={{0,1},{1,0},{2,3},{3,2},{4,5},{5,4},{6,7},{7,6},{8,9},{9,8},{10,11... | collective-permute-start | bytes 1179656 | tf_op jit(solution)/shard_map/ppermute | solution.py:305
  2.9 11.7 %collective-permute-start.1 = (bf16[128,1536]{1,0:T(8,128)(2,1)}, bf16[128,1536]{1,0:T(8,128)(2,1)S(1)}, u32[]{:S(2)}, u32[]{:S(2)}) collective-permute-start(bf16[128,1536]{1,0:T(8,128)(2,1)} %refs_0_.1), channel_id=1, source_target_pairs={{0,8},{8,24},{16,0},{24,16},{1,9},{9,25},{17,1},{25,17},{2,10},{10... | collective-permute-start | bytes 1179656 | tf_op jit(solution)/shard_map/ppermute | solution.py:299
  7.7 36.9 %copy-start.3 = (bf16[128,1536]{1,0:T(8,128)(2,1)S(1)}, bf16[128,1536]{1,0:T(8,128)(2,1)}, u32[]{:S(2)}) copy-start(bf16[128,1536]{1,0:T(8,128)(2,1)} %refs_0_.1) | copy-start | bytes 1179652
  14.6 9.7 %collective-permute-start.2 = (bf16[128,1536]{1,0:T(8,128)(2,1)S(1)}, bf16[128,1536]{1,0:T(8,128)(2,1)S(1)}, u32[]{:S(2)}, u32[]{:S(2)}) collective-permute-start(bf16[128,1536]{1,0:T(8,128)(2,1)S(1)} %collective-permute-done.1.refs_0_), channel_id=1, source_target_pairs={{0,1},{1,0},{2,3},{3,2},{4,5},{5,4},{6,7},{7,6},{8,9},{9,8},{10,11... | collective-permute-start | bytes 1179656 | tf_op jit(solution)/shard_map/ppermute | solution.py:305
  15.1 13.0 %collective-permute-start.3 = (bf16[128,1536]{1,0:T(8,128)(2,1)S(1)}, bf16[128,1536]{1,0:T(8,128)(2,1)S(1)}, u32[]{:S(2)}, u32[]{:S(2)}) collective-permute-start(bf16[128,1536]{1,0:T(8,128)(2,1)S(1)} %collective-permute-done.1.refs_0_), channel_id=1, source_target_pairs={{0,8},{8,24},{16,0},{24,16},{1,9},{9,25},{17,1},{25,17},{2,10},{10... | collective-permute-start | bytes 1179656 | tf_op jit(solution)/shard_map/ppermute | solution.py:299
  16.1 17.8 %collective-permute-start.5 = (bf16[3,192,256]{2,1,0:T(8,128)(2,1)S(1)}, bf16[3,192,256]{2,1,0:T(8,128)(2,1)S(1)}, u32[]{:S(2)}, u32[]{:S(2)}) collective-permute-start(bf16[3,192,256]{2,1,0:T(8,128)(2,1)S(1)} %get-tuple-element.41), channel_id=1, source_target_pairs={{0,8},{8,24},{16,0},{24,16},{1,9},{9,25},{17,1},{25,17},{2,10},{10... | collective-permute-start | bytes 884744 | tf_op jit(solution)/shard_map/ppermute | solution.py:299
  19.3 14.5 %collective-permute-start.9 = (bf16[3,192,256]{2,1,0:T(8,128)(2,1)S(1)}, bf16[3,192,256]{2,1,0:T(8,128)(2,1)S(1)}, u32[]{:S(2)}, u32[]{:S(2)}) collective-permute-start(bf16[3,192,256]{2,1,0:T(8,128)(2,1)S(1)} %get-tuple-element.62.refs_0_), channel_id=1, source_target_pairs={{0,4},{2,6},{4,0},{6,2},{1,5},{3,7},{5,1},{7,3},{8,12},{10,14},{12... | collective-permute-start | bytes 884744 | tf_op jit(solution)/shard_map/ppermute | solution.py:302
  28.2 16.3 %collective-permute-start.4 = (bf16[128,1536]{1,0:T(8,128)(2,1)S(1)}, bf16[128,1536]{1,0:T(8,128)(2,1)S(1)}, u32[]{:S(2)}, u32[]{:S(2)}) collective-permute-start(bf16[128,1536]{1,0:T(8,128)(2,1)S(1)} %collective-permute-done.3.refs_0_), channel_id=1, source_target_pairs={{0,1},{1,0},{2,3},{3,2},{4,5},{5,4},{6,7},{7,6},{8,9},{9,8},{10,11... | collective-permute-start | bytes 1179656 | tf_op jit(solution)/shard_map/ppermute | solution.py:305
  29.7 14.8 %collective-permute-start.10 = (bf16[3,192,256]{2,1,0:T(8,128)(2,1)S(1)}, bf16[3,192,256]{2,1,0:T(8,128)(2,1)S(1)}, u32[]{:S(2)}, u32[]{:S(2)}) collective-permute-start(bf16[3,192,256]{2,1,0:T(8,128)(2,1)S(1)} %get-tuple-element.47), channel_id=1, source_target_pairs={{0,16},{8,0},{16,24},{24,8},{1,17},{9,1},{17,25},{25,9},{2,18},{10... | collective-permute-start | bytes 884744 | tf_op jit(solution)/shard_map/ppermute | solution.py:299
  33.9 10.6 %collective-permute-start.12 = (bf16[3,192,256]{2,1,0:T(8,128)(2,1)S(1)}, bf16[3,192,256]{2,1,0:T(8,128)(2,1)S(1)}, u32[]{:S(2)}, u32[]{:S(2)}) collective-permute-start(bf16[3,192,256]{2,1,0:T(8,128)(2,1)S(1)} %collective-permute-done.5.refs_2_), channel_id=1, source_target_pairs={{0,4},{2,6},{4,0},{6,2},{1,5},{3,7},{5,1},{7,3},{8,12},{10,14},{12... | collective-permute-start | bytes 884744 | tf_op jit(solution)/shard_map/ppermute | solution.py:302
  34.9 18.1 %collective-permute-start.6 = (bf16[128,1536]{1,0:T(8,128)(2,1)S(1)}, bf16[128,1536]{1,0:T(8,128)(2,1)S(1)}, u32[]{:S(2)}, u32[]{:S(2)}) collective-permute-start(bf16[128,1536]{1,0:T(8,128)(2,1)S(1)} %collective-permute-done.3.refs_0_), channel_id=1, source_target_pairs={{0,8},{8,24},{16,0},{24,16},{1,9},{9,25},{17,1},{25,17},{2,10},{10... | collective-permute-start | bytes 1179656 | tf_op jit(solution)/shard_map/ppermute | solution.py:299
  41.3 14.1 %collective-permute-start.11 = (bf16[3,192,256]{2,1,0:T(8,128)(2,1)S(1)}, bf16[3,192,256]{2,1,0:T(8,128)(2,1)S(1)}, u32[]{:S(2)}, u32[]{:S(2)}) collective-permute-start(bf16[3,192,256]{2,1,0:T(8,128)(2,1)S(1)} %get-tuple-element.49), channel_id=1, source_target_pairs={{0,24},{8,16},{16,8},{24,0},{1,25},{9,17},{17,9},{25,1},{2,26},{10... | collective-permute-start | bytes 884744 | tf_op jit(solution)/shard_map/ppermute | solution.py:299
  44.5 17.9 %collective-permute-start.13 = (bf16[3,192,256]{2,1,0:T(8,128)(2,1)S(1)}, bf16[3,192,256]{2,1,0:T(8,128)(2,1)S(1)}, u32[]{:S(2)}, u32[]{:S(2)}) collective-permute-start(bf16[3,192,256]{2,1,0:T(8,128)(2,1)S(1)} %collective-permute-done.10.refs_3_), channel_id=1, source_target_pairs={{0,4},{2,6},{4,0},{6,2},{1,5},{3,7},{5,1},{7,3},{8,12},{10,14},{12... | collective-permute-start | bytes 884744 | tf_op jit(solution)/shard_map/ppermute | solution.py:302
  47.7 5.3 %collective-permute-start.7 = (bf16[2,128,256]{2,1,0:T(8,128)(2,1)S(1)}, bf16[2,128,256]{2,1,0:T(8,128)(2,1)S(1)}, u32[]{:S(2)}, u32[]{:S(2)}) collective-permute-start(bf16[2,128,256]{2,1,0:T(8,128)(2,1)S(1)} %get-tuple-element.64.refs_0_), channel_id=1, source_target_pairs={{0,4},{2,6},{4,0},{6,2},{1,5},{3,7},{5,1},{7,3},{8,12},{10,14},{12... | collective-permute-start | bytes 393224 | tf_op jit(solution)/shard_map/ppermute | solution.py:302
  49.7 12.7 %collective-permute-start.14 = (bf16[2,128,256]{2,1,0:T(8,128)(2,1)S(1)}, bf16[2,128,256]{2,1,0:T(8,128)(2,1)S(1)}, u32[]{:S(2)}, u32[]{:S(2)}) collective-permute-start(bf16[2,128,256]{2,1,0:T(8,128)(2,1)S(1)} %get-tuple-element.53), channel_id=1, source_target_pairs={{0,8},{8,24},{16,0},{24,16},{1,9},{9,25},{17,1},{25,17},{2,10},{10... | collective-permute-start | bytes 393224 | tf_op jit(solution)/shard_map/ppermute | solution.py:299
  53.0 21.7 %collective-permute-start.8 = (bf16[128,1536]{1,0:T(8,128)(2,1)S(1)}, bf16[128,1536]{1,0:T(8,128)(2,1)S(1)}, u32[]{:S(2)}, u32[]{:S(2)}) collective-permute-start(bf16[128,1536]{1,0:T(8,128)(2,1)S(1)} %collective-permute-done.6.refs_0_), channel_id=1, source_target_pairs={{0,1},{1,0},{2,3},{3,2},{4,5},{5,4},{6,7},{7,6},{8,9},{9,8},{10,11... | collective-permute-start | bytes 1179656 | tf_op jit(solution)/shard_map/ppermute | solution.py:305
  62.4 17.3 %collective-permute-start.15 = (bf16[3,192,256]{2,1,0:T(8,128)(2,1)S(1)}, bf16[3,192,256]{2,1,0:T(8,128)(2,1)S(1)}, u32[]{:S(2)}, u32[]{:S(2)}) collective-permute-start(bf16[3,192,256]{2,1,0:T(8,128)(2,1)S(1)} %collective-permute-done.11.refs_0_), channel_id=1, source_target_pairs={{0,4},{2,6},{4,0},{6,2},{1,5},{3,7},{5,1},{7,3},{8,12},{10,14},{12... | collective-permute-start | bytes 884744 | tf_op jit(solution)/shard_map/ppermute | solution.py:302
  63.7 6.6 %collective-permute-start.16 = (bf16[2,128,256]{2,1,0:T(8,128)(2,1)S(1)}, bf16[2,128,256]{2,1,0:T(8,128)(2,1)S(1)}, u32[]{:S(2)}, u32[]{:S(2)}) collective-permute-start(bf16[2,128,256]{2,1,0:T(8,128)(2,1)S(1)} %get-tuple-element.56), channel_id=1, source_target_pairs={{0,16},{8,0},{16,24},{24,8},{1,17},{9,1},{17,25},{25,9},{2,18},{10... | collective-permute-start | bytes 393224 | tf_op jit(solution)/shard_map/ppermute | solution.py:299
  64.8 9.8 %collective-permute-start.17 = (bf16[2,128,256]{2,1,0:T(8,128)(2,1)S(1)}, bf16[2,128,256]{2,1,0:T(8,128)(2,1)S(1)}, u32[]{:S(2)}, u32[]{:S(2)}) collective-permute-start(bf16[2,128,256]{2,1,0:T(8,128)(2,1)S(1)} %get-tuple-element.58), channel_id=1, source_target_pairs={{0,24},{8,16},{16,8},{24,0},{1,25},{9,17},{17,9},{25,1},{2,26},{10... | collective-permute-start | bytes 393224 | tf_op jit(solution)/shard_map/ppermute | solution.py:299
  70.2 5.0 %collective-permute-start.18 = (bf16[2,128,256]{2,1,0:T(8,128)(2,1)S(1)}, bf16[2,128,256]{2,1,0:T(8,128)(2,1)S(1)}, u32[]{:S(2)}, u32[]{:S(2)}) collective-permute-start(bf16[2,128,256]{2,1,0:T(8,128)(2,1)S(1)} %collective-permute-done.14.refs_2_), channel_id=1, source_target_pairs={{0,4},{2,6},{4,0},{6,2},{1,5},{3,7},{5,1},{7,3},{8,12},{10,14},{12... | collective-permute-start | bytes 393224 | tf_op jit(solution)/shard_map/ppermute | solution.py:302
  70.3 6.3 %collective-permute-start.19 = (bf16[2,128,256]{2,1,0:T(8,128)(2,1)S(1)}, bf16[2,128,256]{2,1,0:T(8,128)(2,1)S(1)}, u32[]{:S(2)}, u32[]{:S(2)}) collective-permute-start(bf16[2,128,256]{2,1,0:T(8,128)(2,1)S(1)} %collective-permute-done.16.refs_3_), channel_id=1, source_target_pairs={{0,4},{2,6},{4,0},{6,2},{1,5},{3,7},{5,1},{7,3},{8,12},{10,14},{12... | collective-permute-start | bytes 393224 | tf_op jit(solution)/shard_map/ppermute | solution.py:302
  74.7 5.0 %collective-permute-start.20 = (bf16[2,128,256]{2,1,0:T(8,128)(2,1)S(1)}, bf16[2,128,256]{2,1,0:T(8,128)(2,1)S(1)}, u32[]{:S(2)}, u32[]{:S(2)}) collective-permute-start(bf16[2,128,256]{2,1,0:T(8,128)(2,1)S(1)} %collective-permute-done.17.refs_0_), channel_id=1, source_target_pairs={{0,4},{2,6},{4,0},{6,2},{1,5},{3,7},{5,1},{7,3},{8,12},{10,14},{12... | collective-permute-start | bytes 393224 | tf_op jit(solution)/shard_map/ppermute | solution.py:302
  80.1 5.7 %collective-permute-start.21 = (bf16[6,3,192,256]{3,2,1,0:T(8,128)(2,1)S(1)}, bf16[6,3,192,256]{3,2,1,0:T(8,128)(2,1)S(1)}, u32[]{:S(2)}, u32[]{:S(2)}) collective-permute-start(bf16[6,3,192,256]{3,2,1,0:T(8,128)(2,1)S(1)} %shard_map.123), channel_id=1, source_target_pairs={{0,2},{2,0},{4,6},{6,4},{1,3},{3,1},{5,7},{7,5},{8,10},{10,8},{12,... | collective-permute-start | bytes 5308424 | tf_op jit(solution)/shard_map/ppermute | solution.py:302
  81.2 7.7 %collective-permute-start.23 = (bf16[6,2,128,256]{3,2,1,0:T(8,128)(2,1)S(1)}, bf16[6,2,128,256]{3,2,1,0:T(8,128)(2,1)S(1)}, u32[]{:S(2)}, u32[]{:S(2)}) collective-permute-start(bf16[6,2,128,256]{3,2,1,0:T(8,128)(2,1)S(1)} %shard_map.126), channel_id=1, source_target_pairs={{0,2},{2,0},{4,6},{6,4},{1,3},{3,1},{5,7},{7,5},{8,10},{10,8},{12,... | collective-permute-start | bytes 2359304 | tf_op jit(solution)/shard_map/ppermute | solution.py:302
  83.6 2.2 %collective-permute-start.22 = (bf16[2,3,192,256]{3,2,1,0:T(8,128)(2,1)S(1)}, bf16[2,3,192,256]{3,2,1,0:T(8,128)(2,1)S(1)}, u32[]{:S(2)}, u32[]{:S(2)}) collective-permute-start(bf16[2,3,192,256]{3,2,1,0:T(8,128)(2,1)S(1)} %shard_map.124), channel_id=1, source_target_pairs={{0,2},{2,0},{4,6},{6,4},{1,3},{3,1},{5,7},{7,5},{8,10},{10,8},{12,... | collective-permute-start | bytes 1769480 | tf_op jit(solution)/shard_map/ppermute | solution.py:302
  83.7 20.1 %slice-start = ((s8[6291456]{0:T(1024)(128)(4,1)}), s8[4194304]{0:T(1024)(128)(4,1)S(1)}, s32[]{:S(2)}) async-start(s8[6291456]{0:T(1024)(128)(4,1)} %bitcast.21), calls=%async_computation | async-start | bytes 8388608
  84.1 4.8 %collective-permute-start.24 = (bf16[2,2,128,256]{3,2,1,0:T(8,128)(2,1)S(1)}, bf16[2,2,128,256]{3,2,1,0:T(8,128)(2,1)S(1)}, u32[]{:S(2)}, u32[]{:S(2)}) collective-permute-start(bf16[2,2,128,256]{3,2,1,0:T(8,128)(2,1)S(1)} %shard_map.127), channel_id=1, source_target_pairs={{0,2},{2,0},{4,6},{6,4},{1,3},{3,1},{5,7},{7,5},{8,10},{10,8},{12,... | collective-permute-start | bytes 786440 | tf_op jit(solution)/shard_map/ppermute | solution.py:302
  85.8 18.0 %slice-start.1 = ((s8[6291456]{0:T(1024)(128)(4,1)}), s8[2097152]{0:T(1024)(128)(4,1)S(1)}, s32[]{:S(2)}) async-start(s8[6291456]{0:T(1024)(128)(4,1)} %bitcast.21), calls=%async_computation.1 | async-start | bytes 4194304
  93.9 4.6 %collective-permute-start.25 = (bf16[128,256]{1,0:T(8,128)(2,1)S(1)}, bf16[128,256]{1,0:T(8,128)(2,1)S(1)}, u32[]{:S(2)}, u32[]{:S(2)}) collective-permute-start(bf16[128,256]{1,0:T(8,128)(2,1)S(1)} %get-tuple-element.66), channel_id=1, source_target_pairs={{0,16},{8,0},{16,24},{24,8},{1,17},{9,1},{17,25},{25,9},{2,18},{10... | collective-permute-start | bytes 196616 | tf_op jit(solution)/shard_map/ppermute | solution.py:299
  96.5 6.3 %collective-permute-start.26 = (bf16[128,256]{1,0:T(8,128)(2,1)S(1)}, bf16[128,256]{1,0:T(8,128)(2,1)S(1)}, u32[]{:S(2)}, u32[]{:S(2)}) collective-permute-start(bf16[128,256]{1,0:T(8,128)(2,1)S(1)} %get-tuple-element.67), channel_id=1, source_target_pairs={{0,24},{8,16},{16,8},{24,0},{1,25},{9,17},{17,9},{25,1},{2,26},{10... | collective-permute-start | bytes 196616 | tf_op jit(solution)/shard_map/ppermute | solution.py:299
  98.2 5.6 %collective-permute-start.27 = (bf16[128,256]{1,0:T(8,128)(2,1)S(1)}, bf16[128,256]{1,0:T(8,128)(2,1)S(1)}, u32[]{:S(2)}, u32[]{:S(2)}) collective-permute-start(bf16[128,256]{1,0:T(8,128)(2,1)S(1)} %get-tuple-element.68), channel_id=1, source_target_pairs={{0,8},{8,24},{16,0},{24,16},{1,9},{9,25},{17,1},{25,17},{2,10},{10... | collective-permute-start | bytes 196616 | tf_op jit(solution)/shard_map/ppermute | solution.py:299
  104.5 10.7 %collective-permute-start.28 = (bf16[128,1536]{1,0:T(8,128)(2,1)S(1)}, bf16[128,1536]{1,0:T(8,128)(2,1)S(1)}, u32[]{:S(2)}, u32[]{:S(2)}) collective-permute-start(bf16[128,1536]{1,0:T(8,128)(2,1)S(1)} %shard_map.130), channel_id=1, source_target_pairs={{0,1},{1,0},{2,3},{3,2},{4,5},{5,4},{6,7},{7,6},{8,9},{9,8},{10,11... | collective-permute-start | bytes 1179656 | tf_op jit(solution)/shard_map/ppermute | solution.py:305
  (10 other events, 27.9 us)

commit v5 on v4

--- a/solution.py
+++ b/solution.py
@@ -352,7 +352,7 @@
         ready += [*hops[:1], *crossed[:1]] if index else []
         found[step, 0] = turn(after(packed[step], *ready), step)
         if index == len(order) - 1:
-            ahead = [spread(cached, 0, *hops[1:2], *mods[:2])]
+            ahead = [spread(cached, 0, *hops[1:2], *mods[:3])]
         cross(hops[-1], *crossed[-1:], *packed[:1], *ahead)
     for index, step in enumerate(order):
         ready = hops[1:2] if index == 0 else []
@@ -370,7 +370,7 @@
     waits += crossed + swapped + ahead
     arrays, stacks = finish(found, last_step, waits, mods + [cached[last_step, 0]])
     qkv = project(mods, arrays, stacks, groups, rest, query_gain, key_gain)
-    arrays, stacks = finish(cached, last_step, [cached[last_step, 0]], [])
+    arrays, stacks = finish(cached, last_step, [cached[last_step, 0], arrays[-1]], [])
     attention = attend(qkv, text_keys, text_values, arrays, stacks, groups, size)
     pieces = [attention[0]] * groups
     for step in sorted(range(1, groups), key=lambda step: -min(step, groups - step)):

time: 116 us -> 117 us (level)
    ppermute x12, waiting for transfers between devices: 6.2 us -> 7.94 us  [swap(): return lax.ppermute(array, 'rest', [(i, i ^ bit) for i in range(rest)])]
  transfers between devices with their start and end apart: 29 -> 29, of which waited for: 16 -> 15; matrix products, arithmetic and copies ran while one was open for 0% -> 0% of each run, Pallas kernels for 8% -> 8%
where the time goes in v5:
time: 117 us
  starting transfers between devices  48.3 us (41%)
  waiting for transfers between devices  48.1 us (41%)
  Pallas kernels  14.8 us (13%)
  local copies, waits for them, and re-layouts  4.63 us (4%)
    ppermute x12, starting transfers between devices, turn(): return lax.ppermute(array, 'group', pairs)  30.4 us
    ppermute x12, waiting for transfers between devices, turn(): return lax.ppermute(array, 'group', pairs)  24 us
    ppermute x5, waiting for transfers between devices, across(): lax.ppermute(array, 'head', [(i, (i + hop) % n_head) for i in range(n_hea...  16.3 us
    ppermute x12, starting transfers between devices, swap(): return lax.ppermute(array, 'rest', [(i, i ^ bit) for i in range(rest)])  9.27 us
    ppermute x5, starting transfers between devices, across(): lax.ppermute(array, 'head', [(i, (i + hop) % n_head) for i in range(n_hea...  8.66 us
    ppermute x12, waiting for transfers between devices, swap(): return lax.ppermute(array, 'rest', [(i, i ^ bit) for i in range(rest)])  7.94 us
    pallas_call x1, Pallas kernels, attend(): pl.pallas_call(functools.partial(attend_kernel, groups, size, stacks), ou...  4.98 us
    unnamed x26, local copies, waits for them, and re-layouts  4.63 us
  transfers between devices with their start and end apart: 29, of which 15 were waited for; matrix products, arithmetic and copies ran while one was open for 0% of the time, Pallas kernels for 8%

profile of v5, /device:TPU:0, one launch (start us, length us, event | category | flops | bytes accessed | tf_op | source)
XLA Modules:
  0.0 117.0 jit_solution(10289766205046994787)
XLA Ops:
  0.0 2.9 %collective-permute-start = (bf16[128,1536]{1,0:T(8,128)(2,1)}, bf16[128,1536]{1,0:T(8,128)(2,1)S(1)}, u32[]{:S(2)}, u32[]{:S(2)}) collective-permute-start(bf16[128,1536]{1,0:T(8,128)(2,1)} %refs_0_.1), channel_id=1, source_target_pairs={{0,1},{1,0},{2,3},{3,2},{4,5},{5,4},{6,7},{7,6},{8,9},{9,8},{10,11... | collective-permute-start | bytes 1179656 | tf_op jit(solution)/shard_map/ppermute | solution.py:305
  2.9 1.6 %collective-permute-start.1 = (bf16[128,1536]{1,0:T(8,128)(2,1)}, bf16[128,1536]{1,0:T(8,128)(2,1)S(1)}, u32[]{:S(2)}, u32[]{:S(2)}) collective-permute-start(bf16[128,1536]{1,0:T(8,128)(2,1)} %refs_0_.1), channel_id=1, source_target_pairs={{0,8},{8,24},{16,0},{24,16},{1,9},{9,25},{17,1},{25,17},{2,10},{10... | collective-permute-start | bytes 1179656 | tf_op jit(solution)/shard_map/ppermute | solution.py:299
  4.5 1.3 %copy-done = bf16[192,3,1024]{2,0,1:T(8,128)(2,1)S(1)} copy-done((bf16[192,3,1024]{2,0,1:T(8,128)(2,1)S(1)}, bf16[192,3,1024]{2,0,1:T(8,128)(2,1)}, u32[]{:S(2)}) %copy-start) | copy-done | bytes 1179672
  8.1 4.2 %collective-permute-done.refs_1_ = bf16[128,1536]{1,0:T(8,128)(2,1)S(1)} collective-permute-done((bf16[128,1536]{1,0:T(8,128)(2,1)}, bf16[128,1536]{1,0:T(8,128)(2,1)S(1)}, u32[]{:S(2)}, u32[]{:S(2)}) %collective-permute-start) | collective-permute-done | bytes 393248 | tf_op jit(solution)/shard_map/ppermute | solution.py:305
  12.3 2.4 %collective-permute-done.1.refs_0_ = bf16[128,1536]{1,0:T(8,128)(2,1)S(1)} collective-permute-done((bf16[128,1536]{1,0:T(8,128)(2,1)}, bf16[128,1536]{1,0:T(8,128)(2,1)S(1)}, u32[]{:S(2)}, u32[]{:S(2)}) %collective-permute-start.1) | collective-permute-done | bytes 393248 | tf_op jit(solution)/shard_map/ppermute | solution.py:299
  16.1 3.3 %collective-permute-start.5 = (bf16[3,192,256]{2,1,0:T(8,128)(2,1)S(1)}, bf16[3,192,256]{2,1,0:T(8,128)(2,1)S(1)}, u32[]{:S(2)}, u32[]{:S(2)}) collective-permute-start(bf16[3,192,256]{2,1,0:T(8,128)(2,1)S(1)} %get-tuple-element.41), channel_id=1, source_target_pairs={{0,8},{8,24},{16,0},{24,16},{1,9},{9,25},{17,1},{25,17},{2,10},{10... | collective-permute-start | bytes 884744 | tf_op jit(solution)/shard_map/ppermute | solution.py:299
  19.3 1.5 %collective-permute-start.9 = (bf16[3,192,256]{2,1,0:T(8,128)(2,1)S(1)}, bf16[3,192,256]{2,1,0:T(8,128)(2,1)S(1)}, u32[]{:S(2)}, u32[]{:S(2)}) collective-permute-start(bf16[3,192,256]{2,1,0:T(8,128)(2,1)S(1)} %get-tuple-element.62.refs_0_), channel_id=1, source_target_pairs={{0,4},{2,6},{4,0},{6,2},{1,5},{3,7},{5,1},{7,3},{8,12},{10,14},{12... | collective-permute-start | bytes 884744 | tf_op jit(solution)/shard_map/ppermute | solution.py:302
  20.8 3.5 %collective-permute-done.2.refs_1_ = bf16[128,1536]{1,0:T(8,128)(2,1)S(1)} collective-permute-done((bf16[128,1536]{1,0:T(8,128)(2,1)S(1)}, bf16[128,1536]{1,0:T(8,128)(2,1)S(1)}, u32[]{:S(2)}, u32[]{:S(2)}) %collective-permute-start.2) | collective-permute-done | bytes 393248 | tf_op jit(solution)/shard_map/ppermute | solution.py:305
  24.3 3.9 %collective-permute-done.3.refs_0_ = bf16[128,1536]{1,0:T(8,128)(2,1)S(1)} collective-permute-done((bf16[128,1536]{1,0:T(8,128)(2,1)S(1)}, bf16[128,1536]{1,0:T(8,128)(2,1)S(1)}, u32[]{:S(2)}, u32[]{:S(2)}) %collective-permute-start.3) | collective-permute-done | bytes 393248 | tf_op jit(solution)/shard_map/ppermute | solution.py:299
  28.2 1.5 %collective-permute-start.4 = (bf16[128,1536]{1,0:T(8,128)(2,1)S(1)}, bf16[128,1536]{1,0:T(8,128)(2,1)S(1)}, u32[]{:S(2)}, u32[]{:S(2)}) collective-permute-start(bf16[128,1536]{1,0:T(8,128)(2,1)S(1)} %collective-permute-done.3.refs_0_), channel_id=1, source_target_pairs={{0,1},{1,0},{2,3},{3,2},{4,5},{5,4},{6,7},{7,6},{8,9},{9,8},{10,11... | collective-permute-start | bytes 1179656 | tf_op jit(solution)/shard_map/ppermute | solution.py:305
  30.8 3.0 %collective-permute-done.5.refs_2_ = bf16[3,192,256]{2,1,0:T(8,128)(2,1)S(1)} collective-permute-done((bf16[3,192,256]{2,1,0:T(8,128)(2,1)S(1)}, bf16[3,192,256]{2,1,0:T(8,128)(2,1)S(1)}, u32[]{:S(2)}, u32[]{:S(2)}) %collective-permute-start.5) | collective-permute-done | bytes 294944 | tf_op jit(solution)/shard_map/ppermute | solution.py:299
  34.9 6.4 %collective-permute-start.6 = (bf16[128,1536]{1,0:T(8,128)(2,1)S(1)}, bf16[128,1536]{1,0:T(8,128)(2,1)S(1)}, u32[]{:S(2)}, u32[]{:S(2)}) collective-permute-start(bf16[128,1536]{1,0:T(8,128)(2,1)S(1)} %collective-permute-done.3.refs_0_), channel_id=1, source_target_pairs={{0,8},{8,24},{16,0},{24,16},{1,9},{9,25},{17,1},{25,17},{2,10},{10... | collective-permute-start | bytes 1179656 | tf_op jit(solution)/shard_map/ppermute | solution.py:299
  41.3 3.2 %collective-permute-start.11 = (bf16[3,192,256]{2,1,0:T(8,128)(2,1)S(1)}, bf16[3,192,256]{2,1,0:T(8,128)(2,1)S(1)}, u32[]{:S(2)}, u32[]{:S(2)}) collective-permute-start(bf16[3,192,256]{2,1,0:T(8,128)(2,1)S(1)} %get-tuple-element.49), channel_id=1, source_target_pairs={{0,24},{8,16},{16,8},{24,0},{1,25},{9,17},{17,9},{25,1},{2,26},{10... | collective-permute-start | bytes 884744 | tf_op jit(solution)/shard_map/ppermute | solution.py:299
  48.5 2.0 %collective-permute-start.7 = (bf16[2,128,256]{2,1,0:T(8,128)(2,1)S(1)}, bf16[2,128,256]{2,1,0:T(8,128)(2,1)S(1)}, u32[]{:S(2)}, u32[]{:S(2)}) collective-permute-start(bf16[2,128,256]{2,1,0:T(8,128)(2,1)S(1)} %get-tuple-element.64.refs_0_), channel_id=1, source_target_pairs={{0,4},{2,6},{4,0},{6,2},{1,5},{3,7},{5,1},{7,3},{8,12},{10,14},{12... | collective-permute-start | bytes 393224 | tf_op jit(solution)/shard_map/ppermute | solution.py:302
  50.5 3.0 %collective-permute-start.14 = (bf16[2,128,256]{2,1,0:T(8,128)(2,1)S(1)}, bf16[2,128,256]{2,1,0:T(8,128)(2,1)S(1)}, u32[]{:S(2)}, u32[]{:S(2)}) collective-permute-start(bf16[2,128,256]{2,1,0:T(8,128)(2,1)S(1)} %get-tuple-element.53), channel_id=1, source_target_pairs={{0,8},{8,24},{16,0},{24,16},{1,9},{9,25},{17,1},{25,17},{2,10},{10... | collective-permute-start | bytes 393224 | tf_op jit(solution)/shard_map/ppermute | solution.py:299
  53.6 2.2 %collective-permute-start.8 = (bf16[128,1536]{1,0:T(8,128)(2,1)S(1)}, bf16[128,1536]{1,0:T(8,128)(2,1)S(1)}, u32[]{:S(2)}, u32[]{:S(2)}) collective-permute-start(bf16[128,1536]{1,0:T(8,128)(2,1)S(1)} %collective-permute-done.6.refs_0_), channel_id=1, source_target_pairs={{0,1},{1,0},{2,3},{3,2},{4,5},{5,4},{6,7},{7,6},{8,9},{9,8},{10,11... | collective-permute-start | bytes 1179656 | tf_op jit(solution)/shard_map/ppermute | solution.py:305
  55.7 6.7 %collective-permute-done.14.refs_2_ = bf16[2,128,256]{2,1,0:T(8,128)(2,1)S(1)} collective-permute-done((bf16[2,128,256]{2,1,0:T(8,128)(2,1)S(1)}, bf16[2,128,256]{2,1,0:T(8,128)(2,1)S(1)}, u32[]{:S(2)}, u32[]{:S(2)}) %collective-permute-start.14) | collective-permute-done | bytes 131104 | tf_op jit(solution)/shard_map/ppermute | solution.py:299
  62.4 1.3 %collective-permute-start.15 = (bf16[3,192,256]{2,1,0:T(8,128)(2,1)S(1)}, bf16[3,192,256]{2,1,0:T(8,128)(2,1)S(1)}, u32[]{:S(2)}, u32[]{:S(2)}) collective-permute-start(bf16[3,192,256]{2,1,0:T(8,128)(2,1)S(1)} %collective-permute-done.11.refs_0_), channel_id=1, source_target_pairs={{0,4},{2,6},{4,0},{6,2},{1,5},{3,7},{5,1},{7,3},{8,12},{10,14},{12... | collective-permute-start | bytes 884744 | tf_op jit(solution)/shard_map/ppermute | solution.py:302
  63.7 1.1 collective-permute-start.16
  64.8 5.4 %collective-permute-start.17 = (bf16[2,128,256]{2,1,0:T(8,128)(2,1)S(1)}, bf16[2,128,256]{2,1,0:T(8,128)(2,1)S(1)}, u32[]{:S(2)}, u32[]{:S(2)}) collective-permute-start(bf16[2,128,256]{2,1,0:T(8,128)(2,1)S(1)} %get-tuple-element.58), channel_id=1, source_target_pairs={{0,24},{8,16},{16,8},{24,0},{1,25},{9,17},{17,9},{25,1},{2,26},{10... | collective-permute-start | bytes 393224 | tf_op jit(solution)/shard_map/ppermute | solution.py:299
  70.3 2.0 %collective-permute-start.19 = (bf16[2,128,256]{2,1,0:T(8,128)(2,1)S(1)}, bf16[2,128,256]{2,1,0:T(8,128)(2,1)S(1)}, u32[]{:S(2)}, u32[]{:S(2)}) collective-permute-start(bf16[2,128,256]{2,1,0:T(8,128)(2,1)S(1)} %collective-permute-done.16.refs_3_), channel_id=1, source_target_pairs={{0,4},{2,6},{4,0},{6,2},{1,5},{3,7},{5,1},{7,3},{8,12},{10,14},{12... | collective-permute-start | bytes 393224 | tf_op jit(solution)/shard_map/ppermute | solution.py:302
  72.3 2.4 %collective-permute-done.17.refs_0_ = bf16[2,128,256]{2,1,0:T(8,128)(2,1)S(1)} collective-permute-done((bf16[2,128,256]{2,1,0:T(8,128)(2,1)S(1)}, bf16[2,128,256]{2,1,0:T(8,128)(2,1)S(1)}, u32[]{:S(2)}, u32[]{:S(2)}) %collective-permute-start.17) | collective-permute-done | bytes 131104 | tf_op jit(solution)/shard_map/ppermute | solution.py:299
  75.2 1.4 %collective-permute-done.19.refs_5_ = bf16[2,128,256]{2,1,0:T(8,128)(2,1)S(1)} collective-permute-done((bf16[2,128,256]{2,1,0:T(8,128)(2,1)S(1)}, bf16[2,128,256]{2,1,0:T(8,128)(2,1)S(1)}, u32[]{:S(2)}, u32[]{:S(2)}) %collective-permute-start.19) | collective-permute-done | bytes 131104 | tf_op jit(solution)/shard_map/ppermute | solution.py:302
  76.6 3.0 %collective-permute-done.20.refs_1_ = bf16[2,128,256]{2,1,0:T(8,128)(2,1)S(1)} collective-permute-done((bf16[2,128,256]{2,1,0:T(8,128)(2,1)S(1)}, bf16[2,128,256]{2,1,0:T(8,128)(2,1)S(1)}, u32[]{:S(2)}, u32[]{:S(2)}) %collective-permute-start.20) | collective-permute-done | bytes 131104 | tf_op jit(solution)/shard_map/ppermute | solution.py:302
  81.7 3.0 %collective-permute-done.22.refs_13_ = bf16[2,3,192,256]{3,2,1,0:T(8,128)(2,1)S(1)} collective-permute-done((bf16[2,3,192,256]{3,2,1,0:T(8,128)(2,1)S(1)}, bf16[2,3,192,256]{3,2,1,0:T(8,128)(2,1)S(1)}, u32[]{:S(2)}, u32[]{:S(2)}) %collective-permute-start.22) | collective-permute-done | bytes 589856 | tf_op jit(solution)/shard_map/ppermute | solution.py:302
  86.8 3.0 %shard_map.125.qkv = bf16[3,512,256]{2,1,0:T(8,128)(2,1)S(1)} custom-call(f32[1,128]{1,0:T(1,128)S(1)} %bitcast.48, f32[1,128]{1,0:T(1,128)S(1)} %bitcast.49, bf16[128,3072]{1,0:T(8,128)(2,1)S(1)} %shard_map.118.refs_0_, bf16[128,3072]{1,0:T(8,128)(2,1)S(1)} %shard_map.120.refs_1_, bf16[128,3072]{1,0:T(8,128)(2,1)S(1)} %shard_map.121.refs_2_, ...), custom_call_target="tpu_custom_call" | custom-call | tf_op jit(solution)/shard_map/pallas_call | solution.py:145
  89.8 5.0 %shard_map.128 = (bf16[128,256]{1,0:T(8,128)(2,1)S(1)}, bf16[128,256]{1,0:T(8,128)(2,1)S(1)}, bf16[128,256]{1,0:T(8,128)(2,1)S(1)}, bf16[128,256]{1,0:T(8,128)(2,1)S(1)}) custom-call(bf16[3,512,256]{2,1,0:T(8,128)(2,1)S(1)} %shard_map.125.qkv, bf16[512,1024]{1,0:T(8,128)(2,1)S(1)} %copy-done.1, bf16[512,1024]{1,0:T(8,128)(2,1)S(1)} %copy-done.2, ...), custom_call_target="tpu_custom_call" | custom-call | tf_op jit(solution)/shard_map/pallas_call | solution.py:233
  94.8 2.6 %collective-permute-start.25 = (bf16[128,256]{1,0:T(8,128)(2,1)S(1)}, bf16[128,256]{1,0:T(8,128)(2,1)S(1)}, u32[]{:S(2)}, u32[]{:S(2)}) collective-permute-start(bf16[128,256]{1,0:T(8,128)(2,1)S(1)} %get-tuple-element.66), channel_id=1, source_target_pairs={{0,16},{8,0},{16,24},{24,8},{1,17},{9,1},{17,25},{25,9},{2,18},{10... | collective-permute-start | bytes 196616 | tf_op jit(solution)/shard_map/ppermute | solution.py:299
  97.4 1.7 %collective-permute-start.26 = (bf16[128,256]{1,0:T(8,128)(2,1)S(1)}, bf16[128,256]{1,0:T(8,128)(2,1)S(1)}, u32[]{:S(2)}, u32[]{:S(2)}) collective-permute-start(bf16[128,256]{1,0:T(8,128)(2,1)S(1)} %get-tuple-element.67), channel_id=1, source_target_pairs={{0,24},{8,16},{16,8},{24,0},{1,25},{9,17},{17,9},{25,1},{2,26},{10... | collective-permute-start | bytes 196616 | tf_op jit(solution)/shard_map/ppermute | solution.py:299
  99.3 4.4 %collective-permute-done.26.refs_2_ = bf16[128,256]{1,0:T(8,128)(2,1)S(1)} collective-permute-done((bf16[128,256]{1,0:T(8,128)(2,1)S(1)}, bf16[128,256]{1,0:T(8,128)(2,1)S(1)}, u32[]{:S(2)}, u32[]{:S(2)}) %collective-permute-start.26) | collective-permute-done | bytes 65568 | tf_op jit(solution)/shard_map/ppermute | solution.py:299
  105.4 1.5 %collective-permute-start.28 = (bf16[128,1536]{1,0:T(8,128)(2,1)S(1)}, bf16[128,1536]{1,0:T(8,128)(2,1)S(1)}, u32[]{:S(2)}, u32[]{:S(2)}) collective-permute-start(bf16[128,1536]{1,0:T(8,128)(2,1)S(1)} %shard_map.130), channel_id=1, source_target_pairs={{0,1},{1,0},{2,3},{3,2},{4,5},{5,4},{6,7},{7,6},{8,9},{9,8},{10,11... | collective-permute-start | bytes 1179656 | tf_op jit(solution)/shard_map/ppermute | solution.py:305
  107.5 8.6 %collective-permute-done.28 = bf16[128,1536]{1,0:T(8,128)(2,1)S(1)} collective-permute-done((bf16[128,1536]{1,0:T(8,128)(2,1)S(1)}, bf16[128,1536]{1,0:T(8,128)(2,1)S(1)}, u32[]{:S(2)}, u32[]{:S(2)}) %collective-permute-start.28) | collective-permute-done | bytes 393248 | tf_op jit(solution)/shard_map/ppermute | solution.py:305
  (67 shorter events, 17.8 us)
Async XLA Ops:
  0.0 12.3 %collective-permute-start = (bf16[128,1536]{1,0:T(8,128)(2,1)}, bf16[128,1536]{1,0:T(8,128)(2,1)S(1)}, u32[]{:S(2)}, u32[]{:S(2)}) collective-permute-start(bf16[128,1536]{1,0:T(8,128)(2,1)} %refs_0_.1), channel_id=1, source_target_pairs={{0,1},{1,0},{2,3},{3,2},{4,5},{5,4},{6,7},{7,6},{8,9},{9,8},{10,11... | collective-permute-start | bytes 1179656 | tf_op jit(solution)/shard_map/ppermute | solution.py:305
  2.9 11.7 %collective-permute-start.1 = (bf16[128,1536]{1,0:T(8,128)(2,1)}, bf16[128,1536]{1,0:T(8,128)(2,1)S(1)}, u32[]{:S(2)}, u32[]{:S(2)}) collective-permute-start(bf16[128,1536]{1,0:T(8,128)(2,1)} %refs_0_.1), channel_id=1, source_target_pairs={{0,8},{8,24},{16,0},{24,16},{1,9},{9,25},{17,1},{25,17},{2,10},{10... | collective-permute-start | bytes 1179656 | tf_op jit(solution)/shard_map/ppermute | solution.py:299
  7.7 36.9 %copy-start.3 = (bf16[128,1536]{1,0:T(8,128)(2,1)S(1)}, bf16[128,1536]{1,0:T(8,128)(2,1)}, u32[]{:S(2)}) copy-start(bf16[128,1536]{1,0:T(8,128)(2,1)} %refs_0_.1) | copy-start | bytes 1179652
  14.6 9.7 %collective-permute-start.2 = (bf16[128,1536]{1,0:T(8,128)(2,1)S(1)}, bf16[128,1536]{1,0:T(8,128)(2,1)S(1)}, u32[]{:S(2)}, u32[]{:S(2)}) collective-permute-start(bf16[128,1536]{1,0:T(8,128)(2,1)S(1)} %collective-permute-done.1.refs_0_), channel_id=1, source_target_pairs={{0,1},{1,0},{2,3},{3,2},{4,5},{5,4},{6,7},{7,6},{8,9},{9,8},{10,11... | collective-permute-start | bytes 1179656 | tf_op jit(solution)/shard_map/ppermute | solution.py:305
  15.1 13.0 %collective-permute-start.3 = (bf16[128,1536]{1,0:T(8,128)(2,1)S(1)}, bf16[128,1536]{1,0:T(8,128)(2,1)S(1)}, u32[]{:S(2)}, u32[]{:S(2)}) collective-permute-start(bf16[128,1536]{1,0:T(8,128)(2,1)S(1)} %collective-permute-done.1.refs_0_), channel_id=1, source_target_pairs={{0,8},{8,24},{16,0},{24,16},{1,9},{9,25},{17,1},{25,17},{2,10},{10... | collective-permute-start | bytes 1179656 | tf_op jit(solution)/shard_map/ppermute | solution.py:299
  16.1 17.8 %collective-permute-start.5 = (bf16[3,192,256]{2,1,0:T(8,128)(2,1)S(1)}, bf16[3,192,256]{2,1,0:T(8,128)(2,1)S(1)}, u32[]{:S(2)}, u32[]{:S(2)}) collective-permute-start(bf16[3,192,256]{2,1,0:T(8,128)(2,1)S(1)} %get-tuple-element.41), channel_id=1, source_target_pairs={{0,8},{8,24},{16,0},{24,16},{1,9},{9,25},{17,1},{25,17},{2,10},{10... | collective-permute-start | bytes 884744 | tf_op jit(solution)/shard_map/ppermute | solution.py:299
  19.3 14.5 %collective-permute-start.9 = (bf16[3,192,256]{2,1,0:T(8,128)(2,1)S(1)}, bf16[3,192,256]{2,1,0:T(8,128)(2,1)S(1)}, u32[]{:S(2)}, u32[]{:S(2)}) collective-permute-start(bf16[3,192,256]{2,1,0:T(8,128)(2,1)S(1)} %get-tuple-element.62.refs_0_), channel_id=1, source_target_pairs={{0,4},{2,6},{4,0},{6,2},{1,5},{3,7},{5,1},{7,3},{8,12},{10,14},{12... | collective-permute-start | bytes 884744 | tf_op jit(solution)/shard_map/ppermute | solution.py:302
  28.2 16.3 %collective-permute-start.4 = (bf16[128,1536]{1,0:T(8,128)(2,1)S(1)}, bf16[128,1536]{1,0:T(8,128)(2,1)S(1)}, u32[]{:S(2)}, u32[]{:S(2)}) collective-permute-start(bf16[128,1536]{1,0:T(8,128)(2,1)S(1)} %collective-permute-done.3.refs_0_), channel_id=1, source_target_pairs={{0,1},{1,0},{2,3},{3,2},{4,5},{5,4},{6,7},{7,6},{8,9},{9,8},{10,11... | collective-permute-start | bytes 1179656 | tf_op jit(solution)/shard_map/ppermute | solution.py:305
  29.7 14.8 %collective-permute-start.10 = (bf16[3,192,256]{2,1,0:T(8,128)(2,1)S(1)}, bf16[3,192,256]{2,1,0:T(8,128)(2,1)S(1)}, u32[]{:S(2)}, u32[]{:S(2)}) collective-permute-start(bf16[3,192,256]{2,1,0:T(8,128)(2,1)S(1)} %get-tuple-element.47), channel_id=1, source_target_pairs={{0,16},{8,0},{16,24},{24,8},{1,17},{9,1},{17,25},{25,9},{2,18},{10... | collective-permute-start | bytes 884744 | tf_op jit(solution)/shard_map/ppermute | solution.py:299
  33.9 10.6 %collective-permute-start.12 = (bf16[3,192,256]{2,1,0:T(8,128)(2,1)S(1)}, bf16[3,192,256]{2,1,0:T(8,128)(2,1)S(1)}, u32[]{:S(2)}, u32[]{:S(2)}) collective-permute-start(bf16[3,192,256]{2,1,0:T(8,128)(2,1)S(1)} %collective-permute-done.5.refs_2_), channel_id=1, source_target_pairs={{0,4},{2,6},{4,0},{6,2},{1,5},{3,7},{5,1},{7,3},{8,12},{10,14},{12... | collective-permute-start | bytes 884744 | tf_op jit(solution)/shard_map/ppermute | solution.py:302
  34.9 18.7 %collective-permute-start.6 = (bf16[128,1536]{1,0:T(8,128)(2,1)S(1)}, bf16[128,1536]{1,0:T(8,128)(2,1)S(1)}, u32[]{:S(2)}, u32[]{:S(2)}) collective-permute-start(bf16[128,1536]{1,0:T(8,128)(2,1)S(1)} %collective-permute-done.3.refs_0_), channel_id=1, source_target_pairs={{0,8},{8,24},{16,0},{24,16},{1,9},{9,25},{17,1},{25,17},{2,10},{10... | collective-permute-start | bytes 1179656 | tf_op jit(solution)/shard_map/ppermute | solution.py:299
  41.3 14.4 %collective-permute-start.11 = (bf16[3,192,256]{2,1,0:T(8,128)(2,1)S(1)}, bf16[3,192,256]{2,1,0:T(8,128)(2,1)S(1)}, u32[]{:S(2)}, u32[]{:S(2)}) collective-permute-start(bf16[3,192,256]{2,1,0:T(8,128)(2,1)S(1)} %get-tuple-element.49), channel_id=1, source_target_pairs={{0,24},{8,16},{16,8},{24,0},{1,25},{9,17},{17,9},{25,1},{2,26},{10... | collective-permute-start | bytes 884744 | tf_op jit(solution)/shard_map/ppermute | solution.py:299
  44.5 17.9 %collective-permute-start.13 = (bf16[3,192,256]{2,1,0:T(8,128)(2,1)S(1)}, bf16[3,192,256]{2,1,0:T(8,128)(2,1)S(1)}, u32[]{:S(2)}, u32[]{:S(2)}) collective-permute-start(bf16[3,192,256]{2,1,0:T(8,128)(2,1)S(1)} %collective-permute-done.10.refs_3_), channel_id=1, source_target_pairs={{0,4},{2,6},{4,0},{6,2},{1,5},{3,7},{5,1},{7,3},{8,12},{10,14},{12... | collective-permute-start | bytes 884744 | tf_op jit(solution)/shard_map/ppermute | solution.py:302
  48.5 5.0 %collective-permute-start.7 = (bf16[2,128,256]{2,1,0:T(8,128)(2,1)S(1)}, bf16[2,128,256]{2,1,0:T(8,128)(2,1)S(1)}, u32[]{:S(2)}, u32[]{:S(2)}) collective-permute-start(bf16[2,128,256]{2,1,0:T(8,128)(2,1)S(1)} %get-tuple-element.64.refs_0_), channel_id=1, source_target_pairs={{0,4},{2,6},{4,0},{6,2},{1,5},{3,7},{5,1},{7,3},{8,12},{10,14},{12... | collective-permute-start | bytes 393224 | tf_op jit(solution)/shard_map/ppermute | solution.py:302
  50.5 11.8 %collective-permute-start.14 = (bf16[2,128,256]{2,1,0:T(8,128)(2,1)S(1)}, bf16[2,128,256]{2,1,0:T(8,128)(2,1)S(1)}, u32[]{:S(2)}, u32[]{:S(2)}) collective-permute-start(bf16[2,128,256]{2,1,0:T(8,128)(2,1)S(1)} %get-tuple-element.53), channel_id=1, source_target_pairs={{0,8},{8,24},{16,0},{24,16},{1,9},{9,25},{17,1},{25,17},{2,10},{10... | collective-permute-start | bytes 393224 | tf_op jit(solution)/shard_map/ppermute | solution.py:299
  53.6 26.1 %collective-permute-start.8 = (bf16[128,1536]{1,0:T(8,128)(2,1)S(1)}, bf16[128,1536]{1,0:T(8,128)(2,1)S(1)}, u32[]{:S(2)}, u32[]{:S(2)}) collective-permute-start(bf16[128,1536]{1,0:T(8,128)(2,1)S(1)} %collective-permute-done.6.refs_0_), channel_id=1, source_target_pairs={{0,1},{1,0},{2,3},{3,2},{4,5},{5,4},{6,7},{7,6},{8,9},{9,8},{10,11... | collective-permute-start | bytes 1179656 | tf_op jit(solution)/shard_map/ppermute | solution.py:305
  62.4 17.3 %collective-permute-start.15 = (bf16[3,192,256]{2,1,0:T(8,128)(2,1)S(1)}, bf16[3,192,256]{2,1,0:T(8,128)(2,1)S(1)}, u32[]{:S(2)}, u32[]{:S(2)}) collective-permute-start(bf16[3,192,256]{2,1,0:T(8,128)(2,1)S(1)} %collective-permute-done.11.refs_0_), channel_id=1, source_target_pairs={{0,4},{2,6},{4,0},{6,2},{1,5},{3,7},{5,1},{7,3},{8,12},{10,14},{12... | collective-permute-start | bytes 884744 | tf_op jit(solution)/shard_map/ppermute | solution.py:302
  63.7 6.6 %collective-permute-start.16 = (bf16[2,128,256]{2,1,0:T(8,128)(2,1)S(1)}, bf16[2,128,256]{2,1,0:T(8,128)(2,1)S(1)}, u32[]{:S(2)}, u32[]{:S(2)}) collective-permute-start(bf16[2,128,256]{2,1,0:T(8,128)(2,1)S(1)} %get-tuple-element.56), channel_id=1, source_target_pairs={{0,16},{8,0},{16,24},{24,8},{1,17},{9,1},{17,25},{25,9},{2,18},{10... | collective-permute-start | bytes 393224 | tf_op jit(solution)/shard_map/ppermute | solution.py:299
  64.8 9.8 %collective-permute-start.17 = (bf16[2,128,256]{2,1,0:T(8,128)(2,1)S(1)}, bf16[2,128,256]{2,1,0:T(8,128)(2,1)S(1)}, u32[]{:S(2)}, u32[]{:S(2)}) collective-permute-start(bf16[2,128,256]{2,1,0:T(8,128)(2,1)S(1)} %get-tuple-element.58), channel_id=1, source_target_pairs={{0,24},{8,16},{16,8},{24,0},{1,25},{9,17},{17,9},{25,1},{2,26},{10... | collective-permute-start | bytes 393224 | tf_op jit(solution)/shard_map/ppermute | solution.py:299
  70.2 5.0 %collective-permute-start.18 = (bf16[2,128,256]{2,1,0:T(8,128)(2,1)S(1)}, bf16[2,128,256]{2,1,0:T(8,128)(2,1)S(1)}, u32[]{:S(2)}, u32[]{:S(2)}) collective-permute-start(bf16[2,128,256]{2,1,0:T(8,128)(2,1)S(1)} %collective-permute-done.14.refs_2_), channel_id=1, source_target_pairs={{0,4},{2,6},{4,0},{6,2},{1,5},{3,7},{5,1},{7,3},{8,12},{10,14},{12... | collective-permute-start | bytes 393224 | tf_op jit(solution)/shard_map/ppermute | solution.py:302
  70.3 6.3 %collective-permute-start.19 = (bf16[2,128,256]{2,1,0:T(8,128)(2,1)S(1)}, bf16[2,128,256]{2,1,0:T(8,128)(2,1)S(1)}, u32[]{:S(2)}, u32[]{:S(2)}) collective-permute-start(bf16[2,128,256]{2,1,0:T(8,128)(2,1)S(1)} %collective-permute-done.16.refs_3_), channel_id=1, source_target_pairs={{0,4},{2,6},{4,0},{6,2},{1,5},{3,7},{5,1},{7,3},{8,12},{10,14},{12... | collective-permute-start | bytes 393224 | tf_op jit(solution)/shard_map/ppermute | solution.py:302
  74.7 5.0 %collective-permute-start.20 = (bf16[2,128,256]{2,1,0:T(8,128)(2,1)S(1)}, bf16[2,128,256]{2,1,0:T(8,128)(2,1)S(1)}, u32[]{:S(2)}, u32[]{:S(2)}) collective-permute-start(bf16[2,128,256]{2,1,0:T(8,128)(2,1)S(1)} %collective-permute-done.17.refs_0_), channel_id=1, source_target_pairs={{0,4},{2,6},{4,0},{6,2},{1,5},{3,7},{5,1},{7,3},{8,12},{10,14},{12... | collective-permute-start | bytes 393224 | tf_op jit(solution)/shard_map/ppermute | solution.py:302
  80.1 6.6 %collective-permute-start.21 = (bf16[6,3,192,256]{3,2,1,0:T(8,128)(2,1)S(1)}, bf16[6,3,192,256]{3,2,1,0:T(8,128)(2,1)S(1)}, u32[]{:S(2)}, u32[]{:S(2)}) collective-permute-start(bf16[6,3,192,256]{3,2,1,0:T(8,128)(2,1)S(1)} %shard_map.123), channel_id=1, source_target_pairs={{0,2},{2,0},{4,6},{6,4},{1,3},{3,1},{5,7},{7,5},{8,10},{10,8},{12,... | collective-permute-start | bytes 5308424 | tf_op jit(solution)/shard_map/ppermute | solution.py:302
  81.2 3.5 %collective-permute-start.22 = (bf16[2,3,192,256]{3,2,1,0:T(8,128)(2,1)S(1)}, bf16[2,3,192,256]{3,2,1,0:T(8,128)(2,1)S(1)}, u32[]{:S(2)}, u32[]{:S(2)}) collective-permute-start(bf16[2,3,192,256]{3,2,1,0:T(8,128)(2,1)S(1)} %shard_map.124), channel_id=1, source_target_pairs={{0,2},{2,0},{4,6},{6,4},{1,3},{3,1},{5,7},{7,5},{8,10},{10,8},{12,... | collective-permute-start | bytes 1769480 | tf_op jit(solution)/shard_map/ppermute | solution.py:302
  85.7 4.1 %collective-permute-start.23 = (bf16[6,2,128,256]{3,2,1,0:T(8,128)(2,1)S(1)}, bf16[6,2,128,256]{3,2,1,0:T(8,128)(2,1)S(1)}, u32[]{:S(2)}, u32[]{:S(2)}) collective-permute-start(bf16[6,2,128,256]{3,2,1,0:T(8,128)(2,1)S(1)} %shard_map.126), channel_id=1, source_target_pairs={{0,2},{2,0},{4,6},{6,4},{1,3},{3,1},{5,7},{7,5},{8,10},{10,8},{12,... | collective-permute-start | bytes 2359304 | tf_op jit(solution)/shard_map/ppermute | solution.py:302
  85.9 18.8 %slice-start = ((s8[6291456]{0:T(1024)(128)(4,1)}), s8[4194304]{0:T(1024)(128)(4,1)S(1)}, s32[]{:S(2)}) async-start(s8[6291456]{0:T(1024)(128)(4,1)} %bitcast.21), calls=%async_computation | async-start | bytes 8388608
  86.3 3.5 %collective-permute-start.24 = (bf16[2,2,128,256]{3,2,1,0:T(8,128)(2,1)S(1)}, bf16[2,2,128,256]{3,2,1,0:T(8,128)(2,1)S(1)}, u32[]{:S(2)}, u32[]{:S(2)}) collective-permute-start(bf16[2,2,128,256]{3,2,1,0:T(8,128)(2,1)S(1)} %shard_map.127), channel_id=1, source_target_pairs={{0,2},{2,0},{4,6},{6,4},{1,3},{3,1},{5,7},{7,5},{8,10},{10,8},{12,... | collective-permute-start | bytes 786440 | tf_op jit(solution)/shard_map/ppermute | solution.py:302
  86.7 18.0 %slice-start.1 = ((s8[6291456]{0:T(1024)(128)(4,1)}), s8[2097152]{0:T(1024)(128)(4,1)S(1)}, s32[]{:S(2)}) async-start(s8[6291456]{0:T(1024)(128)(4,1)} %bitcast.21), calls=%async_computation.1 | async-start | bytes 4194304
  94.8 4.5 %collective-permute-start.25 = (bf16[128,256]{1,0:T(8,128)(2,1)S(1)}, bf16[128,256]{1,0:T(8,128)(2,1)S(1)}, u32[]{:S(2)}, u32[]{:S(2)}) collective-permute-start(bf16[128,256]{1,0:T(8,128)(2,1)S(1)} %get-tuple-element.66), channel_id=1, source_target_pairs={{0,16},{8,0},{16,24},{24,8},{1,17},{9,1},{17,25},{25,9},{2,18},{10... | collective-permute-start | bytes 196616 | tf_op jit(solution)/shard_map/ppermute | solution.py:299
  97.4 6.4 %collective-permute-start.26 = (bf16[128,256]{1,0:T(8,128)(2,1)S(1)}, bf16[128,256]{1,0:T(8,128)(2,1)S(1)}, u32[]{:S(2)}, u32[]{:S(2)}) collective-permute-start(bf16[128,256]{1,0:T(8,128)(2,1)S(1)} %get-tuple-element.67), channel_id=1, source_target_pairs={{0,24},{8,16},{16,8},{24,0},{1,25},{9,17},{17,9},{25,1},{2,26},{10... | collective-permute-start | bytes 196616 | tf_op jit(solution)/shard_map/ppermute | solution.py:299
  99.1 5.6 %collective-permute-start.27 = (bf16[128,256]{1,0:T(8,128)(2,1)S(1)}, bf16[128,256]{1,0:T(8,128)(2,1)S(1)}, u32[]{:S(2)}, u32[]{:S(2)}) collective-permute-start(bf16[128,256]{1,0:T(8,128)(2,1)S(1)} %get-tuple-element.68), channel_id=1, source_target_pairs={{0,8},{8,24},{16,0},{24,16},{1,9},{9,25},{17,1},{25,17},{2,10},{10... | collective-permute-start | bytes 196616 | tf_op jit(solution)/shard_map/ppermute | solution.py:299
  105.4 10.7 %collective-permute-start.28 = (bf16[128,1536]{1,0:T(8,128)(2,1)S(1)}, bf16[128,1536]{1,0:T(8,128)(2,1)S(1)}, u32[]{:S(2)}, u32[]{:S(2)}) collective-permute-start(bf16[128,1536]{1,0:T(8,128)(2,1)S(1)} %shard_map.130), channel_id=1, source_target_pairs={{0,1},{1,0},{2,3},{3,2},{4,5},{5,4},{6,7},{7,6},{8,9},{9,8},{10,11... | collective-permute-start | bytes 1179656 | tf_op jit(solution)/shard_map/ppermute | solution.py:305
  (10 other events, 33.0 us)
